TPU v7x, 32 devices: a whole 2x2x4 slice. The times are simulated.
32 devices in a mesh: fsdp: 8 (over y, x, core), tensor: 4 (over z).
Axes of the slice: x: 2, y: 2, z: 4, core: 2. Of those that a mesh axis runs over, the one named last changes fastest.
Arguments:
- image_rows: bfloat16 [16, 1024, 1024], P('fsdp', 'tensor'), may hold values from -6 to 6
- text_rows: bfloat16 [16, 128, 1024], P('fsdp', 'tensor'), may hold values from -6 to 6
- segment_ids: int32 [16, 128], P('fsdp'), may hold values from 0 to 3, as said below
- cotangent: bfloat16 [16, 1024, 1024], P('fsdp', 'tensor'), may hold values from -6 to 6
- query_weight: bfloat16 [1024, 1024], P('fsdp', 'tensor'), may hold values from -0.1875 to 0.1875
- key_weight: bfloat16 [1024, 1024], P('fsdp', 'tensor'), may hold values from -0.1875 to 0.1875
- value_weight: bfloat16 [1024, 1024], P('fsdp', 'tensor'), may hold values from -0.1875 to 0.1875
- attn_output: bfloat16 [1024, 1024], P('fsdp', 'tensor'), may hold values from -1.5 to 1.5
- cross_query: bfloat16 [1024, 1024], P('fsdp', 'tensor'), may hold values from -0.1875 to 0.1875
- cross_key: bfloat16 [1024, 1024], P('fsdp', 'tensor'), may hold values from -0.1875 to 0.1875
- cross_value: bfloat16 [1024, 1024], P('fsdp', 'tensor'), may hold values from -0.1875 to 0.1875
- cross_output: bfloat16 [1024, 1024], P('fsdp', 'tensor'), may hold values from -0.75 to 0.75
- hidden_in: bfloat16 [1024, 4096], P('fsdp', 'tensor'), may hold values from -0.1875 to 0.1875
- hidden_out: bfloat16 [1024, 4096], P('fsdp', 'tensor'), may hold values from -0.09375 to 0.09375
- gain_attn: float32 [1024], P('fsdp'), may hold values from 0.25 to 1.75
- bias_attn: float32 [1024], P('fsdp'), may hold values from -4 to 4
- gain_cross: float32 [1024], P('fsdp'), may hold values from 0.25 to 1.75
- bias_cross: float32 [1024], P('fsdp'), may hold values from -4 to 4
- gain_mlp: float32 [1024], P('fsdp'), may hold values from 0.25 to 1.75
- bias_mlp: float32 [1024], P('fsdp'), may hold values from -4 to 4
Outputs:
- result: bfloat16 [16, 1024, 1024], P('fsdp', 'tensor')
- input_grad: float32 [16, 1024, 1024], P('fsdp', 'tensor')
- text_grad: float32 [16, 128, 1024], P('fsdp', 'tensor')
- grad_query_weight: float32 [1024, 1024], P('fsdp', 'tensor')
- grad_key_weight: float32 [1024, 1024], P('fsdp', 'tensor')
- grad_value_weight: float32 [1024, 1024], P('fsdp', 'tensor')
- grad_attn_output: float32 [1024, 1024], P('fsdp', 'tensor')
- grad_cross_query: float32 [1024, 1024], P('fsdp', 'tensor')
- grad_cross_key: float32 [1024, 1024], P('fsdp', 'tensor')
- grad_cross_value: float32 [1024, 1024], P('fsdp', 'tensor')
- grad_cross_output: float32 [1024, 1024], P('fsdp', 'tensor')
- grad_hidden_in: float32 [1024, 4096], P('fsdp', 'tensor')
- grad_hidden_out: float32 [1024, 4096], P('fsdp', 'tensor')
- grad_gain_attn: float32 [1024], P('fsdp')
- grad_bias_attn: float32 [1024], P('fsdp')
- grad_gain_cross: float32 [1024], P('fsdp')
- grad_bias_cross: float32 [1024], P('fsdp')
- grad_gain_mlp: float32 [1024], P('fsdp')
- grad_bias_mlp: float32 [1024], P('fsdp')
Inputs may be any that keep to these rules, and one draw needn't show every extreme that they name: `segment_ids`: along each row the ids never fall, and each of the 4 ids appears.
All inputs are finite; a program needn't handle non-finite values.
Results may differ from a plain program's by a relative error of at most 0.035.
Values may be sent and summed in bfloat16 or wider, within the bound.
No kernel may reach another device: no remote copies, remote signals or barrier semaphores. Data moves between devices by JAX's collectives and lax.ppermute only.
A program may use at most 192 MiB of HBM per device.

v0:
```python
import functools
import math

import jax
import jax.numpy as jnp
from jax import lax
from jax.experimental import pallas as pl
from jax.experimental.pallas import tpu as pltpu
from jax.sharding import Mesh
from jax.sharding import PartitionSpec as P

HD = 64
EPS = 1e-05
NEG = -1e30
LOG2E = math.log2(math.e)
BF = jnp.bfloat16
F32 = jnp.float32
NT = (((1,), (1,)), ((), ()))
TN = (((0,), (0,)), ((), ()))
NN = (((1,), (0,)), ((), ()))


def dot(left, right, dims=NN):
    return lax.dot_general(left, right, dims, preferred_element_type=F32)


def lane_head(shape, axis, head):
    return lax.broadcasted_iota(jnp.int32, shape, axis) // HD == head


def self_forward_kernel(q_ref, k_ref, v_ref, mix_ref, lse_ref, *, block):
    length = q_ref.shape[0]
    scale = LOG2E * HD**-0.5
    causal = lax.broadcasted_iota(jnp.int32, (block, block), 0) <= lax.broadcasted_iota(
        jnp.int32, (block, block), 1
    )
    for at in range(length // block):
        lo, hi = at * block, (at + 1) * block
        query = q_ref[lo:hi, :]
        mixes = []
        for head in range(2):
            one = jnp.where(lane_head((1, 2 * HD), 1, head), query, jnp.zeros_like(query))
            diag = jnp.where(causal, dot(k_ref[lo:hi, :], one, NT), NEG)
            peak = jnp.max(diag, 0, keepdims=True)
            if at:
                past = dot(k_ref[:lo, :], one, NT)
                peak = jnp.maximum(peak, jnp.max(past, 0, keepdims=True))
            weights = jnp.exp2((diag - peak) * scale)
            total = jnp.sum(weights, 0, keepdims=True)
            mixed = dot(v_ref[lo:hi, :], weights.astype(BF), TN)
            if at:
                weights = jnp.exp2((past - peak) * scale)
                total = total + jnp.sum(weights, 0, keepdims=True)
                mixed = mixed + dot(v_ref[:lo, :], weights.astype(BF), TN)
            mixes.append(mixed / total)
            lse_ref[0, head : head + 1, lo:hi] = peak * scale + jnp.log2(total)
        both = jnp.where(lane_head((2 * HD, 1), 0, 0), mixes[0], mixes[1])
        mix_ref[lo:hi, :] = both.T.astype(BF)


def self_backward_kernel(
    q_ref, k_ref, v_ref, mix_ref, grad_ref, lse_ref, dq_ref, dk_ref, dv_ref, dk_sum, dv_sum, *, block
):
    length = q_ref.shape[0]
    scale = LOG2E * HD**-0.5
    causal = lax.broadcasted_iota(jnp.int32, (block, block), 0) <= lax.broadcasted_iota(
        jnp.int32, (block, block), 1
    )
    dk_sum[...] = jnp.zeros_like(dk_sum)
    dv_sum[...] = jnp.zeros_like(dv_sum)
    for at in range(length // block):
        lo, hi = at * block, (at + 1) * block
        query = q_ref[lo:hi, :]
        grad = grad_ref[lo:hi, :]
        product = (grad.astype(F32) * mix_ref[lo:hi, :].astype(F32)).T
        grads = []
        for head in range(2):
            picked = lane_head((1, 2 * HD), 1, head)
            one = jnp.where(picked, query, jnp.zeros_like(query))
            one_grad = jnp.where(picked, grad, jnp.zeros_like(grad))
            delta = jnp.sum(product[head * HD : (head + 1) * HD], 0, keepdims=True)
            lse = lse_ref[0, head : head + 1, lo:hi]
            total = jnp.zeros((2 * HD, block), F32)
            for start, stop in ((0, lo), (lo, hi)):
                if start == stop:
                    continue
                keys = k_ref[start:stop, :]
                weights = jnp.exp2(dot(keys, one, NT) * scale - lse)
                if start == lo:
                    weights = jnp.where(causal, weights, 0.0)
                slope = dot(v_ref[start:stop, :], one_grad, NT)
                score_grad = (weights * (slope - delta)).astype(BF)
                dv_sum[start:stop, :] += dot(weights.astype(BF), one_grad)
                dk_sum[start:stop, :] += dot(score_grad, one)
                total = total + dot(keys, score_grad, TN)
            grads.append(total)
        both = jnp.where(lane_head((2 * HD, 1), 0, 0), grads[0], grads[1])
        dq_ref[lo:hi, :] = (both.T * HD**-0.5).astype(BF)
    dk_ref[...] = (dk_sum[...] * HD**-0.5).astype(BF)
    dv_ref[...] = dv_sum[...].astype(BF)


def cross_forward_kernel(q_ref, k_ref, v_ref, ids_ref, caption_ref, mix_ref, lse_ref, *, block):
    length = q_ref.shape[0]
    scale = LOG2E * HD**-0.5
    for at in range(length // block):
        lo, hi = at * block, (at + 1) * block
        query = q_ref[lo:hi, :]
        seen = ids_ref[...] == caption_ref[:, lo:hi]
        mixes = []
        for head in range(2):
            one = jnp.where(lane_head((1, 2 * HD), 1, head), query, jnp.zeros_like(query))
            scores = jnp.where(seen, dot(k_ref[...], one, NT), NEG)
            peak = jnp.max(scores, 0, keepdims=True)
            weights = jnp.exp2((scores - peak) * scale)
            total = jnp.sum(weights, 0, keepdims=True)
            mixes.append(dot(v_ref[...], weights.astype(BF), TN) / total)
            lse_ref[0, head : head + 1, lo:hi] = peak * scale + jnp.log2(total)
        both = jnp.where(lane_head((2 * HD, 1), 0, 0), mixes[0], mixes[1])
        mix_ref[lo:hi, :] = both.T.astype(BF)


def cross_backward_kernel(
    q_ref, k_ref, v_ref, mix_ref, grad_ref, lse_ref, ids_ref, caption_ref, dq_ref, dk_ref, dv_ref, *, block
):
    length = q_ref.shape[0]
    scale = LOG2E * HD**-0.5
    keys, values = k_ref[...], v_ref[...]
    dk_sum = jnp.zeros(keys.shape, F32)
    dv_sum = jnp.zeros(keys.shape, F32)
    for at in range(length // block):
        lo, hi = at * block, (at + 1) * block
        query = q_ref[lo:hi, :]
        grad = grad_ref[lo:hi, :]
        product = (grad.astype(F32) * mix_ref[lo:hi, :].astype(F32)).T
        seen = ids_ref[...] == caption_ref[:, lo:hi]
        grads = []
        for head in range(2):
            picked = lane_head((1, 2 * HD), 1, head)
            one = jnp.where(picked, query, jnp.zeros_like(query))
            one_grad = jnp.where(picked, grad, jnp.zeros_like(grad))
            delta = jnp.sum(product[head * HD : (head + 1) * HD], 0, keepdims=True)
            lse = lse_ref[0, head : head + 1, lo:hi]
            weights = jnp.where(seen, jnp.exp2(dot(keys, one, NT) * scale - lse), 0.0)
            slope = dot(values, one_grad, NT)
            score_grad = (weights * (slope - delta)).astype(BF)
            dv_sum = dv_sum + dot(weights.astype(BF), one_grad)
            dk_sum = dk_sum + dot(score_grad, one)
            grads.append(dot(keys, score_grad, TN))
        both = jnp.where(lane_head((2 * HD, 1), 0, 0), grads[0], grads[1])
        dq_ref[lo:hi, :] = (both.T * HD**-0.5).astype(BF)
    dk_ref[...] = (dk_sum * HD**-0.5).astype(BF)
    dv_ref[...] = dv_sum.astype(BF)


def feed_kernel(
    rows_ref, cot_ref, win_ref, wout_ref, out_in, back_in, gin_ref, gout_ref, out_ref, back_ref, rows_t, cot_t, *, first
):
    step = pl.program_id(0)

    @pl.when(step == 0)
    def _():
        rows_t[...] = rows_ref[...].T
        cot_t[...] = cot_ref[...].T
        if first:
            out_ref[...] = jnp.zeros_like(out_ref)
            back_ref[...] = jnp.zeros_like(back_ref)
        else:
            out_ref[...] = out_in[...]
            back_ref[...] = back_in[...]

    pre = dot(rows_ref[...], win_ref[...])
    square = pre * pre
    slope = math.sqrt(2.0 / math.pi)
    bent = jnp.tanh(pre * (slope + slope * 0.044715 * square))
    half = 0.5 * (1.0 + bent)
    act = (pre * half).astype(BF)
    out_ref[...] += dot(act, wout_ref[...], NT)
    gout_ref[...] = dot(cot_t[...], act).astype(BF)
    bend = half + pre * (0.5 * (1.0 - bent * bent)) * (slope + 3.0 * slope * 0.044715 * square)
    pre_grad = (dot(cot_ref[...], wout_ref[...]) * bend).astype(BF)
    gin_ref[...] = dot(rows_t[...], pre_grad).astype(BF)
    back_ref[...] += dot(pre_grad, win_ref[...], NT)


VMEM_LIMIT = 60 * 1024 * 1024


def params():
    return pltpu.CompilerParams(vmem_limit_bytes=VMEM_LIMIT)


def column(rows, offset):
    return pl.BlockSpec((rows, 2 * HD), lambda i: (0, offset + i))


def self_forward(packed):
    length, width = packed.shape
    pairs = width // (6 * HD)
    return pl.pallas_call(
        functools.partial(self_forward_kernel, block=256),
        grid=(pairs,),
        in_specs=[column(length, 0), column(length, pairs), column(length, 2 * pairs)],
        out_specs=[column(length, 0), pl.BlockSpec((1, 2, length), lambda i: (i, 0, 0))],
        out_shape=[
            jax.ShapeDtypeStruct((length, pairs * 2 * HD), BF),
            jax.ShapeDtypeStruct((pairs, 2, length), F32),
        ],
        compiler_params=params(),
        cost_estimate=pl.CostEstimate(
            flops=8 * pairs * length * length * 2 * HD * 2,
            bytes_accessed=8 * pairs * length * 2 * HD,
            transcendentals=2 * pairs * length * length,
        ),
    )(packed, packed, packed)


def self_backward(packed, mix, grad, lse):
    length, width = packed.shape
    pairs = width // (6 * HD)
    part = jax.ShapeDtypeStruct((length, pairs * 2 * HD), BF)
    return pl.pallas_call(
        functools.partial(self_backward_kernel, block=256),
        grid=(pairs,),
        in_specs=[
            column(length, 0),
            column(length, pairs),
            column(length, 2 * pairs),
            column(length, 0),
            column(length, 0),
            pl.BlockSpec((1, 2, length), lambda i: (i, 0, 0)),
        ],
        out_specs=[column(length, 0)] * 3,
        out_shape=[part] * 3,
        scratch_shapes=[pltpu.VMEM((length, 2 * HD), F32)] * 2,
        compiler_params=params(),
        cost_estimate=pl.CostEstimate(
            flops=20 * pairs * length * length * 2 * HD * 2,
            bytes_accessed=16 * pairs * length * 2 * HD,
            transcendentals=2 * pairs * length * length,
        ),
    )(packed, packed, packed, mix, grad, lse)


def cross_forward(queries, keys, ids, captions):
    length, width = queries.shape
    texts = keys.shape[0]
    pairs = width // (2 * HD)
    return pl.pallas_call(
        functools.partial(cross_forward_kernel, block=min(512, length)),
        grid=(pairs,),
        in_specs=[
            column(length, 0),
            column(texts, 0),
            column(texts, pairs),
            pl.BlockSpec((texts, 1), lambda i: (0, 0)),
            pl.BlockSpec((1, length), lambda i: (0, 0)),
        ],
        out_specs=[column(length, 0), pl.BlockSpec((1, 2, length), lambda i: (i, 0, 0))],
        out_shape=[
            jax.ShapeDtypeStruct((length, width), BF),
            jax.ShapeDtypeStruct((pairs, 2, length), F32),
        ],
        compiler_params=params(),
    )(queries, keys, keys, ids, captions)


def cross_backward(queries, keys, mix, grad, lse, ids, captions):
    length, width = queries.shape
    texts = keys.shape[0]
    pairs = width // (2 * HD)
    return pl.pallas_call(
        functools.partial(cross_backward_kernel, block=min(512, length)),
        grid=(pairs,),
        in_specs=[
            column(length, 0),
            column(texts, 0),
            column(texts, pairs),
            column(length, 0),
            column(length, 0),
            pl.BlockSpec((1, 2, length), lambda i: (i, 0, 0)),
            pl.BlockSpec((texts, 1), lambda i: (0, 0)),
            pl.BlockSpec((1, length), lambda i: (0, 0)),
        ],
        out_specs=[column(length, 0), column(texts, 0), column(texts, 0)],
        out_shape=[
            jax.ShapeDtypeStruct((length, width), BF),
            jax.ShapeDtypeStruct((texts, width), BF),
            jax.ShapeDtypeStruct((texts, width), BF),
        ],
        compiler_params=params(),
    )(queries, keys, keys, mix, grad, lse, ids, captions)


def feed(rows, cot, w_in, w_out, sums):
    length, width = rows.shape
    units = w_in.shape[1]
    block = min(256, units)
    whole = pl.BlockSpec((length, width), lambda i: (0, 0))
    cut = pl.BlockSpec((width, block), lambda i: (0, i))
    first = sums is None
    kernel = functools.partial(feed_kernel, first=first)
    operands = [rows, cot, w_in, w_out]
    specs = [whole, whole, cut, cut]
    if first:
        body = lambda a, b, c, d, *rest: kernel(a, b, c, d, None, None, *rest)
    else:
        body = kernel
        operands += list(sums)
        specs += [whole, whole]
    total = jax.ShapeDtypeStruct((length, width), F32)
    part = jax.ShapeDtypeStruct((width, units), BF)
    return pl.pallas_call(
        body,
        grid=(units // block,),
        in_specs=specs,
        out_specs=[cut, cut, whole, whole],
        out_shape=[part, part, total, total],
        scratch_shapes=[pltpu.VMEM((width, length), BF)] * 2,
        compiler_params=params(),
        cost_estimate=pl.CostEstimate(
            flops=12 * length * width * units,
            bytes_accessed=8 * width * units + 8 * length * width,
            transcendentals=length * units,
        ),
    )(*operands)


def norm_parts(values):
    center = values - jnp.mean(values, -1, keepdims=True)
    inverse = lax.rsqrt(jnp.mean(center * center, -1, keepdims=True) + EPS)
    return center * inverse, inverse


def layer_norm(values, gain, offset):
    return (norm_parts(values)[0] * gain + offset).astype(BF)


def norm_back(values, gain, grad):
    hat, inverse = norm_parts(values)
    scaled = grad * gain
    back = inverse * (
        scaled
        - jnp.mean(scaled, -1, keepdims=True)
        - hat * jnp.mean(scaled * hat, -1, keepdims=True)
    )
    lead = tuple(range(values.ndim - 1))
    return back, jnp.sum(grad * hat, lead), jnp.sum(grad, lead)


def layer(shape, args):
    chips, tops, lows = shape["chip"], shape["hi"], shape["lo"]
    (
        image_rows,
        text_rows,
        segment_ids,
        cotangent,
        query_weight,
        key_weight,
        value_weight,
        attn_output,
        cross_query,
        cross_key,
        cross_value,
        cross_output,
        hidden_in,
        hidden_out,
        *norms,
    ) = args
    images, rows, width = image_rows.shape
    texts = text_rows.shape[1]
    half_rows = rows // 2
    length = rows * lows * tops
    shard = query_weight.shape[0]
    chip, core = lax.axis_index("chip"), lax.axis_index("core")
    top = lax.axis_index("hi")
    own_slot = core * images + top % images

    def swap(value):
        return lax.ppermute(value, "core", [(0, 1), (1, 0)])

    def across(value, bit):
        return lax.ppermute(value, "chip", [(i, i ^ bit) for i in range(chips)])

    def shift(value, step):
        return lax.ppermute(value, "hi", [((i + step) % tops, i) for i in range(tops)])

    def matching(number, back):
        pairs = []
        for source_core in range(2):
            for source_top in range(tops):
                slot = source_top ^ number
                target = (slot // images) * tops + source_core * images + slot % images
                source = source_core * tops + source_top
                pairs.append((target, source) if back else (source, target))
        return pairs

    def to_image(piece_of):
        got = [
            lax.ppermute(piece_of(top ^ number), ("core", "hi"), matching(number, False))
            for number in range(tops)
        ]
        whole = jnp.stack(got)
        return jnp.stack(
            [lax.dynamic_index_in_dim(whole, own_slot ^ place, 0, False) for place in range(tops)]
        )

    def from_image(pieces):
        return [
            lax.ppermute(
                lax.dynamic_index_in_dim(pieces, own_slot ^ number, 0, False),
                ("core", "hi"),
                matching(number, True),
            )
            for number in range(tops)
        ]

    def image_piece(value):
        def piece(slot):
            return lax.dynamic_slice(
                value,
                (slot % images, (slot // images) * half_rows, 0),
                (1, half_rows, width),
            )[0]

        return piece

    def to_rows(pieces):
        got = jnp.stack(from_image(pieces))
        ordered = jnp.stack(
            [lax.dynamic_index_in_dim(got, top ^ slot, 0, False) for slot in range(tops)]
        )
        ordered = ordered.reshape(2, images, half_rows, width)
        return jnp.swapaxes(ordered, 0, 1).reshape(images, rows, width)

    def tp_gather(mine):
        if lows == 1:
            other = swap(mine)
            first = jnp.where(core == 0, mine, other)
            second = jnp.where(core == 0, other, mine)
            return jnp.stack([first, second], 1).reshape(length, width)
        every = lax.all_gather(mine, ("lo", "core"))
        every = every.reshape(lows * 2, tops, half_rows, width)
        return jnp.swapaxes(every, 0, 1).reshape(length, width)

    def tp_reduce(partial):
        if lows == 1:
            cut = partial.reshape(tops, 2, half_rows, width)
            sent = lax.dynamic_index_in_dim(cut, 1 - core, 1, False).astype(BF)
            kept = lax.dynamic_index_in_dim(cut, core, 1, False)
            return kept + swap(sent).astype(F32)
        cut = jnp.swapaxes(partial.astype(BF).reshape(tops, lows * 2, half_rows, width), 0, 1)
        cut = lax.psum_scatter(cut, ("lo", "core"), scatter_dimension=0, tiled=False)
        return cut.astype(F32)

    def core_half(weight, which):
        columns = weight.shape[1] // 2
        return lax.dynamic_slice_in_dim(weight, which * columns, columns, 1)

    def pack(which):
        feeds = [core_half(weight, which) for weight in (hidden_in, hidden_out)]
        cuts = feeds[0].shape[1] // 2
        groups = [
            [core_half(w, which) for w in (query_weight, key_weight, value_weight, attn_output)],
            [core_half(w, which) for w in (cross_query, cross_key, cross_value, cross_output)],
            [w[:, :cuts] for w in feeds],
            [w[:, cuts:] for w in feeds],
        ]
        return jnp.concatenate([w for group in groups for w in group], 1)

    kept = pack(core)
    taken = swap(pack(1 - core))
    own = jnp.concatenate(
        [jnp.where(core == 0, kept, taken), jnp.where(core == 0, taken, kept)], 0
    )
    block_rows = 2 * shard
    group_width = own.shape[1] // 4

    def plane_gather(piece):
        if chips != 4:
            return lax.all_gather(piece, "chip", axis=0, tiled=True)
        side = across(piece, 1)
        over = across(piece, 2)
        corner_low = across(side[:shard], 2)
        corner_high = across(over[shard:], 1)
        corner = jnp.concatenate([corner_low, corner_high], 0)
        pieces = jnp.stack([piece, side, over, corner])
        ordered = [lax.dynamic_index_in_dim(pieces, chip ^ place, 0, False) for place in range(4)]
        return jnp.concatenate(ordered, 0)

    def plane_scatter(grads):
        if chips != 4:
            return lax.psum_scatter(grads, "chip", scatter_dimension=0, tiled=True).astype(F32)

        def rows_of(place, low, count):
            return lax.dynamic_slice_in_dim(grads, (chip ^ place) * block_rows + low, count, 0)

        by_side = across(rows_of(3, 0, shard), 1)
        by_over = across(rows_of(3, shard, shard), 2)
        to_over = jnp.concatenate(
            [rows_of(2, 0, shard).astype(F32) + by_side.astype(F32), rows_of(2, shard, shard).astype(F32)], 0
        ).astype(BF)
        to_side = jnp.concatenate(
            [rows_of(1, 0, shard).astype(F32), rows_of(1, shard, shard).astype(F32) + by_over.astype(F32)], 0
        ).astype(BF)
        over, side = across(to_over, 2), across(to_side, 1)
        return rows_of(0, 0, block_rows).astype(F32) + over.astype(F32) + side.astype(F32)

    def top_scatter(pieces):
        total = pieces[0].astype(F32)
        for step in range(1, tops):
            total = total + shift(pieces[step].astype(BF), tops - step).astype(F32)
        return total

    def core_split(total):
        cut = total.reshape(2, shard, total.shape[1])
        mine = lax.dynamic_index_in_dim(cut, core, 0, False)
        other = swap(lax.dynamic_index_in_dim(cut, 1 - core, 0, False).astype(BF)).astype(F32)
        return jnp.where(core == 0, mine, other), jnp.where(core == 0, other, mine)

    own_wide = plane_gather(own)

    def fetch(group, count):
        part = own[:, group * group_width : (group + 1) * group_width]
        columns = group_width // count
        got = [shift(part, step).reshape(block_rows, count, 1, columns) for step in range(1, tops)]
        rest = jnp.concatenate(got, 2).reshape(block_rows, (tops - 1) * group_width)
        rest = plane_gather(rest).reshape(width, count, (tops - 1) * columns)
        near = own_wide[:, group * group_width : (group + 1) * group_width]
        near = near.reshape(width, count, columns)
        return [
            jnp.concatenate([near[:, one], rest[:, one]], 1) for one in range(count)
        ]

    def give(grads):
        count = len(grads)
        columns = grads[0].shape[1] // tops
        summed = plane_scatter(jnp.concatenate(grads, 1)).reshape(block_rows, count, tops, columns)
        pieces = [summed[:, :, step].reshape(block_rows, count * columns) for step in range(tops)]
        low, high = core_split(top_scatter(pieces))
        low, high = low.reshape(shard, count, columns), high.reshape(shard, count, columns)
        return [(low[:, one], high[:, one]) for one in range(count)]

    packed_norms = lax.all_gather(jnp.stack(norms), ("chip", "core"), axis=1, tiled=True)
    gain_one, bias_one, gain_two, bias_two, gain_three, bias_three = packed_norms

    w_query, w_key, w_value, w_out = fetch(0, 4)
    inputs = to_image(image_piece(image_rows)).astype(F32)
    c_query, c_key, c_value, c_out = fetch(1, 4)
    in_low, out_low = fetch(2, 2)
    in_high, out_high = fetch(3, 2)

    text = to_image(lambda slot: text_rows[slot % images])
    if lows > 1:
        text = lax.all_gather(text, "lo", axis=1)
    text = text.reshape(tops * lows * texts, width)
    other_ids = swap(segment_ids)
    ids = jnp.where(core == top // images, segment_ids, other_ids)
    ids = lax.dynamic_index_in_dim(ids, top % images, 0, False)
    captions = jnp.repeat(ids, length // ids.shape[0])[None, :]
    ids = ids[:, None]
    cot = to_image(image_piece(cotangent))

    full_one = tp_gather(layer_norm(inputs, gain_one, bias_one))
    packed = dot(full_one, jnp.concatenate([w_query, w_key, w_value], 1)).astype(BF)
    self_mix, self_lse = self_forward(packed)
    after_attn = inputs + tp_reduce(dot(self_mix, w_out, NT))
    full_two = tp_gather(layer_norm(after_attn, gain_two, bias_two))
    queries = dot(full_two, c_query).astype(BF)
    w_text = jnp.concatenate([c_key, c_value], 1)
    keys = dot(text, w_text).astype(BF)
    cross_mix, cross_lse = cross_forward(queries, keys, ids, captions)
    after_cross = after_attn + tp_reduce(dot(cross_mix, c_out, NT))
    full_three = tp_gather(layer_norm(after_cross, gain_three, bias_three))
    full_cot = tp_gather(cot)
    gin_low, gout_low, *sums = feed(full_three, full_cot, in_low, out_low, None)
    gin_high, gout_high, out_sum, back_sum = feed(full_three, full_cot, in_high, out_high, sums)
    low_grads = give([gin_low, gout_low])
    high_grads = give([gin_high, gout_high])
    result = to_rows((after_cross + tp_reduce(out_sum)).astype(BF))

    back_three, dgain_three, dbias_three = norm_back(after_cross, gain_three, tp_reduce(back_sum))
    grad_cross = cot.astype(F32) + back_three
    full_grad = tp_gather(grad_cross.astype(BF))
    mix_grad = dot(full_grad, c_out).astype(BF)
    dq, dk, dv = cross_backward(queries, keys, cross_mix, mix_grad, cross_lse, ids, captions)
    back_sum = dot(dq, c_query, NT)
    dkv = jnp.concatenate([dk, dv], 1)
    cross_grads = give(
        [
            dot(full_two, dq, TN).astype(BF),
            dot(text, dk, TN).astype(BF),
            dot(text, dv, TN).astype(BF),
            dot(full_grad, cross_mix, TN).astype(BF),
        ]
    )
    text_part = dot(dkv, w_text, NT).astype(BF).reshape(tops, lows, texts, width)
    if lows > 1:
        text_part = lax.psum_scatter(text_part, "lo", scatter_dimension=1, tiled=True)
    got = [part.astype(F32) for part in from_image(text_part[:, 0])]
    got = jnp.stack(got)
    got = [lax.dynamic_index_in_dim(got, top ^ slot, 0, False) for slot in range(tops)]
    text_grad = jnp.stack([got[i] + got[images + i] for i in range(images)])

    back_two, dgain_two, dbias_two = norm_back(after_attn, gain_two, tp_reduce(back_sum))
    grad_attn = grad_cross + back_two
    full_grad = tp_gather(grad_attn.astype(BF))
    mix_grad = dot(full_grad, w_out).astype(BF)
    dq, dk, dv = self_backward(packed, self_mix, mix_grad, self_lse)
    dqkv = jnp.concatenate([dq, dk, dv], 1)
    dwqkv = dot(full_one, dqkv, TN).astype(BF)
    span = dq.shape[1]
    self_grads = give(
        [
            dwqkv[:, :span],
            dwqkv[:, span : 2 * span],
            dwqkv[:, 2 * span :],
            dot(full_grad, self_mix, TN).astype(BF),
        ]
    )
    back_sum = dot(dqkv, jnp.concatenate([w_query, w_key, w_value], 1), NT)
    back_one, dgain_one, dbias_one = norm_back(inputs, gain_one, tp_reduce(back_sum))
    input_grad = to_rows((grad_attn + back_one).astype(BF)).astype(F32)

    norm_sums = lax.psum(
        jnp.stack([dgain_one, dbias_one, dgain_two, dbias_two, dgain_three, dbias_three]),
        ("chip", "core", "hi", "lo"),
    )
    norm_sums = lax.dynamic_slice_in_dim(norm_sums, (chip * 2 + core) * shard, shard, 1)

    feeds = [
        jnp.concatenate([low_grads[i][0], high_grads[i][0], low_grads[i][1], high_grads[i][1]], 1)
        for i in range(2)
    ]
    joined = [jnp.concatenate(pair, 1) for pair in (*self_grads, *cross_grads)]
    return (result, input_grad, text_grad, *joined, *feeds, *[norm_sums[i] for i in range(6)])


BLOCK = 256
ANY = pl.BlockSpec(memory_space=pltpu.HBM)
SMEM = pl.BlockSpec(memory_space=pltpu.SMEM)
VMEM = pl.BlockSpec(memory_space=pltpu.VMEM)
MIB = 1024 * 1024


def like(*shape, dtype=BF):
    return jax.ShapeDtypeStruct(shape, dtype)


def call(body, outs, ins, operands, scratch=(), limit=60, grid=None, flops=0, moved=0):
    single = not isinstance(outs, (list, tuple))
    extra = {} if grid is None else {"grid": grid}
    cost = pl.CostEstimate(flops=1, bytes_accessed=1, transcendentals=0)
    out_specs, out_shape = ([outs[0]], [outs[1]]) if single else ([o[0] for o in outs], [o[1] for o in outs])
    return list(pl.pallas_call(
        body,
        in_specs=ins,
        out_specs=out_specs,
        out_shape=out_shape,
        scratch_shapes=list(scratch),
        compiler_params=pltpu.CompilerParams(vmem_limit_bytes=limit * MIB),
        cost_estimate=cost,
        **extra,
    )(*operands))


def run_copies(copies, sems):
    started = [pltpu.make_async_copy(source, target, sems.at[i]) for i, (source, target) in enumerate(copies)]
    for copy in started:
        copy.start()
    for copy in started:
        copy.wait()


def at(offset, count, unit=128):
    return pl.ds(pl.multiple_of(offset, unit), count)


def prepare_kernel(place, image, text, ids, cot, norms, wq, wk, wv, wo, cq, ck, cv, co, win, wout, *outs):
    keep, sent, rows_keep, rows_sent, cot_keep, cot_sent, sems = outs
    core = place[1]
    copies = []
    for target, which in ((sent, 1 - core), (keep, core)):
        for group, weights in enumerate(((wq, wk, wv, wo), (cq, ck, cv, co))):
            for one, weight in enumerate(weights):
                copies.append(
                    (
                        weight.at[:, at(which * 128, 128)],
                        target.at[group * 128 : (group + 1) * 128, one * 128 : (one + 1) * 128],
                    )
                )
        for part in range(2):
            for one, weight in enumerate((win, wout)):
                copies.append(
                    (
                        weight.at[:, at(which * 512 + part * 256, 256)],
                        target.at[256 + part * 128 : 384 + part * 128, one * 256 : (one + 1) * 256],
                    )
                )
        copies.append((norms, target.at[512:528, :]))
    for target, cots, which in ((rows_sent, cot_sent, 1 - core), (rows_keep, cot_keep, core)):
        for one in range(2):
            copies.append((image.at[one, at(which * 128, 128), :], target.at[one]))
            copies.append((cot.at[one, at(which * 128, 128), :], cots.at[one, 0:128, :]))
            copies.append((text.at[one], cots.at[one, 128:160, :]))
            copies.append((ids.at[one], cots.at[one, 160:176, :]))
    run_copies(copies, sems)


def prepare(place, image, text, ids, cot, norms, weights):
    return call(
        prepare_kernel,
        [(VMEM, like(528, 512))] * 2 + [(VMEM, like(2, 128, 1024))] * 2 + [(VMEM, like(2, 176, 1024))] * 2,
        [SMEM] + [ANY] * 15,
        (place, image, text, ids, cot, norms, *weights),
        [pltpu.SemaphoreType.DMA((42,))],
    )


def pick_kernel(place, keep, taken, *outs):
    core, top = place[1], place[2]
    for step, out in enumerate(outs):
        image = (top + 4 - step) % 4

        @pl.when(image // 2 == core)
        def _():
            out[...] = keep[image % 2]

        @pl.when(image // 2 != core)
        def _():
            out[...] = taken[image % 2]


def pick(place, keep, taken):
    return call(
        pick_kernel,
        [(VMEM, like(*keep.shape[1:]))] * 4,
        [SMEM, VMEM, VMEM],
        (place, keep, taken),
    )


def join_kernel(*refs):
    keep, taken, singles, doubles, sems = refs[0], refs[1], refs[2:6], refs[6:8], refs[8]
    copies = []
    for group in range(4):
        for half, source in enumerate((keep, taken)):
            part = source.at[group * 128 : (group + 1) * 128, :]
            copies.append((part, singles[group].at[half * 128 : (half + 1) * 128, :]))
            low = (group % 2) * 256 + half * 128
            copies.append((part, doubles[group // 2].at[low : low + 128, :]))
    for half, source in enumerate((keep, taken)):
        low = 512 + half * 16
        copies.append((source.at[512:528, :], doubles[0].at[low : low + 16, :]))
    run_copies(copies, sems)


def join(keep, taken):
    return call(
        join_kernel,
        [(VMEM, like(256, 512))] * 4 + [(VMEM, like(544, 512)), (VMEM, like(512, 512))],
        [ANY] * 2,
        (keep, taken),
        [pltpu.SemaphoreType.DMA((18,))],
        limit=60,
    )


def stack_kernel(*refs):
    *parts, whole, sems = refs
    copies, low = [], 0
    for part in parts:
        copies.append((part, whole.at[low : low + part.shape[0]]))
        low += part.shape[0]
    run_copies(copies, sems)


def stack(parts):
    rows = sum(part.shape[0] for part in parts)
    return call(
        stack_kernel,
        [(VMEM, like(rows, *parts[0].shape[1:]))],
        [ANY] * len(parts),
        parts,
        [pltpu.SemaphoreType.DMA((len(parts),))],
        limit=60,
    )[0]


def arrange_kernel(place, *refs):
    messages, rows, text, sems = refs[:4], refs[4], refs[5], refs[6]
    copies = []
    for number, message in enumerate(messages):
        copies.append((message.at[0:128, :], rows.at[number]))
        copies.append((message.at[128:160, :], text.at[at((place[2] + number) % 4 * 32, 32, 32), :]))
    run_copies(copies, sems)


def arrange(place, messages):
    return call(
        arrange_kernel,
        [(VMEM, like(4, 128, 1024)), (VMEM, like(128, 1024))],
        [SMEM] + [ANY] * 4,
        (place, *messages),
        [pltpu.SemaphoreType.DMA((8,))],
    )


def turn_kernel(place, whole, rest, sems):
    run_copies(
        [(whole.at[(place[2] + step) % 4], rest.at[(step - 1) * 256 : step * 256, :]) for step in range(1, 4)], sems
    )


def turn(place, whole):
    return call(
        turn_kernel,
        [(VMEM, like(768, 512))],
        [SMEM, ANY],
        (place, whole),
        [pltpu.SemaphoreType.DMA((3,))],
    )[0]


def assemble_kernel(place, *refs, low, far_parts, norms):
    own, side, over, corner, rest, rside, rover = refs[:7]
    rcorner = refs[7 : 7 + far_parts]
    outs = refs[7 + far_parts :]
    whole, buffer, loads, stores = outs[0], outs[-3], outs[-2], outs[-1]
    chip, core = place[0], place[1]
    batches = []
    for source in range(4):
        copies = []
        for half in range(2):
            row = at((chip ^ source) * 256 + (core ^ half) * 128, 128)
            near = (own, side, over, corner)[source]
            first = half * 128 + (0 if source == 3 else low)
            copies.append((near.at[first : first + 128, :], buffer.at[row, 0:512]))
            for step in range(3):
                first = step * 256 + half * 128
                far = (rest, rside, rover, rcorner[first * far_parts // 768])[source]
                if source == 3:
                    first %= 768 // far_parts
                columns = slice((step + 1) * 512, (step + 2) * 512)
                copies.append((far.at[first : first + 128, :], buffer.at[row, columns]))
        batches.append([pltpu.make_async_copy(a, b, loads.at[source * 8 + i]) for i, (a, b) in enumerate(copies)])
    for batch in batches:
        for copy in batch:
            copy.start()
    stored = []
    if norms:
        pairs = []
        for source, piece in enumerate((own, side, over, outs[1])):
            for half in range(2):
                column = (chip ^ source) * 256 + (core ^ half) * 128
                first = (256 if source == 3 else 512) + half * 16
                pairs.append((piece.at[first : first + 16, 0:128], outs[2].at[:, at(column, 128)]))
        for i, (a, b) in enumerate(pairs):
            stored.append(pltpu.make_async_copy(a, b, stores.at[4 + i]))
            stored[-1].start()
    for source, batch in enumerate(batches):
        for copy in batch:
            copy.wait()
        rows = at((chip ^ source) * 256, 256)
        stored.append(pltpu.make_async_copy(buffer.at[rows, :], whole.at[rows, :], stores.at[source]))
        stored[-1].start()
    for copy in stored:
        copy.wait()


def assemble(place, near, far, low, norms=None):
    outs = [(ANY, like(1024, 2048))]
    operands = (place, *near, *far)
    if norms is not None:
        outs.append((VMEM, like(16, 1024)))
        operands += (norms,)

    def body(*refs):
        count = len(operands)
        if norms is None:
            assemble_kernel(*refs, low=low, far_parts=len(far) - 3, norms=False)
        else:
            assemble_kernel(
                *refs[: count - 1], refs[count], refs[count - 1], *refs[count + 1 :],
                low=low, far_parts=len(far) - 3, norms=True,
            )

    return call(
        body,
        outs,
        [SMEM] + [ANY] * (len(operands) - 1),
        operands,
        [pltpu.VMEM((1024, 2048), BF), pltpu.SemaphoreType.DMA((32,)), pltpu.SemaphoreType.DMA((12,))],
    )


def norm_row(norms, one):
    return norms[one : one + 1, :].astype(F32)


def normalized(values, gain, bias):
    center = values - jnp.mean(values, -1, keepdims=True)
    inverse = lax.rsqrt(jnp.mean(center * center, -1, keepdims=True) + EPS)
    return (center * inverse * gain + bias).astype(BF)


def columns_of(weights, one, count=128):
    return jnp.concatenate([weights[:, s * 512 + one * count : s * 512 + (one + 1) * count] for s in range(4)], 1)


def image_blocks(place, own, other):
    core, top = place[1], place[2]
    for number in range(4):
        yield (top + number) % 4 * 256 + core * 128, own, number
        yield (top + number) % 4 * 256 + (1 - core) * 128, other, number


def one_head(values, head):
    return jnp.where(lane_head((1, 2 * HD), 1, head), values, jnp.zeros_like(values))


def softmax_mix(scores, values):
    scale = LOG2E * HD**-0.5
    peak = jnp.max(scores[0], 0, keepdims=True)
    for part in scores[1:]:
        peak = jnp.maximum(peak, jnp.max(part, 0, keepdims=True))
    total, mixed = 0.0, 0.0
    for part, rows in zip(scores, values):
        weights = jnp.exp2((part - peak) * scale)
        total = total + jnp.sum(weights, 0, keepdims=True)
        mixed = mixed + dot(rows, weights.astype(BF), TN)
    return mixed / total, peak * scale + jnp.log2(total)


def causal_mask():
    return lax.broadcasted_iota(jnp.int32, (BLOCK, BLOCK), 0) <= lax.broadcasted_iota(
        jnp.int32, (BLOCK, BLOCK), 1
    )


def self_fwd_kernel(place, own, other, norms, weights, normed, qkv, mix, lse, part):
    gain, bias = norm_row(norms, 0), norm_row(norms, 1)
    for row, half, number in image_blocks(place, own, other):
        normed[at(row, 128), :] = normalized(half[number].astype(F32), gain, bias)
    w_in = jnp.concatenate([columns_of(weights, one) for one in range(3)], 1)
    for low in range(0, 1024, BLOCK):
        qkv[low : low + BLOCK, :] = dot(normed[low : low + BLOCK, :], w_in).astype(BF)
    causal = causal_mask()

    def pair_step(pair, carry):
        lanes = at(pair * 128, 128)
        k_lanes, v_lanes = at(512 + pair * 128, 128), at(1024 + pair * 128, 128)
        for low in range(0, 1024, BLOCK):
            high = low + BLOCK
            query = qkv[low:high, lanes]
            mixes = []
            for head in range(2):
                one = one_head(query, head)
                scores = [jnp.where(causal, dot(qkv[low:high, k_lanes], one, NT), NEG)]
                values = [qkv[low:high, v_lanes]]
                if low:
                    scores.append(dot(qkv[:low, k_lanes], one, NT))
                    values.append(qkv[:low, v_lanes])
                mixed, logsum = softmax_mix(scores, values)
                mixes.append(mixed)
                lse[pair, head : head + 1, low:high] = logsum
            both = jnp.where(lane_head((128, 1), 0, 0), mixes[0], mixes[1])
            mix[low:high, lanes] = both.T.astype(BF)
        return carry

    lax.fori_loop(0, 4, pair_step, 0)
    w_out = columns_of(weights, 3)
    for low in range(0, 1024, BLOCK):
        part[low : low + BLOCK, :] = dot(mix[low : low + BLOCK, :], w_out, NT).astype(BF)


def fused_self_forward(place, own, other, norms, weights):
    return call(
        self_fwd_kernel,
        [
            (VMEM, like(1024, 1024)),
            (VMEM, like(1024, 1536)),
            (VMEM, like(1024, 512)),
            (VMEM, like(4, 2, 1024, dtype=F32)),
            (VMEM, like(1024, 1024)),
        ],
        [SMEM] + [VMEM] * 4,
        (place, own, other, norms, weights),
        limit=60,
        flops=10 * 2**30,
        moved=14 * MIB,
    )


def cross_fwd_kernel(
    place, own, other, mine, theirs, norms, text, ids, caption, weights, after, normed, queries, keys, mix, lse, part
):
    gain, bias = norm_row(norms, 2), norm_row(norms, 3)
    for row, half, number in image_blocks(place, own, other):
        rows = at(row, 128)
        values = half[number].astype(F32) + (mine[rows, :].astype(F32) + theirs[rows, :].astype(F32))
        after[rows, :] = values
        normed[rows, :] = normalized(values, gain, bias)
    w_query = columns_of(weights, 0)
    for low in range(0, 1024, BLOCK):
        queries[low : low + BLOCK, :] = dot(normed[low : low + BLOCK, :], w_query).astype(BF)
    w_text = jnp.concatenate([columns_of(weights, 1), columns_of(weights, 2)], 1)
    keys[...] = dot(text[...], w_text).astype(BF)

    def pair_step(pair, carry):
        lanes, v_lanes = at(pair * 128, 128), at(512 + pair * 128, 128)
        for low in range(0, 1024, 512):
            high = low + 512
            query = queries[low:high, lanes]
            seen = ids[...] == caption[:, low:high]
            mixes = []
            for head in range(2):
                scores = jnp.where(seen, dot(keys[:, lanes], one_head(query, head), NT), NEG)
                mixed, logsum = softmax_mix([scores], [keys[:, v_lanes]])
                mixes.append(mixed)
                lse[pair, head : head + 1, low:high] = logsum
            both = jnp.where(lane_head((128, 1), 0, 0), mixes[0], mixes[1])
            mix[low:high, lanes] = both.T.astype(BF)
        return carry

    lax.fori_loop(0, 4, pair_step, 0)
    w_out = columns_of(weights, 3)
    for low in range(0, 1024, BLOCK):
        part[low : low + BLOCK, :] = dot(mix[low : low + BLOCK, :], w_out, NT).astype(BF)


def fused_cross_forward(place, own, other, mine, theirs, norms, text, ids, caption, weights):
    return call(
        cross_fwd_kernel,
        [
            (VMEM, like(1024, 1024, dtype=F32)),
            (VMEM, like(1024, 1024)),
            (VMEM, like(1024, 512)),
            (VMEM, like(128, 1024)),
            (VMEM, like(1024, 512)),
            (VMEM, like(4, 2, 1024, dtype=F32)),
            (VMEM, like(1024, 1024)),
        ],
        [SMEM] + [VMEM] * 9,
        (place, own, other, mine, theirs, norms, text, ids, caption, weights),
        limit=60,
        flops=5 * 2**30,
        moved=20 * MIB,
    )


def cut_grads(place, grads, columns, own, side, over, low, high):
    chip = place[0]
    own[:, columns] = grads[at(chip * 256, 256), :].astype(BF)
    side[:, columns] = grads[at((chip ^ 1) * 256, 256), :].astype(BF)
    over[:, columns] = grads[at((chip ^ 2) * 256, 256), :].astype(BF)
    low[:, columns] = grads[at((chip ^ 3) * 256, 128), :].astype(BF)
    high[:, columns] = grads[at((chip ^ 3) * 256 + 128, 128), :].astype(BF)


GRAD_SHAPES = [(256, 2048)] * 3 + [(128, 2048)] * 2


def feed_step(rows, cot, rows_t, cot_t, weights, out_sum, back_sum, grads):
    w_in, w_out = weights[:, :256], weights[:, 256:]
    slope = math.sqrt(2.0 / math.pi)
    acts, pre_grads = [], []
    for low in range(0, 1024, BLOCK):
        part = slice(low, low + BLOCK)
        pre = dot(rows[part, :], w_in)
        square = pre * pre
        bent = jnp.tanh(pre * (slope + slope * 0.044715 * square))
        half = 0.5 * (1.0 + bent)
        act = (pre * half).astype(BF)
        bend = half + pre * (0.5 * (1.0 - bent * bent)) * (slope + 3.0 * slope * 0.044715 * square)
        pre_grad = (dot(cot[part, :], w_out) * bend).astype(BF)
        out_sum[part, :] += dot(act, w_out, NT)
        back_sum[part, :] += dot(pre_grad, w_in, NT)
        acts.append(act)
        pre_grads.append(pre_grad)
    grads[:, :256] = dot(rows_t[...], jnp.concatenate(pre_grads, 0))
    grads[:, 256:] = dot(cot_t[...], jnp.concatenate(acts, 0))


def feed_first_kernel(
    place, after, mine, theirs, norms, cot_own, cot_other, weights,
    g_own, g_side, g_over, g_low, g_high, after_cross, normed, cot, out_sum, back_sum, rows_t, cot_t, grads,
):
    @pl.when(pl.program_id(0) == 0)
    def _():
        gain, bias = norm_row(norms, 4), norm_row(norms, 5)
        for low in range(0, 1024, 128):
            rows = slice(low, low + 128)
            values = after[rows, :] + (mine[rows, :].astype(F32) + theirs[rows, :].astype(F32))
            after_cross[rows, :] = values
            normed[rows, :] = normalized(values, gain, bias)
        for row, half, number in image_blocks(place, cot_own, cot_other):
            cot[at(row, 128), :] = half[number]
        rows_t[...] = normed[...].T
        cot_t[...] = cot[...].T
        out_sum[...] = jnp.zeros_like(out_sum)
        back_sum[...] = jnp.zeros_like(back_sum)

    feed_step(normed, cot, rows_t, cot_t, weights, out_sum, back_sum, grads)
    cut_grads(place, grads, slice(None), g_own, g_side, g_over, g_low, g_high)


def feed_second_kernel(
    place, normed, cot, out_in, back_in, weights,
    g_own, g_side, g_over, g_low, g_high, out_keep, out_sent, back, out_sum, back_sum, rows_t, cot_t, grads,
):
    step, core = pl.program_id(0), place[1]

    @pl.when(step == 0)
    def _():
        rows_t[...] = normed[...].T
        cot_t[...] = cot[...].T
        out_sum[...] = out_in[...]
        back_sum[...] = back_in[...]

    feed_step(normed, cot, rows_t, cot_t, weights, out_sum, back_sum, grads)
    cut_grads(place, grads, slice(None), g_own, g_side, g_over, g_low, g_high)

    @pl.when(step == 3)
    def _():
        back[...] = back_sum[...].astype(BF)
        for block in range(4):
            out_keep[block] = out_sum[at(block * 256 + core * 128, 128), :]
            out_sent[block] = out_sum[at(block * 256 + (1 - core) * 128, 128), :].astype(BF)


def once(*shape):
    zeros = (0,) * len(shape)
    return pl.BlockSpec(shape, lambda i: zeros, pipeline_mode=pl.Buffered(1))


def grad_outs():
    return [(pl.BlockSpec((rows, 512), lambda i: (0, i)), like(rows, n)) for rows, n in GRAD_SHAPES]


FEED_FLOPS = 13 * 2**30


def feed_first(place, after, mine, theirs, norms, cot_own, cot_other, weights):
    square = once(1024, 1024)
    return call(
        feed_first_kernel,
        grad_outs()
        + [
            (square, like(1024, 1024, dtype=F32)),
            (square, like(1024, 1024)),
            (square, like(1024, 1024)),
            (square, like(1024, 1024, dtype=F32)),
            (square, like(1024, 1024, dtype=F32)),
        ],
        [SMEM, square, square, square, once(16, 1024), once(4, 128, 1024), once(4, 128, 1024)]
        + [pl.BlockSpec((1024, 512), lambda i: (0, i))],
        (place, after, mine, theirs, norms, cot_own, cot_other, weights),
        [pltpu.VMEM((1024, 1024), BF)] * 2 + [pltpu.VMEM((1024, 512), F32)],
        limit=60,
        grid=(4,),
        flops=FEED_FLOPS,
        moved=30 * MIB,
    )


def feed_second(place, normed, cot, out_in, back_in, weights):
    square = once(1024, 1024)
    return call(
        feed_second_kernel,
        grad_outs()
        + [
            (once(4, 128, 1024), like(4, 128, 1024, dtype=F32)),
            (once(4, 128, 1024), like(4, 128, 1024)),
            (square, like(1024, 1024)),
        ],
        [SMEM, square, square, square, square, pl.BlockSpec((1024, 512), lambda i: (0, i))],
        (place, normed, cot, out_in, back_in, weights),
        [pltpu.VMEM((1024, 1024), F32)] * 2
        + [pltpu.VMEM((1024, 1024), BF)] * 2
        + [pltpu.VMEM((1024, 512), F32)],
        limit=60,
        grid=(4,),
        flops=FEED_FLOPS,
        moved=26 * MIB,
    )


def norm_backward(values, gain, grad):
    center = values - jnp.mean(values, -1, keepdims=True)
    inverse = lax.rsqrt(jnp.mean(center * center, -1, keepdims=True) + EPS)
    hat = center * inverse
    scaled = grad * gain
    back = inverse * (
        scaled - jnp.mean(scaled, -1, keepdims=True) - hat * jnp.mean(scaled * hat, -1, keepdims=True)
    )
    return back, grad * hat


def norm_block(values_of, mine, theirs, base_of, gain, norms, keep):
    gain = norm_row(*gain)
    gain_sum, bias_sum = jnp.zeros((8, 1024), F32), jnp.zeros((8, 1024), F32)
    for low in range(0, 1024, 128):
        rows = slice(low, low + 128)
        grad = mine[rows, :].astype(F32) + theirs[rows, :].astype(F32)
        back, term = norm_backward(values_of(rows), gain, grad)
        keep(rows, base_of(rows) + back)
        gain_sum = gain_sum + jnp.sum(term.reshape(16, 8, 1024), 0)
        bias_sum = bias_sum + jnp.sum(grad.reshape(16, 8, 1024), 0)
    norms[0:1, :] = jnp.sum(gain_sum, 0, keepdims=True)
    norms[1:2, :] = jnp.sum(bias_sum, 0, keepdims=True)


def head_grads(keys, values, one, one_grad, lse, delta, mask):
    weights = jnp.exp2(dot(keys, one, NT) * (LOG2E * HD**-0.5) - lse)
    if mask is not None:
        weights = jnp.where(mask, weights, 0.0)
    slope = dot(values, one_grad, NT)
    return weights.astype(BF), (weights * (slope - delta)).astype(BF)


def cross_bwd_kernel(
    place, after, mine, theirs, cot, gain, weights, normed, text, queries, keys, mix, lse, ids, caption,
    grad_cross, part, norms, text_part, g_own, g_side, g_over, g_low, g_high, low_grad, mix_grad, dq, dkv, grads,
):
    def keep(rows, value):
        grad_cross[rows, :] = value
        low_grad[rows, :] = value.astype(BF)

    norm_block(lambda rows: after[rows, :], mine, theirs, lambda rows: cot[rows, :].astype(F32), (gain, 4), norms, keep)
    w_out = columns_of(weights, 3)
    for low in range(0, 1024, BLOCK):
        mix_grad[low : low + BLOCK, :] = dot(low_grad[low : low + BLOCK, :], w_out).astype(BF)

    def pair_step(pair, carry):
        lanes, v_lanes = at(pair * 128, 128), at(512 + pair * 128, 128)
        dk_sum, dv_sum = jnp.zeros((128, 128), F32), jnp.zeros((128, 128), F32)
        for low in range(0, 1024, 512):
            high = low + 512
            query, grad = queries[low:high, lanes], mix_grad[low:high, lanes]
            product = (grad.astype(F32) * mix[low:high, lanes].astype(F32)).T
            seen = ids[...] == caption[:, low:high]
            back = []
            for head in range(2):
                one, one_grad = one_head(query, head), one_head(grad, head)
                delta = jnp.sum(product[head * HD : (head + 1) * HD], 0, keepdims=True)
                prob, score_grad = head_grads(
                    keys[:, lanes], keys[:, v_lanes], one, one_grad, lse[pair, head : head + 1, low:high], delta, seen
                )
                dv_sum = dv_sum + dot(prob, one_grad)
                dk_sum = dk_sum + dot(score_grad, one)
                back.append(dot(keys[:, lanes], score_grad, TN))
            both = jnp.where(lane_head((128, 1), 0, 0), back[0], back[1])
            dq[low:high, lanes] = (both.T * HD**-0.5).astype(BF)
        dkv[:, lanes] = (dk_sum * HD**-0.5).astype(BF)
        dkv[:, v_lanes] = dv_sum.astype(BF)
        return carry

    lax.fori_loop(0, 4, pair_step, 0)
    w_query = columns_of(weights, 0)
    for low in range(0, 1024, BLOCK):
        part[low : low + BLOCK, :] = dot(dq[low : low + BLOCK, :], w_query, NT).astype(BF)
    w_text = jnp.concatenate([columns_of(weights, 1), columns_of(weights, 2)], 1)
    text_part[...] = dot(dkv[...], w_text, NT).astype(BF)
    for one, (left, right) in enumerate(
        ((normed, dq[...]), (text, dkv[:, :512]), (text, dkv[:, 512:]), (low_grad, mix[...]))
    ):
        grads[...] = dot(left[...], right, TN)
        for s in range(4):
            columns = slice(s * 512 + one * 128, s * 512 + (one + 1) * 128)
            cut_grads(
                place, grads.at[:, s * 128 : (s + 1) * 128], columns, g_own, g_side, g_over, g_low, g_high
            )


def fused_cross_backward(place, after, mine, theirs, cot, gain, weights, normed, text, queries, keys, mix, lse, ids, caption):
    return call(
        cross_bwd_kernel,
        [
            (VMEM, like(1024, 1024, dtype=F32)),
            (VMEM, like(1024, 1024)),
            (VMEM, like(8, 1024, dtype=F32)),
            (VMEM, like(128, 1024)),
        ]
        + [(VMEM, like(*shape)) for shape in GRAD_SHAPES],
        [SMEM] + [VMEM] * 14,
        (place, after, mine, theirs, cot, gain, weights, normed, text, queries, keys, mix, lse, ids, caption),
        [
            pltpu.VMEM((1024, 1024), BF),
            pltpu.VMEM((1024, 512), BF),
            pltpu.VMEM((1024, 512), BF),
            pltpu.VMEM((128, 1024), BF),
            pltpu.VMEM((1024, 512), F32),
        ],
        limit=60,
        flops=9 * 2**30,
        moved=32 * MIB,
    )


def self_bwd_kernel(
    place, after, mine, theirs, base, gain, weights, qkv, mix, lse,
    grad_own, low_grad, norms, dqkv, mix_grad, dk_sum, dv_sum,
):
    core = place[1]

    def keep(rows, value):
        low_grad[rows, :] = value.astype(BF)

        @pl.when(core == (rows.start // 128) % 2)
        def _():
            grad_own[rows.start // 256] = value

    norm_block(lambda rows: after[rows, :], mine, theirs, lambda rows: base[rows, :], (gain, 2), norms, keep)
    w_out = columns_of(weights, 3)
    for low in range(0, 1024, BLOCK):
        mix_grad[low : low + BLOCK, :] = dot(low_grad[low : low + BLOCK, :], w_out).astype(BF)
    causal = causal_mask()

    def pair_step(pair, carry):
        lanes = at(pair * 128, 128)
        k_lanes, v_lanes = at(512 + pair * 128, 128), at(1024 + pair * 128, 128)
        dk_sum[...] = jnp.zeros_like(dk_sum)
        dv_sum[...] = jnp.zeros_like(dv_sum)
        for low in range(0, 1024, BLOCK):
            high = low + BLOCK
            query, grad = qkv[low:high, lanes], mix_grad[low:high, lanes]
            product = (grad.astype(F32) * mix[low:high, lanes].astype(F32)).T
            back = []
            for head in range(2):
                one, one_grad = one_head(query, head), one_head(grad, head)
                delta = jnp.sum(product[head * HD : (head + 1) * HD], 0, keepdims=True)
                total = jnp.zeros((128, BLOCK), F32)
                for start, stop in ((0, low), (low, high)):
                    if start == stop:
                        continue
                    prob, score_grad = head_grads(
                        qkv[start:stop, k_lanes],
                        qkv[start:stop, v_lanes],
                        one,
                        one_grad,
                        lse[pair, head : head + 1, low:high],
                        delta,
                        causal if start == low else None,
                    )
                    dv_sum[start:stop, :] += dot(prob, one_grad)
                    dk_sum[start:stop, :] += dot(score_grad, one)
                    total = total + dot(qkv[start:stop, k_lanes], score_grad, TN)
                back.append(total)
            both = jnp.where(lane_head((128, 1), 0, 0), back[0], back[1])
            dqkv[low:high, lanes] = (both.T * HD**-0.5).astype(BF)
        dqkv[:, k_lanes] = (dk_sum[...] * HD**-0.5).astype(BF)
        dqkv[:, v_lanes] = dv_sum[...].astype(BF)
        return carry

    lax.fori_loop(0, 4, pair_step, 0)


def fused_self_backward(place, after, mine, theirs, base, gain, weights, qkv, mix, lse):
    return call(
        self_bwd_kernel,
        [
            (VMEM, like(4, 128, 1024, dtype=F32)),
            (VMEM, like(1024, 1024)),
            (VMEM, like(8, 1024, dtype=F32)),
            (VMEM, like(1024, 1536)),
        ],
        [SMEM] + [VMEM] * 9,
        (place, after, mine, theirs, base, gain, weights, qkv, mix, lse),
        [pltpu.VMEM((1024, 512), BF), pltpu.VMEM((1024, 128), F32), pltpu.VMEM((1024, 128), F32)],
        limit=60,
        flops=9 * 2**30,
        moved=32 * MIB,
    )


def self_grads_kernel(place, normed, low_grad, dq, dk, dv, mix, g_own, g_side, g_over, g_low, g_high, rows_t, grad_t, grads):
    @pl.when(pl.program_id(0) == 0)
    def _():
        rows_t[...] = normed[...].T
        grad_t[...] = low_grad[...].T

    grads[:, :384] = dot(rows_t[...], jnp.concatenate([dq[...], dk[...], dv[...]], 1))
    grads[:, 384:] = dot(grad_t[...], mix[...])
    cut_grads(place, grads, slice(None), g_own, g_side, g_over, g_low, g_high)


def self_grads(place, normed, low_grad, dqkv, mix):
    square = once(1024, 1024)

    def cut(offset):
        return pl.BlockSpec((1024, 128), lambda i: (0, offset + i))

    return call(
        self_grads_kernel,
        grad_outs(),
        [SMEM, square, square, cut(0), cut(4), cut(8), cut(0)],
        (place, normed, low_grad, dqkv, dqkv, dqkv, mix),
        [pltpu.VMEM((1024, 1024), BF)] * 2 + [pltpu.VMEM((1024, 512), F32)],
        limit=60,
        grid=(4,),
        flops=4 * 2**30,
        moved=12 * MIB,
    )


def self_back_kernel(place, dqkv, weights, kept, sent):
    core = place[1]
    w_in = jnp.concatenate([columns_of(weights, one) for one in range(3)], 1)
    for block in range(4):
        for target, half in ((sent, 1 - core), (kept, core)):
            value = dot(dqkv[at(block * 256 + half * 128, 128), :], w_in, NT)
            target[block] = value.astype(target.dtype)


def self_back(place, dqkv, weights):
    return call(
        self_back_kernel,
        [(VMEM, like(4, 128, 1024, dtype=F32)), (VMEM, like(4, 128, 1024))],
        [SMEM, VMEM, VMEM],
        (place, dqkv, weights),
        limit=60,
        flops=3 * 2**30,
        moved=10 * MIB,
    )


def last_norm_kernel(place, rows, grad_own, mine, theirs, gain, text_part, *outs):
    pieces, norms = outs[:4], outs[4]
    gain_sum, bias_sum = jnp.zeros((8, 1024), F32), jnp.zeros((8, 1024), F32)
    for number in range(4):
        block = (place[2] + number) % 4
        grad = mine[block] + theirs[block].astype(F32)
        back, term = norm_backward(rows[number].astype(F32), norm_row(gain, 0), grad)
        pieces[-number % 4][0:128, :] = (grad_own[block] + back).astype(BF)
        pieces[-number % 4][128:160, :] = text_part[at(block * 32, 32, 32), :]
        gain_sum = gain_sum + jnp.sum(term.reshape(16, 8, 1024), 0)
        bias_sum = bias_sum + jnp.sum(grad.reshape(16, 8, 1024), 0)
    norms[0:1, :] = jnp.sum(gain_sum, 0, keepdims=True)
    norms[1:2, :] = jnp.sum(bias_sum, 0, keepdims=True)


def last_norm(place, rows, grad_own, mine, theirs, gain, text_part):
    return call(
        last_norm_kernel,
        [(VMEM, like(160, 1024))] * 4 + [(VMEM, like(8, 1024, dtype=F32))],
        [SMEM] + [VMEM] * 6,
        (place, rows, grad_own, mine, theirs, gain, text_part),
        limit=60,
        moved=8 * MIB,
    )


def finish_kernel(place, after, out_keep, theirs, *rest):
    messages, rows, sems = rest[:4], rest[4], rest[5]
    core, top = place[1], place[2]
    run_copies(
        [(after.at[at((top + 4 - n) % 4 * 256 + core * 128, 128), :], rows.at[n]) for n in range(4)], sems
    )
    for number in range(4):
        block = (top + 4 - number) % 4
        value = rows[number] + (out_keep[block] + theirs[block].astype(F32))
        messages[number][...] = value.astype(BF)


def finish(place, after, out_keep, theirs):
    return call(
        finish_kernel,
        [(VMEM, like(128, 1024))] * 4,
        [SMEM, ANY] + [VMEM] * 2,
        (place, after, out_keep, theirs),
        [pltpu.VMEM((4, 128, 1024), F32), pltpu.SemaphoreType.DMA((4,))],
        limit=60,
        moved=8 * MIB,
    )


def part_kernel(place, *refs):
    pieces, mine, sent = refs[:4], refs[4], refs[5]
    core, top = place[1], place[2]
    for step, piece in enumerate(pieces):
        image = (top + step) % 4

        @pl.when(image // 2 == core)
        def _():
            mine[image % 2] = piece[...]

        @pl.when(image // 2 != core)
        def _():
            sent[image % 2] = piece[...]


def part_images(place, pieces):
    return call(
        part_kernel,
        [(VMEM, like(2, *pieces[0].shape))] * 2,
        [SMEM] + [VMEM] * 4,
        (place, *pieces),
    )


def land_kernel(place, mine, taken, rows, *text):
    core = place[1]
    for one in range(2):
        rows[one, at(core * 128, 128), :] = mine[one, 0:128, :].astype(rows.dtype)
        rows[one, at((1 - core) * 128, 128), :] = taken[one, 0:128, :].astype(rows.dtype)
        if text:
            text[0][one] = mine[one, 128:160, :].astype(F32) + taken[one, 128:160, :].astype(F32)


def land(place, mine, taken, dtype):
    outs = [(VMEM, like(2, 256, 1024, dtype=dtype))]
    if mine.shape[1] > 128:
        outs.append((VMEM, like(2, 32, 1024, dtype=F32)))
    return call(land_kernel, outs, [SMEM, VMEM, VMEM], (place, mine, taken))


def relay_kernel(over, side, from_side, from_over, to_over, to_side):
    to_over[0:128, :] = (over[0:128, :].astype(F32) + from_side[...].astype(F32)).astype(BF)
    to_over[128:256, :] = over[128:256, :]
    to_side[0:128, :] = side[0:128, :]
    to_side[128:256, :] = (side[128:256, :].astype(F32) + from_over[...].astype(F32)).astype(BF)


def relay(over, side, from_side, from_over):
    return call(
        relay_kernel,
        [(VMEM, like(256, 2048))] * 2,
        [VMEM] * 4,
        (over, side, from_side, from_over),
        limit=60,
        moved=5 * MIB,
    )


def plane_sum_kernel(own, over, side, keep, *sent):
    for s in range(4):
        columns = slice(s * 512, (s + 1) * 512)
        total = own[:, columns].astype(F32) + over[:, columns].astype(F32) + side[:, columns].astype(F32)
        if s:
            sent[s - 1][...] = total.astype(BF)
        else:
            keep[...] = total


def plane_sum(own, over, side):
    return call(
        plane_sum_kernel,
        [(VMEM, like(256, 512, dtype=F32))] + [(VMEM, like(256, 512))] * 3,
        [VMEM] * 3,
        (own, over, side),
        limit=60,
        moved=5 * MIB,
    )


def plane_sum_whole_kernel(place, own, over, side, whole):
    for step in range(4):
        columns = slice(step * 512, (step + 1) * 512)
        total = own[:, columns].astype(F32) + over[:, columns].astype(F32) + side[:, columns].astype(F32)
        whole[at((place[2] + step) % 4 * 256, 256), :] = total.astype(BF)


def plane_sum_whole(place, own, over, side):
    return call(
        plane_sum_whole_kernel,
        [(VMEM, like(1024, 512))],
        [SMEM] + [VMEM] * 3,
        (place, own, over, side),
    )[0]


def line_sum_kernel(place, keep, one, two, three, mine, other):
    core = place[1]
    for target, half in ((other, 1 - core), (mine, core)):
        rows = at(half * 128, 128)
        total = keep[rows, :]
        for part in (one, two, three):
            total = total + part[rows, :].astype(F32)
        target[...] = total.astype(target.dtype)


def line_sum(place, keep, parts):
    return call(
        line_sum_kernel,
        [(VMEM, like(128, 512, dtype=F32)), (VMEM, like(128, 512))],
        [SMEM] + [VMEM] * 4,
        (place, keep, *parts),
        limit=60,
        moved=2 * MIB,
    )


def spread_kernel(place, mine, other, *outs):
    core, columns = place[1], mine.shape[1] // len(outs)
    for one, out in enumerate(outs):
        cut = slice(one * columns, (one + 1) * columns)
        out[:, at(core * columns, columns)] = mine[:, cut].astype(F32)
        out[:, at((1 - core) * columns, columns)] = other[:, cut].astype(F32)


def spread(place, mine, other):
    return call(
        spread_kernel,
        [(VMEM, like(128, 256, dtype=F32))] * 4,
        [SMEM] + [VMEM] * 2,
        (place, mine, other),
        limit=60,
        moved=MIB,
    )


def spread_feed_kernel(place, mine_one, other_one, mine_two, other_two, *outs):
    core = place[1]
    for part, (mine, other) in enumerate(((mine_one, other_one), (mine_two, other_two))):
        for one, out in enumerate(outs):
            cut = slice(one * 256, (one + 1) * 256)
            out[:, at(core * 512 + part * 256, 256)] = mine[:, cut].astype(F32)
            out[:, at((1 - core) * 512 + part * 256, 256)] = other[:, cut].astype(F32)


def spread_feed(place, *halves):
    return call(
        spread_feed_kernel,
        [(VMEM, like(128, 1024, dtype=F32))] * 2,
        [SMEM] + [VMEM] * 4,
        (place, *halves),
        limit=60,
        moved=2 * MIB,
    )


tie = lax.optimization_barrier


def packed_layer(args):
    image_rows, text_rows, segment_ids, cotangent, *others = args
    weights, norms = others[:10], others[10:]
    chip, core, top = lax.axis_index("chip"), lax.axis_index("core"), lax.axis_index("hi")
    place = jnp.stack([chip, core, top, core * 2 + top % 2]).astype(jnp.int32)

    def swap(value):
        return lax.ppermute(value, "core", [(0, 1), (1, 0)])

    def across(value, bit):
        return lax.ppermute(value, "chip", [(i, i ^ bit) for i in range(4)])

    def shift(value, step):
        return lax.ppermute(value, "hi", [((i + step) % 4, i) for i in range(4)])

    def line(part):
        return [shift(part, step) for step in range(1, 4)]

    def exchange(pieces):
        return [pieces[0]] + [shift(piece, step) for step, piece in enumerate(pieces) if step]

    def gather_line(part):
        return lax.all_gather(part, "hi")

    def sides(value):
        return [across(value, 1), across(value, 2)]

    def corners(pair, cut):
        return [across(pair[0][:cut], 2), across(pair[1][cut:], 1)]

    def grad_corners(grads):
        return [across(grads[3], 1), across(grads[4], 2)]

    def grad_sides(grads, got):
        to_over, to_side = relay(grads[2], grads[1], *got)
        return [across(to_over, 2), across(to_side, 1)]

    def halves(total):
        cut = total.reshape(2, 128, 512)
        sent = lax.dynamic_index_in_dim(cut, 1 - core, 0, False)
        return lax.dynamic_index_in_dim(cut, core, 0, False), swap(sent)

    ids_wide = jnp.pad(segment_ids.astype(BF)[:, None, :], ((0, 0), (0, 15), (0, 896)))
    norms_wide = jnp.pad(jnp.stack(norms).astype(BF), ((0, 10), (0, 384)))
    keep, sent, rows_keep, rows_sent, cot_keep, cot_sent = prepare(
        place, image_rows, text_rows, ids_wide, cotangent, norms_wide, weights
    )
    v = {"rows_keep": rows_keep, "cot_keep": cot_keep}
    v["taken"], v["rows_taken"], v["cot_taken"] = swap(sent), swap(rows_sent), swap(cot_sent)
    v = tie(v)
    v["singles"] = join(keep, v.pop("taken"))
    v["near_first"], v["near_second"] = v["singles"][4:]
    v["singles"] = v["singles"][:4]
    v = tie(v)

    v["line"] = line(v["singles"][0])
    v["near_one"] = sides(v["near_first"])
    v["pieces"] = pick(place, v.pop("rows_keep"), v.pop("rows_taken"))
    v["cot_pieces"] = pick(place, v.pop("cot_keep"), v.pop("cot_taken"))
    v = tie(v)

    v["rest_self"] = stack(v.pop("line"))
    v["far_self"] = sides(v["rest_self"])
    v["pieces"] = exchange(v["pieces"])
    line_cross = gather_line(v["singles"][1])
    v = tie(v)

    v["far_self"] += corners(v["far_self"], 384)
    v["near_one"] += corners(v["near_one"], 256)
    v["rows_own"] = stack([piece[None] for piece in v.pop("pieces")])
    v["rows_other"] = swap(v["rows_own"])
    v["rest_cross"] = turn(place, line_cross)
    v = tie(v)

    v["far_cross"] = sides(v["rest_cross"])
    v["cot_pieces"] = exchange(v["cot_pieces"])
    line_one = gather_line(v["singles"][2])
    near = v["near_one"]
    v["w_self"], v["norms"] = assemble(
        place, (v["near_first"], *near[:2], near[2]), (v.pop("rest_self"), *v.pop("far_self")), 0, near[3]
    )
    v["normed_one"], v["qkv"], v["self_mix"], v["self_lse"], v["mine"] = fused_self_forward(
        place, v["rows_own"], v["rows_other"], v["norms"], v["w_self"]
    )
    v = tie(v)

    v["theirs"] = swap(v["mine"])
    v["far_cross"] += corners(v["far_cross"], 384)
    cot_pieces = v.pop("cot_pieces")
    v["cot_own"], v["text"] = arrange(place, cot_pieces)
    v["cot_other"] = swap(v["cot_own"])
    ids = cot_pieces[0][160, :128].astype(jnp.int32)
    v["caption"] = jnp.repeat(ids, 8)[None, :]
    v["ids"] = ids[:, None]
    v["rest_one"] = turn(place, line_one)
    v = tie(v)

    v["far_one"] = sides(v["rest_one"])
    v["near_two"] = sides(v["near_second"])
    line_two = gather_line(v.pop("singles")[3])
    near = v.pop("near_one")
    (v["w_cross"],) = assemble(
        place, (v.pop("near_first"), *near[:2], near[3]), (v.pop("rest_cross"), *v.pop("far_cross")), 256
    )
    v["after_attn"], v["normed_two"], v["queries"], v["keys"], v["cross_mix"], v["cross_lse"], v["mine"] = (
        fused_cross_forward(
            place, v["rows_own"], v.pop("rows_other"), v["mine"], v["theirs"], v["norms"], v["text"], v["ids"],
            v["caption"], v["w_cross"],
        )
    )
    v = tie(v)

    v["theirs"] = swap(v["mine"])
    v["far_one"] += corners(v["far_one"], 384)
    v["near_two"] += corners(v["near_two"], 256)
    v["rest_two"] = turn(place, line_two)
    v = tie(v)

    v["far_two"] = [*sides(v["rest_two"]), across(v["rest_two"], 3)]
    near = v["near_two"]
    (w_one,) = assemble(
        place, (v["near_second"], *near[:2], near[2]), (v.pop("rest_one"), *v.pop("far_one")), 0
    )
    *v["grads_one"], v["after_cross"], v["normed_three"], v["cot"], v["out_sum"], v["back_sum"] = feed_first(
        place, v["after_attn"], v["mine"], v["theirs"], v["norms"], v.pop("cot_own"), v.pop("cot_other"), w_one
    )
    v = tie(v)

    v["got_one"] = grad_corners(v["grads_one"])
    near = v.pop("near_two")
    (w_two,) = assemble(
        place, (v.pop("near_second"), *near[:2], near[3]), (v.pop("rest_two"), *v.pop("far_two")), 256
    )
    *v["grads_two"], v["out_keep"], v["out_sent"], v["mine"] = feed_second(
        place, v.pop("normed_three"), v["cot"], v.pop("out_sum"), v.pop("back_sum"), w_two
    )
    v = tie(v)

    v["theirs"] = swap(v["mine"])
    v["sides_one"] = grad_sides(v["grads_one"], v.pop("got_one"))
    v["got_two"] = grad_corners(v["grads_two"])
    v["grad_cross"], v["part"], v["norms_three"], v["text_part"], *v["grads_three"] = fused_cross_backward(
        place, v["after_cross"], v.pop("mine"), v.pop("theirs"), v.pop("cot"), v["norms"], v.pop("w_cross"),
        v.pop("normed_two"), v.pop("text"), v.pop("queries"), v.pop("keys"), v.pop("cross_mix"),
        v.pop("cross_lse"), v.pop("ids"), v.pop("caption"),
    )
    v = tie(v)

    v["theirs"] = swap(v["part"])
    v["out_theirs"] = swap(v.pop("out_sent"))
    v["to_two"] = relay(v["grads_two"][2], v["grads_two"][1], *v.pop("got_two"))
    v["total_one"] = plane_sum_whole(place, v.pop("grads_one")[0], *v.pop("sides_one"))
    v = tie(v)

    to_two = v.pop("to_two")
    v["sides_two"] = [across(to_two[0], 2), across(to_two[1], 1)]
    v["got_three"] = grad_corners(v["grads_three"])
    line_one = lax.psum_scatter(v.pop("total_one"), "hi", scatter_dimension=0, tiled=True)
    v["grad_own"], v["low_grad"], v["norms_two"], v["dqkv"] = fused_self_backward(
        place, v.pop("after_attn"), v.pop("part"), v.pop("theirs"), v.pop("grad_cross"), v["norms"], v["w_self"],
        v.pop("qkv"), v["self_mix"], v.pop("self_lse"),
    )
    v = tie(v)

    v["sides_three"] = grad_sides(v["grads_three"], v.pop("got_three"))
    v["total_two"] = plane_sum_whole(place, v.pop("grads_two")[0], *v.pop("sides_two"))
    v["grads_four"] = self_grads(place, v.pop("normed_one"), v.pop("low_grad"), v["dqkv"], v.pop("self_mix"))
    v["pieces"] = finish(place, v.pop("after_cross"), v.pop("out_keep"), v.pop("out_theirs"))
    v = tie(v)

    v["got_four"] = grad_corners(v["grads_four"])
    line_two = lax.psum_scatter(v.pop("total_two"), "hi", scatter_dimension=0, tiled=True)
    pieces = exchange(v.pop("pieces"))
    v["kept"], v["sent"] = self_back(place, v.pop("dqkv"), v.pop("w_self"))
    v["theirs"] = swap(v.pop("sent"))
    v["feed_one"] = halves(line_one)
    v = tie(v)

    v["sides_four"] = grad_sides(v["grads_four"], v.pop("got_four"))
    *input_pieces, norms_one = last_norm(
        place, v.pop("rows_own"), v.pop("grad_own"), v.pop("kept"), v.pop("theirs"), v.pop("norms"), v.pop("text_part")
    )
    v["input_pieces"] = exchange(input_pieces)
    total_three = plane_sum_whole(place, v.pop("grads_three")[0], *v.pop("sides_three"))
    line_three = lax.psum_scatter(total_three, "hi", scatter_dimension=0, tiled=True)
    sums = jnp.concatenate([norms_one[:2], 0.5 * v.pop("norms_two")[:2], 0.5 * v.pop("norms_three")[:2]], 0)
    v["sums"] = sums + swap(sums)
    v["feed_two"] = halves(line_two)
    mine, sent = part_images(place, pieces)
    (v["result"],) = land(place, mine, swap(sent), BF)
    v = tie(v)

    sums_four = plane_sum(v.pop("grads_four")[0], *v.pop("sides_four"))
    v["line_four"] = [shift(piece, 3 - i) for i, piece in enumerate(sums_four[1:])]
    v["feed_grads"] = spread_feed(place, *v.pop("feed_one"), *v.pop("feed_two"))
    sums = v.pop("sums")
    sums = sums + across(sums, 1)
    v["sums"] = sums + across(sums, 2)
    mine, sent = part_images(place, v.pop("input_pieces"))
    v["input_grad"], v["text_grad"] = land(place, mine, swap(sent), F32)
    v["kept"] = sums_four[0]
    v = tie(v)

    kept, sent = line_sum(place, v.pop("kept"), v.pop("line_four"))
    own_grads = spread(place, kept, swap(sent))
    cross_grads = spread(place, *halves(line_three))
    sums = v.pop("sums")
    for bit in (1, 2):
        sums = sums + lax.ppermute(sums, "hi", [(i, i ^ bit) for i in range(4)])
    sums = lax.dynamic_slice_in_dim(sums, (chip * 2 + core) * 128, 128, 1)
    return (
        v["result"], v["input_grad"], v["text_grad"], *own_grads, *cross_grads, *v["feed_grads"],
        *[sums[i] for i in range(6)],
    )


def solution(mesh):
    fsdp, tensor = mesh.shape["fsdp"], mesh.shape["tensor"]

    def run(*args):
        images = args[0].shape[0] // fsdp
        tops = 2 * images
        shape = {"chip": fsdp // 2, "core": 2, "hi": tops, "lo": tensor // tops}
        fine = Mesh(mesh.devices.reshape(tuple(shape.values())), tuple(shape))
        first, second = ("chip", "core"), ("hi", "lo")
        wide, weight, norm = P(first, second, None), P(first, second), P(first)
        outs = (wide,) * 3 + (weight,) * 10 + (norm,) * 6
        packed = (
            (fsdp, tensor, images) == (8, 4, 2)
            and args[0].shape[1:] == (1024, 1024)
            and args[1].shape[1:] == (128, 1024)
            and args[12].shape == (1024, 4096)
        )
        return jax.shard_map(
            lambda *local: packed_layer(local) if packed else layer(shape, local),
            mesh=fine,
            in_specs=(wide, wide, P(first, None), wide) + (weight,) * 10 + (norm,) * 6,
            out_specs=outs,
            check_vma=False,
        )(*args)

    return run
```

profile of v0, /device:TPU:9, one launch (start us, length us, event | category | flops | bytes accessed | tf_op | source)
XLA Modules:
  0.0 608.8 jit_solution(13195014925721470390)
XLA Ops:
  37.3 9.6 %collective-permute-done.4.refs_1_ = bf16[256,512]{1,0:T(8,128)(2,1)S(1)} collective-permute-done((bf16[256,512]{1,0:T(8,128)(2,1)}, bf16[256,512]{1,0:T(8,128)(2,1)S(1)}, u32[]{:S(2)}, u32[]{:S(2)}) %collective-permute-start.4) | collective-permute-done | bytes 262176 | tf_op jit(solution)/shard_map/ppermute | solution.py:1649
  46.9 5.6 collective-permute-done.5.refs_2_
  63.1 19.4 %collective-permute-done.11 = bf16[128,1024]{1,0:T(8,128)(2,1)S(1)} collective-permute-done((bf16[128,1024]{1,0:T(8,128)(2,1)S(1)}, bf16[128,1024]{1,0:T(8,128)(2,1)S(1)}, u32[]{:S(2)}, u32[]{:S(2)}) %collective-permute-start.11) | collective-permute-done | bytes 262176 | tf_op jit(solution)/shard_map/ppermute | solution.py:1649
  82.5 10.9 %collective-permute-done.12 = bf16[128,1024]{1,0:T(8,128)(2,1)S(1)} collective-permute-done((bf16[128,1024]{1,0:T(8,128)(2,1)S(1)}, bf16[128,1024]{1,0:T(8,128)(2,1)S(1)}, u32[]{:S(2)}, u32[]{:S(2)}) %collective-permute-start.12) | collective-permute-done | bytes 262176 | tf_op jit(solution)/shard_map/ppermute | solution.py:1649
  106.3 8.3 %collective-permute-done.15.refs_4_ = bf16[256,512]{1,0:T(8,128)(2,1)S(1)} collective-permute-done((bf16[256,512]{1,0:T(8,128)(2,1)S(1)}, bf16[256,512]{1,0:T(8,128)(2,1)S(1)}, u32[]{:S(2)}, u32[]{:S(2)}) %collective-permute-start.15) | collective-permute-done | bytes 262176 | tf_op jit(solution)/shard_map/ppermute | solution.py:1646
  130.9 24.9 %shard_map.347 = (bf16[1024,1024]{1,0:T(8,128)(2,1)}, bf16[1024,1536]{1,0:T(8,128)(2,1)}, bf16[1024,512]{1,0:T(8,128)(2,1)}, f32[4,2,1024]{2,1,0:T(2,128)}, bf16[1024,1024]{1,0:T(8,128)(2,1)}) custom-call(s32[4]{0:T(128)} %pad_add_fusion.place.refs_0_, bf16[4,128,1024]{2,1,0:T(8,128)(2,1)} %shard_map.345.own.rows, bf16[4,128,1024]{2,1,0:T(8,128)(2,1)} %copy-done, ...), custom_call_target="tpu_custom_call" | custom-call | flops 1 | bytes 1 | tf_op jit(solution)/shard_map/pallas_call | solution.py:655
  167.9 18.2 %all-gather.9.cloned.1.call-done = bf16[1024,512]{1,0:T(8,128)(2,1)} async-done(((bf16[256,512]{1,0:T(8,128)(2,1)}), bf16[1024,512]{1,0:T(8,128)(2,1)}) %all-gather.9.cloned.1.call-update) | async-done | bytes 1048592 | tf_op jit(solution)/shard_map/all_gather | solution.py:1658
  196.9 15.8 %shard_map.351 = (f32[1024,1024]{1,0:T(8,128)}, bf16[1024,1024]{1,0:T(8,128)(2,1)}, bf16[1024,512]{1,0:T(8,128)(2,1)}, bf16[128,1024]{1,0:T(8,128)(2,1)}, bf16[1...) custom-call(s32[4]{0:T(128)} %pad_add_fusion.place.refs_0_, ...), custom_call_target="tpu_custom_call" | custom-call | flops 1 | bytes 1 | tf_op jit(solution)/shard_map/pallas_call | solution.py:655
  212.7 5.8 collective-permute-done.29.refs_2_
  229.8 18.1 %all-gather.11.cloned.1.call-done = bf16[1024,512]{1,0:T(8,128)(2,1)} async-done(((bf16[256,512]{1,0:T(8,128)(2,1)}), bf16[1024,512]{1,0:T(8,128)(2,1)}) %all-gather.11.cloned.1.call-update) | async-done | bytes 1048592 | tf_op jit(solution)/shard_map/all_gather | solution.py:1658
  257.8 29.9 %shard_map.354 = (bf16[256,2048]{1,0:T(8,128)(2,1)}, bf16[256,2048]{1,0:T(8,128)(2,1)}, bf16[256,2048]{1,0:T(8,128)(2,1)}, bf16[128,2048]{1,0:T(8,128)(2,1)}, bf...) custom-call(s32[4]{0:T(128)} %pad_add_fusion.place.refs_0_, ...), custom_call_target="tpu_custom_call" | custom-call | flops 1 | bytes 1 | tf_op jit(solution)/shard_map/pallas_call | solution.py:655
  294.6 27.9 %shard_map.356 = (bf16[256,2048]{1,0:T(8,128)(2,1)}, bf16[256,2048]{1,0:T(8,128)(2,1)}, bf16[256,2048]{1,0:T(8,128)(2,1)}, bf16[128,2048]{1,0:T(8,128)(2,1)}, bf...) custom-call(s32[4]{0:T(128)} %pad_add_fusion.place.refs_0_, ...), custom_call_target="tpu_custom_call" | custom-call | flops 1 | bytes 1 | tf_op jit(solution)/shard_map/pallas_call | solution.py:655
  333.3 25.2 %shard_map.357 = (f32[1024,1024]{1,0:T(8,128)}, bf16[1024,1024]{1,0:T(8,128)(2,1)}, f32[8,1024]{1,0:T(8,128)}, bf16[128,1024]{1,0:T(8,128)(2,1)}, bf16[256,2048]...) custom-call(s32[4]{0:T(128)} %pad_add_fusion.place.refs_0_, ...), custom_call_target="tpu_custom_call" | custom-call | flops 1 | bytes 1 | tf_op jit(solution)/shard_map/pallas_call | solution.py:655
  358.5 5.2 collective-permute-done.41.from_side
  375.6 32.1 %shard_map.361 = (f32[4,128,1024]{2,1,0:T(8,128)}, bf16[1024,1024]{1,0:T(8,128)(2,1)}, f32[8,1024]{1,0:T(8,128)}, bf16[1024,1536]{1,0:T(8,128)(2,1)}) custom-call(s32[4]{0:T(128)} %pad_add_fusion.place.refs_0_, f32[1024,1024]{1,0:T(8,128)} %get-tuple-element.854.after, bf16[1024,1024]{1,0:T(8,128)(2,1)} %get-tuple-element.855.mine, ...), custom_call_target="tpu_custom_call" | custom-call | flops 1 | bytes 1 | tf_op jit(solution)/shard_map/pallas_call | solution.py:655
  421.2 12.7 %shard_map.362 = (bf16[256,2048]{1,0:T(8,128)(2,1)}, bf16[256,2048]{1,0:T(8,128)(2,1)}, bf16[256,2048]{1,0:T(8,128)(2,1)}, bf16[128,2048]{1,0:T(8,128)(2,1)}, bf16[128,2048]{1,0:T(8,128)(2,1)}) custom-call(s32[4]{0:T(128)} %pad_add_fusion.place.refs_0_, bf16[1024,1024]{1,0:T(8,128)(2,1)} %get-tuple-element.883.normed, ...), custom_call_target="tpu_custom_call" | custom-call | flops 1 | bytes 1 | tf_op jit(solution)/shard_map/pallas_call | solution.py:655
  436.2 12.9 %shard_map.366 = (f32[4,128,1024]{2,1,0:T(8,128)}, bf16[4,128,1024]{2,1,0:T(8,128)(2,1)}) custom-call(s32[4]{0:T(128)} %pad_add_fusion.place.refs_0_, bf16[1024,1536]{1,0:T(8,128)(2,1)} %get-tuple-element.921.dq.dk.dv.dqkv, bf16[1024,2048]{1,0:T(8,128)(2,1)} %get-tuple-element.922.weights), custom_call_target="tpu_custom_call" | custom-call | flops 1 | bytes 1 | tf_op jit(solution)/shard_map/pallas_call | solution.py:655
  456.7 9.0 %collective-permute-done.55.from_side = bf16[128,2048]{1,0:T(8,128)(2,1)S(1)} collective-permute-done((bf16[128,2048]{1,0:T(8,128)(2,1)}, bf16[128,2048]{1,0:T(8,128)(2,1)S(1)}, u32[]{:S(2)}, u32[]{:S(2)}) %collective-permute-start.55) | collective-permute-done | bytes 524320 | tf_op jit(solution)/shard_map/ppermute | solution.py:1646
  478.3 21.7 %collective-permute-done.63.refs_2_ = bf16[128,1024]{1,0:T(8,128)(2,1)S(1)} collective-permute-done((bf16[128,1024]{1,0:T(8,128)(2,1)}, bf16[128,1024]{1,0:T(8,128)(2,1)S(1)}, u32[]{:S(2)}, u32[]{:S(2)}) %collective-permute-start.63) | collective-permute-done | bytes 262176 | tf_op jit(solution)/shard_map/ppermute | solution.py:1649
  500.0 11.5 %collective-permute-done.64.refs_3_ = bf16[128,1024]{1,0:T(8,128)(2,1)S(1)} collective-permute-done((bf16[128,1024]{1,0:T(8,128)(2,1)S(1)}, bf16[128,1024]{1,0:T(8,128)(2,1)S(1)}, u32[]{:S(2)}, u32[]{:S(2)}) %collective-permute-start.64) | collective-permute-done | bytes 262176 | tf_op jit(solution)/shard_map/ppermute | solution.py:1649
  515.0 5.4 shard_map.367
  531.7 12.1 %collective-permute-done.60.refs_2_ = bf16[160,1024]{1,0:T(8,128)(2,1)S(1)} collective-permute-done((bf16[160,1024]{1,0:T(8,128)(2,1)}, bf16[160,1024]{1,0:T(8,128)(2,1)S(1)}, u32[]{:S(2)}, u32[]{:S(2)}) %collective-permute-start.60) | collective-permute-done | bytes 327712 | tf_op jit(solution)/shard_map/ppermute | solution.py:1649
  543.8 6.9 %collective-permute-done.61.refs_3_ = bf16[160,1024]{1,0:T(8,128)(2,1)S(1)} collective-permute-done((bf16[160,1024]{1,0:T(8,128)(2,1)S(1)}, bf16[160,1024]{1,0:T(8,128)(2,1)S(1)}, u32[]{:S(2)}, u32[]{:S(2)}) %collective-permute-start.61) | collective-permute-done | bytes 327712 | tf_op jit(solution)/shard_map/ppermute | solution.py:1649
  572.4 10.3 %collective-permute-done.71.two = bf16[256,512]{1,0:T(8,128)(2,1)S(1)} collective-permute-done((bf16[256,512]{1,0:T(8,128)(2,1)}, bf16[256,512]{1,0:T(8,128)(2,1)S(1)}, u32[]{:S(2)}, u32[]{:S(2)}) %collective-permute-start.71) | collective-permute-done | bytes 262176 | tf_op jit(solution)/shard_map/ppermute | solution.py:1649
  (349 shorter events, 234.3 us)
Async XLA Ops:
  7.2 96.4 %all-gather.7.cloned.1.call-start = ((), (), s32[]{:S(2)}) async-start(), calls=%async_computation.6 | async-start | bytes 1310720 | tf_op jit(solution)/shard_map/all_gather | solution.py:1658
  55.4 38.1 %collective-permute-start.8 = (bf16[768,512]{1,0:T(8,128)(2,1)}, bf16[768,512]{1,0:T(8,128)(2,1)S(1)}, u32[]{:S(2)}, u32[]{:S(2)}) collective-permute-start(bf16[768,512]{1,0:T(8,128)(2,1)} %shard_map.343.refs_5_), channel_id=1, source_target_pairs={{0,8},{8,0},{16,24},{24,16},{1,9},{9,1},{17,25},{25,17},{2,10},{10... | collective-permute-start | bytes 2359304 | tf_op jit(solution)/shard_map/ppermute | solution.py:1646
  55.7 37.8 %collective-permute-start.9 = (bf16[768,512]{1,0:T(8,128)(2,1)}, bf16[768,512]{1,0:T(8,128)(2,1)S(1)}, u32[]{:S(2)}, u32[]{:S(2)}) collective-permute-start(bf16[768,512]{1,0:T(8,128)(2,1)} %shard_map.343.refs_5_), channel_id=1, source_target_pairs={{0,16},{8,24},{16,0},{24,8},{1,17},{9,25},{17,1},{25,9},{2,18},{10... | collective-permute-start | bytes 2359304 | tf_op jit(solution)/shard_map/ppermute | solution.py:1646
  56.0 130.1 %all-gather.9.cloned.1.call-start = ((), (), s32[]{:S(2)}) async-start(), calls=%async_computation.7 | async-start | bytes 1310720 | tf_op jit(solution)/shard_map/all_gather | solution.py:1658
  118.0 37.8 %collective-permute-start.21 = (bf16[768,512]{1,0:T(8,128)(2,1)}, bf16[768,512]{1,0:T(8,128)(2,1)S(1)}, u32[]{:S(2)}, u32[]{:S(2)}) collective-permute-start(bf16[768,512]{1,0:T(8,128)(2,1)} %shard_map.344.refs_5_), channel_id=1, source_target_pairs={{0,8},{8,0},{16,24},{24,16},{1,9},{9,1},{17,25},{25,17},{2,10},{10... | collective-permute-start | bytes 2359304 | tf_op jit(solution)/shard_map/ppermute | solution.py:1646
  119.5 36.3 %collective-permute-start.22 = (bf16[768,512]{1,0:T(8,128)(2,1)}, bf16[768,512]{1,0:T(8,128)(2,1)S(1)}, u32[]{:S(2)}, u32[]{:S(2)}) collective-permute-start(bf16[768,512]{1,0:T(8,128)(2,1)} %shard_map.344.refs_5_), channel_id=1, source_target_pairs={{0,16},{8,24},{16,0},{24,8},{1,17},{9,25},{17,1},{25,9},{2,18},{10... | collective-permute-start | bytes 2359304 | tf_op jit(solution)/shard_map/ppermute | solution.py:1646
  119.5 36.2 %collective-permute-start.18 = (bf16[176,1024]{1,0:T(8,128)(2,1)}, bf16[176,1024]{1,0:T(8,128)(2,1)S(1)}, u32[]{:S(2)}, u32[]{:S(2)}) collective-permute-start(bf16[176,1024]{1,0:T(8,128)(2,1)} %get-tuple-element.584), channel_id=1, source_target_pairs={{1,0},{2,1},{3,2},{0,3},{5,4},{6,5},{7,6},{4,7},{9,8},{10,9},{11,1... | collective-permute-start | bytes 1081352 | tf_op jit(solution)/shard_map/ppermute | solution.py:1649
  159.0 88.9 %all-gather.11.cloned.1.call-start = ((), (), s32[]{:S(2)}) async-start(), calls=%async_computation.8 | async-start | bytes 1310720 | tf_op jit(solution)/shard_map/all_gather | solution.py:1658
  221.6 231.9 %reduce-scatter.4.cloned.1.call-start = ((), (), s32[]{:S(2)}) async-start(), calls=%async_computation.3 | async-start | bytes 1310720 | tf_op jit(solution)/shard_map/reduce_scatter | solution.py:1793
  250.7 37.1 %collective-permute-start.36 = (bf16[768,512]{1,0:T(8,128)(2,1)}, bf16[768,512]{1,0:T(8,128)(2,1)S(1)}, u32[]{:S(2)}, u32[]{:S(2)}) collective-permute-start(bf16[768,512]{1,0:T(8,128)(2,1)} %shard_map.352.refs_5_), channel_id=1, source_target_pairs={{0,8},{8,0},{16,24},{24,16},{1,9},{9,1},{17,25},{25,17},{2,10},{10... | collective-permute-start | bytes 2359304 | tf_op jit(solution)/shard_map/ppermute | solution.py:1646
  251.9 35.8 %collective-permute-start.37 = (bf16[768,512]{1,0:T(8,128)(2,1)}, bf16[768,512]{1,0:T(8,128)(2,1)S(1)}, u32[]{:S(2)}, u32[]{:S(2)}) collective-permute-start(bf16[768,512]{1,0:T(8,128)(2,1)} %shard_map.352.refs_5_), channel_id=1, source_target_pairs={{0,16},{8,24},{16,0},{24,8},{1,17},{9,25},{17,1},{25,9},{2,18},{10... | collective-permute-start | bytes 2359304 | tf_op jit(solution)/shard_map/ppermute | solution.py:1646
  253.1 34.6 %collective-permute-start.38 = (bf16[768,512]{1,0:T(8,128)(2,1)}, bf16[768,512]{1,0:T(8,128)(2,1)}, u32[]{:S(2)}, u32[]{:S(2)}) collective-permute-start(bf16[768,512]{1,0:T(8,128)(2,1)} %shard_map.352.refs_5_), channel_id=1, source_target_pairs={{0,24},{8,16},{16,8},{24,0},{1,25},{9,17},{17,9},{25,1},{2,26},{10... | collective-permute-start | bytes 2359304 | tf_op jit(solution)/shard_map/ppermute | solution.py:1646
  287.8 34.8 %collective-permute-start.39 = (bf16[128,2048]{1,0:T(8,128)(2,1)}, bf16[128,2048]{1,0:T(8,128)(2,1)S(1)}, u32[]{:S(2)}, u32[]{:S(2)}) collective-permute-start(bf16[128,2048]{1,0:T(8,128)(2,1)} %get-tuple-element.742), channel_id=1, source_target_pairs={{0,8},{8,0},{16,24},{24,16},{1,9},{9,1},{17,25},{25,17},{2,10},{10... | collective-permute-start | bytes 1572872 | tf_op jit(solution)/shard_map/ppermute | solution.py:1646
  328.3 35.4 %collective-permute-start.44 = (bf16[256,2048]{1,0:T(8,128)(2,1)}, bf16[256,2048]{1,0:T(8,128)(2,1)S(1)}, u32[]{:S(2)}, u32[]{:S(2)}) collective-permute-start(bf16[256,2048]{1,0:T(8,128)(2,1)} %get-tuple-element.818), channel_id=1, source_target_pairs={{0,16},{8,24},{16,0},{24,8},{1,17},{9,25},{17,1},{25,9},{2,18},{10... | collective-permute-start | bytes 3145736 | tf_op jit(solution)/shard_map/ppermute | solution.py:1646
  328.7 35.1 %collective-permute-start.45 = (bf16[256,2048]{1,0:T(8,128)(2,1)}, bf16[256,2048]{1,0:T(8,128)(2,1)}, u32[]{:S(2)}, u32[]{:S(2)}) collective-permute-start(bf16[256,2048]{1,0:T(8,128)(2,1)} %get-tuple-element.819), channel_id=1, source_target_pairs={{0,8},{8,0},{16,24},{24,16},{1,9},{9,1},{17,25},{25,17},{2,10},{10... | collective-permute-start | bytes 3145736 | tf_op jit(solution)/shard_map/ppermute | solution.py:1646
  328.9 34.8 %collective-permute-start.41 = (bf16[128,2048]{1,0:T(8,128)(2,1)}, bf16[128,2048]{1,0:T(8,128)(2,1)}, u32[]{:S(2)}, u32[]{:S(2)}) collective-permute-start(bf16[128,2048]{1,0:T(8,128)(2,1)} %get-tuple-element.781), channel_id=1, source_target_pairs={{0,8},{8,0},{16,24},{24,16},{1,9},{9,1},{17,25},{25,17},{2,10},{10... | collective-permute-start | bytes 1572872 | tf_op jit(solution)/shard_map/ppermute | solution.py:1646
  372.4 36.3 %collective-permute-start.51 = (bf16[256,2048]{1,0:T(8,128)(2,1)}, bf16[256,2048]{1,0:T(8,128)(2,1)S(1)}, u32[]{:S(2)}, u32[]{:S(2)}) collective-permute-start(bf16[256,2048]{1,0:T(8,128)(2,1)} %get-tuple-element.878), channel_id=1, source_target_pairs={{0,16},{8,24},{16,0},{24,8},{1,17},{9,25},{17,1},{25,9},{2,18},{10... | collective-permute-start | bytes 3145736 | tf_op jit(solution)/shard_map/ppermute | solution.py:1646
  373.6 35.1 %collective-permute-start.52 = (bf16[256,2048]{1,0:T(8,128)(2,1)}, bf16[256,2048]{1,0:T(8,128)(2,1)}, u32[]{:S(2)}, u32[]{:S(2)}) collective-permute-start(bf16[256,2048]{1,0:T(8,128)(2,1)} %get-tuple-element.879), channel_id=1, source_target_pairs={{0,8},{8,0},{16,24},{24,16},{1,9},{9,1},{17,25},{25,17},{2,10},{10... | collective-permute-start | bytes 3145736 | tf_op jit(solution)/shard_map/ppermute | solution.py:1646
  374.0 155.6 %reduce-scatter.6.cloned.1.call-start = ((), (), s32[]{:S(2)}) async-start(), calls=%async_computation.4 | async-start | bytes 1310720 | tf_op jit(solution)/shard_map/reduce_scatter | solution.py:1807
  374.0 34.7 %collective-permute-start.49 = (bf16[128,2048]{1,0:T(8,128)(2,1)}, bf16[128,2048]{1,0:T(8,128)(2,1)S(1)}, u32[]{:S(2)}, u32[]{:S(2)}) collective-permute-start(bf16[128,2048]{1,0:T(8,128)(2,1)} %get-tuple-element.864), channel_id=1, source_target_pairs={{0,8},{8,0},{16,24},{24,16},{1,9},{9,1},{17,25},{25,17},{2,10},{10... | collective-permute-start | bytes 1572872 | tf_op jit(solution)/shard_map/ppermute | solution.py:1646
  435.9 157.0 %reduce-scatter.8.cloned.1.call-start = ((), (), s32[]{:S(2)}) async-start(), calls=%async_computation.5 | async-start | bytes 1310720 | tf_op jit(solution)/shard_map/reduce_scatter | solution.py:1820
  471.8 39.7 %collective-permute-start.64 = (bf16[128,1024]{1,0:T(8,128)(2,1)S(1)}, bf16[128,1024]{1,0:T(8,128)(2,1)S(1)}, u32[]{:S(2)}, u32[]{:S(2)}) collective-permute-start(bf16[128,1024]{1,0:T(8,128)(2,1)S(1)} %copy-done.57), channel_id=1, source_target_pairs={{3,0},{0,1},{1,2},{2,3},{7,4},{4,5},{5,6},{6,7},{11,8},{8,9},{9,10... | collective-permute-start | bytes 786440 | tf_op jit(solution)/shard_map/ppermute | solution.py:1649
  476.3 74.4 %collective-permute-start.66 = (bf16[256,2048]{1,0:T(8,128)(2,1)}, bf16[256,2048]{1,0:T(8,128)(2,1)S(1)}, u32[]{:S(2)}, u32[]{:S(2)}) collective-permute-start(bf16[256,2048]{1,0:T(8,128)(2,1)} %get-tuple-element.956), channel_id=1, source_target_pairs={{0,16},{8,24},{16,0},{24,8},{1,17},{9,25},{17,1},{25,9},{2,18},{10... | collective-permute-start | bytes 3145736 | tf_op jit(solution)/shard_map/ppermute | solution.py:1646
  477.4 73.3 %collective-permute-start.67 = (bf16[256,2048]{1,0:T(8,128)(2,1)}, bf16[256,2048]{1,0:T(8,128)(2,1)S(1)}, u32[]{:S(2)}, u32[]{:S(2)}) collective-permute-start(bf16[256,2048]{1,0:T(8,128)(2,1)} %get-tuple-element.957), channel_id=1, source_target_pairs={{0,8},{8,0},{16,24},{24,16},{1,9},{9,1},{17,25},{25,17},{2,10},{10... | collective-permute-start | bytes 3145736 | tf_op jit(solution)/shard_map/ppermute | solution.py:1646
  (121 other events, 1719.9 us)
Sparse Core Ops, SparseCore 0:
  56.1 42.9 all-gather.6
  159.1 26.8 all-gather.8
  221.7 26.1 all-gather.10
  374.1 24.4 reduce-scatter.3
  436.0 26.1 reduce-scatter.5
  469.9 43.0 reduce-scatter.7
where the time goes:
time: 613 us; the launch traced here: 609 us
  Pallas kernels  282 us (46%)
  waiting for transfers between devices  195 us (32%)
  starting transfers between devices  79.5 us (13%)
  local copies, waits for them, and re-layouts  30.8 us (5%)
  between operations  15.2 us (2%)
    pallas_call x40, Pallas kernels, call(): pl.pallas_call(body, in_specs=ins, out_specs=out_specs, out_shape=out_sha...  282 us
    ppermute x18, waiting for transfers between devices, shift(): return lax.ppermute(value, 'hi', [((i + step) % 4, i) for i in range(4)])  114 us
    ppermute x41, waiting for transfers between devices, across(): return lax.ppermute(value, 'chip', [(i, i ^ bit) for i in range(4)])  37.8 us
    all_gather x3, waiting for transfers between devices, gather_line(): return lax.all_gather(part, 'hi')  36.3 us
    ppermute x41, starting transfers between devices, across(): return lax.ppermute(value, 'chip', [(i, i ^ bit) for i in range(4)])  32.3 us
    ppermute x18, starting transfers between devices, shift(): return lax.ppermute(value, 'hi', [((i + step) % 4, i) for i in range(4)])  25.5 us
    ppermute x18, starting transfers between devices, swap(): return lax.ppermute(value, 'core', [(0, 1), (1, 0)])  20.1 us
  transfers between devices with their start and end apart: 85, of which 26 were waited for; matrix products, arithmetic and copies ran while one was open for 4% of the time, Pallas kernels for 44%

commit v1 on v0

--- a/solution.py
+++ b/solution.py
@@ -677,7 +677,7 @@
 
 
 def prepare_kernel(place, image, text, ids, cot, norms, wq, wk, wv, wo, cq, ck, cv, co, win, wout, *outs):
-    keep, sent, rows_keep, rows_sent, cot_keep, cot_sent, sems = outs
+    keep, sent, rows_keep, rows_sent, cot_keep, cot_sent, text_pair, sems = outs
     core = place[1]
     copies = []
     for target, which in ((sent, 1 - core), (keep, core)):
@@ -701,16 +701,17 @@
     for target, cots, which in ((rows_sent, cot_sent, 1 - core), (rows_keep, cot_keep, core)):
         for one in range(2):
             copies.append((image.at[one, at(which * 128, 128), :], target.at[one]))
-            copies.append((cot.at[one, at(which * 128, 128), :], cots.at[one, 0:128, :]))
-            copies.append((text.at[one], cots.at[one, 128:160, :]))
-            copies.append((ids.at[one], cots.at[one, 160:176, :]))
+            copies.append((cot.at[one, at(which * 128, 128), :], cots.at[one]))
+    for one in range(2):
+        copies.append((text.at[one], text_pair.at[one, 0:32, :]))
+        copies.append((ids.at[one], text_pair.at[one, 32:48, :]))
     run_copies(copies, sems)
 
 
 def prepare(place, image, text, ids, cot, norms, weights):
     return call(
         prepare_kernel,
-        [(VMEM, like(528, 512))] * 2 + [(VMEM, like(2, 128, 1024))] * 2 + [(VMEM, like(2, 176, 1024))] * 2,
+        [(VMEM, like(528, 512))] * 2 + [(VMEM, like(2, 128, 1024))] * 4 + [(VMEM, like(2, 48, 1024))],
         [SMEM] + [ANY] * 15,
         (place, image, text, ids, cot, norms, *weights),
         [pltpu.SemaphoreType.DMA((42,))],
@@ -740,29 +741,26 @@
     )
 
 
-def join_kernel(*refs):
-    keep, taken, singles, doubles, sems = refs[0], refs[1], refs[2:6], refs[6:8], refs[8]
+def join_kernel(place, keep, taken, *refs):
+    singles, near, sems = refs[:4], refs[4], refs[5]
     copies = []
-    for group in range(4):
-        for half, source in enumerate((keep, taken)):
+    for half, source in enumerate((keep, taken)):
+        core = place[1] ^ half
+        for group in range(4):
             part = source.at[group * 128 : (group + 1) * 128, :]
-            copies.append((part, singles[group].at[half * 128 : (half + 1) * 128, :]))
-            low = (group % 2) * 256 + half * 128
-            copies.append((part, doubles[group // 2].at[low : low + 128, :]))
-    for half, source in enumerate((keep, taken)):
-        low = 512 + half * 16
-        copies.append((source.at[512:528, :], doubles[0].at[low : low + 16, :]))
+            copies.append((part, singles[group].at[at(core * 128, 128), :]))
+        copies.append((source.at[0:128, :], near.at[at(core * 128, 128), :]))
+        copies.append((source.at[512:528, :], near.at[at(256 + core * 16, 16, 16), :]))
     run_copies(copies, sems)
 
 
-def join(keep, taken):
+def join(place, keep, taken):
     return call(
         join_kernel,
-        [(VMEM, like(256, 512))] * 4 + [(VMEM, like(544, 512)), (VMEM, like(512, 512))],
-        [ANY] * 2,
-        (keep, taken),
-        [pltpu.SemaphoreType.DMA((18,))],
-        limit=60,
+        [(VMEM, like(256, 512))] * 4 + [(VMEM, like(288, 512))],
+        [SMEM] + [ANY] * 2,
+        (place, keep, taken),
+        [pltpu.SemaphoreType.DMA((12,))],
     )
 
 
@@ -788,110 +786,105 @@
 
 
 def arrange_kernel(place, *refs):
-    messages, rows, text, sems = refs[:4], refs[4], refs[5], refs[6]
-    copies = []
-    for number, message in enumerate(messages):
-        copies.append((message.at[0:128, :], rows.at[number]))
-        copies.append((message.at[128:160, :], text.at[at((place[2] + number) % 4 * 32, 32, 32), :]))
-    run_copies(copies, sems)
+    messages, text, sems = refs[:4], refs[4], refs[5]
+    run_copies(
+        [(m.at[0:32, :], text.at[at((place[2] + i) % 4 * 32, 32, 32), :]) for i, m in enumerate(messages)], sems
+    )
 
 
 def arrange(place, messages):
     return call(
         arrange_kernel,
-        [(VMEM, like(4, 128, 1024)), (VMEM, like(128, 1024))],
+        [(VMEM, like(128, 1024))],
         [SMEM] + [ANY] * 4,
         (place, *messages),
-        [pltpu.SemaphoreType.DMA((8,))],
-    )
-
-
-def turn_kernel(place, whole, rest, sems):
-    run_copies(
-        [(whole.at[(place[2] + step) % 4], rest.at[(step - 1) * 256 : step * 256, :]) for step in range(1, 4)], sems
-    )
-
-
-def turn(place, whole):
-    return call(
-        turn_kernel,
-        [(VMEM, like(768, 512))],
-        [SMEM, ANY],
-        (place, whole),
-        [pltpu.SemaphoreType.DMA((3,))],
+        [pltpu.SemaphoreType.DMA((4,))],
     )[0]
 
 
-def assemble_kernel(place, *refs, low, far_parts, norms):
-    own, side, over, corner, rest, rside, rover = refs[:7]
-    rcorner = refs[7 : 7 + far_parts]
-    outs = refs[7 + far_parts :]
-    whole, buffer, loads, stores = outs[0], outs[-3], outs[-2], outs[-1]
-    chip, core = place[0], place[1]
-    batches = []
-    for source in range(4):
-        copies = []
-        for half in range(2):
-            row = at((chip ^ source) * 256 + (core ^ half) * 128, 128)
-            near = (own, side, over, corner)[source]
-            first = half * 128 + (0 if source == 3 else low)
-            copies.append((near.at[first : first + 128, :], buffer.at[row, 0:512]))
-            for step in range(3):
-                first = step * 256 + half * 128
-                far = (rest, rside, rover, rcorner[first * far_parts // 768])[source]
-                if source == 3:
-                    first %= 768 // far_parts
-                columns = slice((step + 1) * 512, (step + 2) * 512)
-                copies.append((far.at[first : first + 128, :], buffer.at[row, columns]))
-        batches.append([pltpu.make_async_copy(a, b, loads.at[source * 8 + i]) for i, (a, b) in enumerate(copies)])
-    for batch in batches:
-        for copy in batch:
+def gather_copies(batches, buffer, whole, rows_of, loads, stores, extra=()):
+    started = []
+    for i, batch in enumerate(batches):
+        copies = [pltpu.make_async_copy(a, b, loads.at[i * 8 + j]) for j, (a, b) in enumerate(batch)]
+        for copy in copies:
             copy.start()
-    stored = []
-    if norms:
-        pairs = []
-        for source, piece in enumerate((own, side, over, outs[1])):
-            for half in range(2):
-                column = (chip ^ source) * 256 + (core ^ half) * 128
-                first = (256 if source == 3 else 512) + half * 16
-                pairs.append((piece.at[first : first + 16, 0:128], outs[2].at[:, at(column, 128)]))
-        for i, (a, b) in enumerate(pairs):
-            stored.append(pltpu.make_async_copy(a, b, stores.at[4 + i]))
-            stored[-1].start()
-    for source, batch in enumerate(batches):
-        for copy in batch:
+        started.append(copies)
+    stored = [pltpu.make_async_copy(a, b, stores.at[4 + i]) for i, (a, b) in enumerate(extra)]
+    for copy in stored:
+        copy.start()
+    for i, copies in enumerate(started):
+        for copy in copies:
             copy.wait()
-        rows = at((chip ^ source) * 256, 256)
-        stored.append(pltpu.make_async_copy(buffer.at[rows, :], whole.at[rows, :], stores.at[source]))
+        rows = rows_of(i)
+        stored.append(pltpu.make_async_copy(buffer.at[rows, :], whole.at[rows, :], stores.at[i]))
         stored[-1].start()
     for copy in stored:
         copy.wait()
 
 
-def assemble(place, near, far, low, norms=None):
-    outs = [(ANY, like(1024, 2048))]
-    operands = (place, *near, *far)
-    if norms is not None:
-        outs.append((VMEM, like(16, 1024)))
-        operands += (norms,)
-
-    def body(*refs):
-        count = len(operands)
-        if norms is None:
-            assemble_kernel(*refs, low=low, far_parts=len(far) - 3, norms=False)
-        else:
-            assemble_kernel(
-                *refs[: count - 1], refs[count], refs[count - 1], *refs[count + 1 :],
-                low=low, far_parts=len(far) - 3, norms=True,
-            )
-
-    return call(
-        body,
-        outs,
-        [SMEM] + [ANY] * (len(operands) - 1),
-        operands,
-        [pltpu.VMEM((1024, 2048), BF), pltpu.SemaphoreType.DMA((32,)), pltpu.SemaphoreType.DMA((12,))],
-    )
+def assemble_first_kernel(place, *refs):
+    near, far = refs[:5], refs[5:10]
+    whole, norms, buffer, loads, stores = refs[10:]
+    chip, top = place[0], place[2]
+    batches, extra = [], []
+    for source in range(4):
+        batch = []
+        for half in range(2):
+            row = at((chip ^ source) * 256 + half * 128, 128)
+            piece, first = (near[source], half * 128) if source < 3 else (near[3 + half], 0)
+            batch.append((piece.at[first : first + 128, :], buffer.at[row, at(top * 512, 512, 512)]))
+            low = 256 + half * 16 if source < 3 else 128 + half * 16
+            piece = near[source] if source < 3 else near[4]
+            column = at((chip ^ source) * 256 + half * 128, 128)
+            extra.append((piece.at[low : low + 16, 0:128], norms.at[:, column]))
+            for step in range(3):
+                first = step * 256 + half * 128
+                piece = far[source] if source < 3 else far[3 + first // 384]
+                first = first if source < 3 else first % 384
+                columns = at((top + 1 + step) % 4 * 512, 512, 512)
+                batch.append((piece.at[first : first + 128, :], buffer.at[row, columns]))
+        batches.append(batch)
+    gather_copies(batches, buffer, whole, lambda i: at((chip ^ i) * 256, 256), loads, stores, extra)
+
+
+ASSEMBLE_SCRATCH = [
+    pltpu.VMEM((1024, 2048), BF),
+    pltpu.SemaphoreType.DMA((32,)),
+    pltpu.SemaphoreType.DMA((12,)),
+]
+
+
+def assemble_first(place, near, far):
+    return call(
+        assemble_first_kernel,
+        [(ANY, like(1024, 2048)), (VMEM, like(16, 1024))],
+        [SMEM] + [ANY] * 10,
+        (place, *near, *far),
+        ASSEMBLE_SCRATCH,
+    )
+
+
+def assemble_kernel(place, own, side, over, low, high, whole, buffer, loads, stores):
+    chip = place[0]
+    batches = []
+    for source in range(4):
+        batch = []
+        for top in range(4):
+            piece = (own, side, over, low if top < 2 else high)[source]
+            rows, columns = at((chip ^ source) * 256, 256), slice(top * 512, (top + 1) * 512)
+            batch.append((piece.at[top % 2 if source == 3 else top], buffer.at[rows, columns]))
+        batches.append(batch)
+    gather_copies(batches, buffer, whole, lambda i: at((chip ^ i) * 256, 256), loads, stores)
+
+
+def assemble(place, own, others):
+    return call(
+        assemble_kernel,
+        [(ANY, like(1024, 2048))],
+        [SMEM] + [ANY] * 5,
+        (place, own, *others),
+        ASSEMBLE_SCRATCH,
+    )[0]
 
 
 def norm_row(norms, one):
@@ -1084,7 +1077,7 @@
 
 def feed_first_kernel(
     place, after, mine, theirs, norms, cot_own, cot_other, weights,
-    g_own, g_side, g_over, g_low, g_high, after_cross, normed, cot, out_sum, back_sum, rows_t, cot_t, grads,
+    g_whole, after_cross, normed, cot, out_sum, back_sum, rows_t, cot_t, grads,
 ):
     @pl.when(pl.program_id(0) == 0)
     def _():
@@ -1099,10 +1092,14 @@
         rows_t[...] = normed[...].T
         cot_t[...] = cot[...].T
         out_sum[...] = jnp.zeros_like(out_sum)
+        for block in range(4):
+            rows = at(block * 256 + place[1] * 128, 128)
+            out_sum[rows, :] = after_cross[rows, :]
         back_sum[...] = jnp.zeros_like(back_sum)
 
     feed_step(normed, cot, rows_t, cot_t, weights, out_sum, back_sum, grads)
-    cut_grads(place, grads, slice(None), g_own, g_side, g_over, g_low, g_high)
+    for chip in range(4):
+        g_whole[chip, 0] = grads[chip * 256 : (chip + 1) * 256, :].astype(BF)
 
 
 def feed_second_kernel(
@@ -1118,7 +1115,7 @@
         out_sum[...] = out_in[...]
         back_sum[...] = back_in[...]
 
-    feed_step(normed, cot, rows_t, cot_t, weights, out_sum, back_sum, grads)
+    feed_step(normed, cot, rows_t, cot_t, weights[:, 0].reshape(1024, 512), out_sum, back_sum, grads)
     cut_grads(place, grads, slice(None), g_own, g_side, g_over, g_low, g_high)
 
     @pl.when(step == 3)
@@ -1145,7 +1142,7 @@
     square = once(1024, 1024)
     return call(
         feed_first_kernel,
-        grad_outs()
+        [(pl.BlockSpec((4, 1, 256, 512), lambda i: (0, i, 0, 0)), like(4, 4, 256, 512))]
         + [
             (square, like(1024, 1024, dtype=F32)),
             (square, like(1024, 1024)),
@@ -1174,7 +1171,7 @@
             (once(4, 128, 1024), like(4, 128, 1024)),
             (square, like(1024, 1024)),
         ],
-        [SMEM, square, square, square, square, pl.BlockSpec((1024, 512), lambda i: (0, i))],
+        [SMEM, square, square, square, square, pl.BlockSpec((4, 1, 256, 512), lambda i: (0, i, 0, 0))],
         (place, normed, cot, out_in, back_in, weights),
         [pltpu.VMEM((1024, 1024), F32)] * 2
         + [pltpu.VMEM((1024, 1024), BF)] * 2
@@ -1425,8 +1422,7 @@
     )
 
 
-def last_norm_kernel(place, rows, grad_own, mine, theirs, gain, text_part, *outs):
-    pieces, norms = outs[:4], outs[4]
+def last_norm_kernel(place, rows, grad_own, mine, theirs, gain, text_part, sums_two, sums_three, *pieces):
     gain_sum, bias_sum = jnp.zeros((8, 1024), F32), jnp.zeros((8, 1024), F32)
     for number in range(4):
         block = (place[2] + number) % 4
@@ -1436,42 +1432,34 @@
         pieces[-number % 4][128:160, :] = text_part[at(block * 32, 32, 32), :]
         gain_sum = gain_sum + jnp.sum(term.reshape(16, 8, 1024), 0)
         bias_sum = bias_sum + jnp.sum(grad.reshape(16, 8, 1024), 0)
-    norms[0:1, :] = jnp.sum(gain_sum, 0, keepdims=True)
-    norms[1:2, :] = jnp.sum(bias_sum, 0, keepdims=True)
-
-
-def last_norm(place, rows, grad_own, mine, theirs, gain, text_part):
+    sums = [jnp.sum(gain_sum, 0, keepdims=True), jnp.sum(bias_sum, 0, keepdims=True)]
+    sums += [0.5 * sums_two[0:2, :], 0.5 * sums_three[0:2, :], jnp.zeros((10, 1024), F32)]
+    sums = jnp.concatenate(sums, 0).astype(BF)
+    for piece in pieces:
+        piece[160:176, :] = sums
+
+
+def last_norm(place, rows, grad_own, mine, theirs, gain, text_part, sums_two, sums_three):
     return call(
         last_norm_kernel,
-        [(VMEM, like(160, 1024))] * 4 + [(VMEM, like(8, 1024, dtype=F32))],
-        [SMEM] + [VMEM] * 6,
-        (place, rows, grad_own, mine, theirs, gain, text_part),
-        limit=60,
-        moved=8 * MIB,
-    )
-
-
-def finish_kernel(place, after, out_keep, theirs, *rest):
-    messages, rows, sems = rest[:4], rest[4], rest[5]
-    core, top = place[1], place[2]
-    run_copies(
-        [(after.at[at((top + 4 - n) % 4 * 256 + core * 128, 128), :], rows.at[n]) for n in range(4)], sems
-    )
-    for number in range(4):
-        block = (top + 4 - number) % 4
-        value = rows[number] + (out_keep[block] + theirs[block].astype(F32))
-        messages[number][...] = value.astype(BF)
-
-
-def finish(place, after, out_keep, theirs):
+        [(VMEM, like(176, 1024))] * 4,
+        [SMEM] + [VMEM] * 8,
+        (place, rows, grad_own, mine, theirs, gain, text_part, sums_two, sums_three),
+    )
+
+
+def finish_kernel(place, out_keep, theirs, *pieces):
+    for number, piece in enumerate(pieces):
+        block = (place[2] + 4 - number) % 4
+        piece[...] = (out_keep[block] + theirs[block].astype(F32)).astype(BF)
+
+
+def finish(place, out_keep, theirs):
     return call(
         finish_kernel,
         [(VMEM, like(128, 1024))] * 4,
-        [SMEM, ANY] + [VMEM] * 2,
-        (place, after, out_keep, theirs),
-        [pltpu.VMEM((4, 128, 1024), F32), pltpu.SemaphoreType.DMA((4,))],
-        limit=60,
-        moved=8 * MIB,
+        [SMEM] + [VMEM] * 2,
+        (place, out_keep, theirs),
     )
 
 
@@ -1489,6 +1477,13 @@
         def _():
             sent[image % 2] = piece[...]
 
+    if pieces[0].shape[0] > 160:
+        total = 0.0
+        for piece in pieces:
+            total = total + piece[160:176, :].astype(F32)
+        mine[0, 160:176, :] = total.astype(BF)
+        sent[0, 160:176, :] = total.astype(BF)
+
 
 def part_images(place, pieces):
     return call(
@@ -1499,19 +1494,21 @@
     )
 
 
-def land_kernel(place, mine, taken, rows, *text):
+def land_kernel(place, mine, taken, rows, *more):
     core = place[1]
     for one in range(2):
         rows[one, at(core * 128, 128), :] = mine[one, 0:128, :].astype(rows.dtype)
         rows[one, at((1 - core) * 128, 128), :] = taken[one, 0:128, :].astype(rows.dtype)
-        if text:
-            text[0][one] = mine[one, 128:160, :].astype(F32) + taken[one, 128:160, :].astype(F32)
+        if more:
+            more[0][one] = mine[one, 128:160, :].astype(F32) + taken[one, 128:160, :].astype(F32)
+    if more:
+        more[1][...] = mine[0, 160:168, :].astype(F32) + taken[0, 160:168, :].astype(F32)
 
 
 def land(place, mine, taken, dtype):
     outs = [(VMEM, like(2, 256, 1024, dtype=dtype))]
     if mine.shape[1] > 128:
-        outs.append((VMEM, like(2, 32, 1024, dtype=F32)))
+        outs += [(VMEM, like(2, 32, 1024, dtype=F32)), (VMEM, like(8, 1024, dtype=F32))]
     return call(land_kernel, outs, [SMEM, VMEM, VMEM], (place, mine, taken))
 
 
@@ -1533,9 +1530,9 @@
     )
 
 
-def plane_sum_kernel(own, over, side, keep, *sent):
+def plane_sum_kernel(place, own, over, side, keep, *sent):
     for s in range(4):
-        columns = slice(s * 512, (s + 1) * 512)
+        columns = at((place[2] + s) % 4 * 512, 512, 512)
         total = own[:, columns].astype(F32) + over[:, columns].astype(F32) + side[:, columns].astype(F32)
         if s:
             sent[s - 1][...] = total.astype(BF)
@@ -1543,30 +1540,30 @@
             keep[...] = total
 
 
-def plane_sum(own, over, side):
+def plane_sum(place, own, over, side):
     return call(
         plane_sum_kernel,
         [(VMEM, like(256, 512, dtype=F32))] + [(VMEM, like(256, 512))] * 3,
-        [VMEM] * 3,
-        (own, over, side),
+        [SMEM] + [VMEM] * 3,
+        (place, own, over, side),
         limit=60,
         moved=5 * MIB,
     )
 
 
-def plane_sum_whole_kernel(place, own, over, side, whole):
+def plane_sum_whole_kernel(own, over, side, whole):
     for step in range(4):
         columns = slice(step * 512, (step + 1) * 512)
         total = own[:, columns].astype(F32) + over[:, columns].astype(F32) + side[:, columns].astype(F32)
-        whole[at((place[2] + step) % 4 * 256, 256), :] = total.astype(BF)
-
-
-def plane_sum_whole(place, own, over, side):
+        whole[step * 256 : (step + 1) * 256, :] = total.astype(BF)
+
+
+def plane_sum_whole(own, over, side):
     return call(
         plane_sum_whole_kernel,
         [(VMEM, like(1024, 512))],
-        [SMEM] + [VMEM] * 3,
-        (place, own, over, side),
+        [VMEM] * 3,
+        (own, over, side),
     )[0]
 
 
@@ -1677,66 +1674,62 @@
 
     ids_wide = jnp.pad(segment_ids.astype(BF)[:, None, :], ((0, 0), (0, 15), (0, 896)))
     norms_wide = jnp.pad(jnp.stack(norms).astype(BF), ((0, 10), (0, 384)))
-    keep, sent, rows_keep, rows_sent, cot_keep, cot_sent = prepare(
+    keep, sent, rows_keep, rows_sent, cot_keep, cot_sent, text_pair = prepare(
         place, image_rows, text_rows, ids_wide, cotangent, norms_wide, weights
     )
-    v = {"rows_keep": rows_keep, "cot_keep": cot_keep}
+    v = {"rows_keep": rows_keep, "cot_keep": cot_keep, "text_pair": text_pair}
     v["taken"], v["rows_taken"], v["cot_taken"] = swap(sent), swap(rows_sent), swap(cot_sent)
-    v = tie(v)
-    v["singles"] = join(keep, v.pop("taken"))
-    v["near_first"], v["near_second"] = v["singles"][4:]
-    v["singles"] = v["singles"][:4]
-    v = tie(v)
-
-    v["line"] = line(v["singles"][0])
-    v["near_one"] = sides(v["near_first"])
+    v["text_taken"] = swap(text_pair)
+    v = tie(v)
+    *v["singles"], v["near"] = join(place, keep, v.pop("taken"))
+    v = tie(v)
+
+    v["near"] = [v["near"], *sides(v["near"])]
+    lines = line(v["singles"][0])
     v["pieces"] = pick(place, v.pop("rows_keep"), v.pop("rows_taken"))
     v["cot_pieces"] = pick(place, v.pop("cot_keep"), v.pop("cot_taken"))
-    v = tie(v)
-
-    v["rest_self"] = stack(v.pop("line"))
-    v["far_self"] = sides(v["rest_self"])
-    v["pieces"] = exchange(v["pieces"])
+    v["text_pieces"] = pick(place, v.pop("text_pair"), v.pop("text_taken"))
+    v = tie(v)
+    v["near"] += corners(v["near"][1:], 128)
+    v["line"] = lines
+    v = tie(v)
+
+    rest = stack(v.pop("line"))
+    v["far_self"] = [rest, *sides(rest)]
+    pieces = exchange(v.pop("pieces"))
     line_cross = gather_line(v["singles"][1])
     v = tie(v)
-
-    v["far_self"] += corners(v["far_self"], 384)
-    v["near_one"] += corners(v["near_one"], 256)
+    v["far_self"] += corners(v["far_self"][1:], 384)
+    v["pieces"], v["line_cross"] = pieces, line_cross
+    v = tie(v)
     v["rows_own"] = stack([piece[None] for piece in v.pop("pieces")])
     v["rows_other"] = swap(v["rows_own"])
-    v["rest_cross"] = turn(place, line_cross)
-    v = tie(v)
-
-    v["far_cross"] = sides(v["rest_cross"])
-    v["cot_pieces"] = exchange(v["cot_pieces"])
+    v["w_self"], v["norms"] = assemble_first(place, v.pop("near"), v.pop("far_self"))
     line_one = gather_line(v["singles"][2])
-    near = v["near_one"]
-    v["w_self"], v["norms"] = assemble(
-        place, (v["near_first"], *near[:2], near[2]), (v.pop("rest_self"), *v.pop("far_self")), 0, near[3]
-    )
+    v = tie(v)
+
+    v["far_cross"] = sides(v["line_cross"])
+    v["text_pieces"] = exchange(v["text_pieces"])
+    v["line_one"] = line_one
     v["normed_one"], v["qkv"], v["self_mix"], v["self_lse"], v["mine"] = fused_self_forward(
         place, v["rows_own"], v["rows_other"], v["norms"], v["w_self"]
     )
     v = tie(v)
 
     v["theirs"] = swap(v["mine"])
-    v["far_cross"] += corners(v["far_cross"], 384)
-    cot_pieces = v.pop("cot_pieces")
-    v["cot_own"], v["text"] = arrange(place, cot_pieces)
-    v["cot_other"] = swap(v["cot_own"])
-    ids = cot_pieces[0][160, :128].astype(jnp.int32)
+    v["far_cross"] += corners(v["far_cross"], 2)
+    line_two = gather_line(v.pop("singles")[3])
+    text_pieces = v.pop("text_pieces")
+    v["text"] = arrange(place, text_pieces)
+    ids = text_pieces[0][32, :128].astype(jnp.int32)
     v["caption"] = jnp.repeat(ids, 8)[None, :]
     v["ids"] = ids[:, None]
-    v["rest_one"] = turn(place, line_one)
-    v = tie(v)
-
-    v["far_one"] = sides(v["rest_one"])
-    v["near_two"] = sides(v["near_second"])
-    line_two = gather_line(v.pop("singles")[3])
-    near = v.pop("near_one")
-    (v["w_cross"],) = assemble(
-        place, (v.pop("near_first"), *near[:2], near[3]), (v.pop("rest_cross"), *v.pop("far_cross")), 256
-    )
+    v = tie(v)
+
+    v["far_one"] = sides(v["line_one"])
+    v["line_two"] = line_two
+    v["cot_pieces"] = exchange(v["cot_pieces"])
+    v["w_cross"] = assemble(place, v.pop("line_cross"), v.pop("far_cross"))
     v["after_attn"], v["normed_two"], v["queries"], v["keys"], v["cross_mix"], v["cross_lse"], v["mine"] = (
         fused_cross_forward(
             place, v["rows_own"], v.pop("rows_other"), v["mine"], v["theirs"], v["norms"], v["text"], v["ids"],
@@ -1746,51 +1739,46 @@
     v = tie(v)
 
     v["theirs"] = swap(v["mine"])
-    v["far_one"] += corners(v["far_one"], 384)
-    v["near_two"] += corners(v["near_two"], 256)
-    v["rest_two"] = turn(place, line_two)
-    v = tie(v)
-
-    v["far_two"] = [*sides(v["rest_two"]), across(v["rest_two"], 3)]
-    near = v["near_two"]
-    (w_one,) = assemble(
-        place, (v["near_second"], *near[:2], near[2]), (v.pop("rest_one"), *v.pop("far_one")), 0
-    )
-    *v["grads_one"], v["after_cross"], v["normed_three"], v["cot"], v["out_sum"], v["back_sum"] = feed_first(
+    v["far_one"] += corners(v["far_one"], 2)
+    v["cot_own"] = stack([piece[None] for piece in v.pop("cot_pieces")])
+    v["cot_other"] = swap(v["cot_own"])
+    w_two = lax.all_gather(v.pop("line_two"), "chip")
+    v = tie(v)
+
+    v["w_two"] = w_two
+    w_one = assemble(place, v.pop("line_one"), v.pop("far_one"))
+    v["grads_one"], v["after_cross"], v["normed_three"], v["cot"], v["out_sum"], v["back_sum"] = feed_first(
         place, v["after_attn"], v["mine"], v["theirs"], v["norms"], v.pop("cot_own"), v.pop("cot_other"), w_one
     )
     v = tie(v)
 
-    v["got_one"] = grad_corners(v["grads_one"])
-    near = v.pop("near_two")
-    (w_two,) = assemble(
-        place, (v.pop("near_second"), *near[:2], near[3]), (v.pop("rest_two"), *v.pop("far_two")), 256
-    )
+    total_one = lax.psum_scatter(v.pop("grads_one"), "chip", scatter_dimension=0, tiled=False)
     *v["grads_two"], v["out_keep"], v["out_sent"], v["mine"] = feed_second(
-        place, v.pop("normed_three"), v["cot"], v.pop("out_sum"), v.pop("back_sum"), w_two
+        place, v.pop("normed_three"), v["cot"], v.pop("out_sum"), v.pop("back_sum"), v.pop("w_two")
     )
     v = tie(v)
 
     v["theirs"] = swap(v["mine"])
-    v["sides_one"] = grad_sides(v["grads_one"], v.pop("got_one"))
+    v["out_theirs"] = swap(v.pop("out_sent"))
+    v = tie(v)
     v["got_two"] = grad_corners(v["grads_two"])
+    v["pieces"] = exchange(finish(place, v.pop("out_keep"), v.pop("out_theirs")))
     v["grad_cross"], v["part"], v["norms_three"], v["text_part"], *v["grads_three"] = fused_cross_backward(
-        place, v["after_cross"], v.pop("mine"), v.pop("theirs"), v.pop("cot"), v["norms"], v.pop("w_cross"),
+        place, v.pop("after_cross"), v.pop("mine"), v.pop("theirs"), v.pop("cot"), v["norms"], v.pop("w_cross"),
         v.pop("normed_two"), v.pop("text"), v.pop("queries"), v.pop("keys"), v.pop("cross_mix"),
         v.pop("cross_lse"), v.pop("ids"), v.pop("caption"),
     )
     v = tie(v)
 
     v["theirs"] = swap(v["part"])
-    v["out_theirs"] = swap(v.pop("out_sent"))
+    v["total_one"] = total_one
     v["to_two"] = relay(v["grads_two"][2], v["grads_two"][1], *v.pop("got_two"))
-    v["total_one"] = plane_sum_whole(place, v.pop("grads_one")[0], *v.pop("sides_one"))
     v = tie(v)
 
     to_two = v.pop("to_two")
     v["sides_two"] = [across(to_two[0], 2), across(to_two[1], 1)]
     v["got_three"] = grad_corners(v["grads_three"])
-    line_one = lax.psum_scatter(v.pop("total_one"), "hi", scatter_dimension=0, tiled=True)
+    v["line_one"] = lax.psum_scatter(v.pop("total_one"), "hi", scatter_dimension=0, tiled=False)
     v["grad_own"], v["low_grad"], v["norms_two"], v["dqkv"] = fused_self_backward(
         place, v.pop("after_attn"), v.pop("part"), v.pop("theirs"), v.pop("grad_cross"), v["norms"], v["w_self"],
         v.pop("qkv"), v["self_mix"], v.pop("self_lse"),
@@ -1798,54 +1786,46 @@
     v = tie(v)
 
     v["sides_three"] = grad_sides(v["grads_three"], v.pop("got_three"))
-    v["total_two"] = plane_sum_whole(place, v.pop("grads_two")[0], *v.pop("sides_two"))
+    total_two = plane_sum_whole(v.pop("grads_two")[0], *v.pop("sides_two"))
+    line_two = lax.psum_scatter(total_two, "hi", scatter_dimension=0, tiled=True)
     v["grads_four"] = self_grads(place, v.pop("normed_one"), v.pop("low_grad"), v["dqkv"], v.pop("self_mix"))
-    v["pieces"] = finish(place, v.pop("after_cross"), v.pop("out_keep"), v.pop("out_theirs"))
+    mine, sent = part_images(place, v.pop("pieces"))
+    (v["result"],) = land(place, mine, swap(sent), BF)
+    v["feed_one"] = halves(v.pop("line_one"))
     v = tie(v)
 
     v["got_four"] = grad_corners(v["grads_four"])
-    line_two = lax.psum_scatter(v.pop("total_two"), "hi", scatter_dimension=0, tiled=True)
-    pieces = exchange(v.pop("pieces"))
-    v["kept"], v["sent"] = self_back(place, v.pop("dqkv"), v.pop("w_self"))
-    v["theirs"] = swap(v.pop("sent"))
-    v["feed_one"] = halves(line_one)
+    total_three, dqkv = tie((plane_sum_whole(v.pop("grads_three")[0], *v.pop("sides_three")), v.pop("dqkv")))
+    line_three = lax.psum_scatter(total_three, "hi", scatter_dimension=0, tiled=True)
+    v["line_two"] = line_two
+    v["kept"], v["sent"] = self_back(place, dqkv, v.pop("w_self"))
     v = tie(v)
 
     v["sides_four"] = grad_sides(v["grads_four"], v.pop("got_four"))
-    *input_pieces, norms_one = last_norm(
-        place, v.pop("rows_own"), v.pop("grad_own"), v.pop("kept"), v.pop("theirs"), v.pop("norms"), v.pop("text_part")
-    )
-    v["input_pieces"] = exchange(input_pieces)
-    total_three = plane_sum_whole(place, v.pop("grads_three")[0], *v.pop("sides_three"))
-    line_three = lax.psum_scatter(total_three, "hi", scatter_dimension=0, tiled=True)
-    sums = jnp.concatenate([norms_one[:2], 0.5 * v.pop("norms_two")[:2], 0.5 * v.pop("norms_three")[:2]], 0)
-    v["sums"] = sums + swap(sums)
-    v["feed_two"] = halves(line_two)
-    mine, sent = part_images(place, pieces)
-    (v["result"],) = land(place, mine, swap(sent), BF)
-    v = tie(v)
-
-    sums_four = plane_sum(v.pop("grads_four")[0], *v.pop("sides_four"))
-    v["line_four"] = [shift(piece, 3 - i) for i, piece in enumerate(sums_four[1:])]
-    v["feed_grads"] = spread_feed(place, *v.pop("feed_one"), *v.pop("feed_two"))
-    sums = v.pop("sums")
+    pieces = last_norm(
+        place, v.pop("rows_own"), v.pop("grad_own"), v.pop("kept"), swap(v.pop("sent")), v.pop("norms"),
+        v.pop("text_part"), v.pop("norms_two"), v.pop("norms_three"),
+    )
+    input_pieces = exchange(pieces)
+    v = tie(v)
+
+    v["kept"], *sums_four = plane_sum(place, v.pop("grads_four")[0], *v.pop("sides_four"))
+    v["line_four"] = [shift(piece, 3 - i) for i, piece in enumerate(sums_four)]
+    v["feed_grads"] = spread_feed(place, *v.pop("feed_one"), *halves(v.pop("line_two")))
+    later = tie((place, sums_four))[0]
+    mine, sent = part_images(later, input_pieces)
+    v["input_grad"], v["text_grad"], sums = land(place, mine, swap(sent), F32)
     sums = sums + across(sums, 1)
-    v["sums"] = sums + across(sums, 2)
-    mine, sent = part_images(place, v.pop("input_pieces"))
-    v["input_grad"], v["text_grad"] = land(place, mine, swap(sent), F32)
-    v["kept"] = sums_four[0]
+    sums = sums + across(sums, 2)
+    v["sums"] = lax.dynamic_slice_in_dim(sums, (chip * 2 + core) * 128, 128, 1)
+    v["cross_grads"] = spread(place, *halves(line_three))
     v = tie(v)
 
     kept, sent = line_sum(place, v.pop("kept"), v.pop("line_four"))
     own_grads = spread(place, kept, swap(sent))
-    cross_grads = spread(place, *halves(line_three))
-    sums = v.pop("sums")
-    for bit in (1, 2):
-        sums = sums + lax.ppermute(sums, "hi", [(i, i ^ bit) for i in range(4)])
-    sums = lax.dynamic_slice_in_dim(sums, (chip * 2 + core) * 128, 128, 1)
     return (
-        v["result"], v["input_grad"], v["text_grad"], *own_grads, *cross_grads, *v["feed_grads"],
-        *[sums[i] for i in range(6)],
+        v["result"], v["input_grad"], v["text_grad"], *own_grads, *v["cross_grads"], *v["feed_grads"],
+        *[v["sums"][i] for i in range(6)],
     )
 
 

time: 613 us -> 522 us (0.85)
  waiting for transfers between devices: 195 us -> 133 us
  Pallas kernels: 282 us -> 267 us
  local copies, waits for them, and re-layouts: 30.8 us -> 23.5 us
    ppermute x18 -> x21, waiting for transfers between devices: 114 us -> 60.3 us  [shift(): return lax.ppermute(value, 'hi', [((i + step) % 4, i) for i in range(4)])]
    all_gather x3, waiting for transfers between devices: 36.3 us -> 0.69 us  [gather_line(): return lax.all_gather(part, 'hi')]
    ppermute x41 -> x30, waiting for transfers between devices: 37.8 us -> 61.9 us  [across(): return lax.ppermute(value, 'chip', [(i, i ^ bit) for i in range(4)])]
    pallas_call x40 -> x36, Pallas kernels: 282 us -> 267 us  [call(): pl.pallas_call(body, in_specs=ins, out_specs=out_specs, out_shape=out_sha...]
    slice x10 -> x8, local copies, waits for them, and re-layouts: 10.9 us -> 2.84 us  [corners(): return [across(pair[0][:cut], 2), across(pair[1][cut:], 1)]]
    ppermute x41 -> x30, starting transfers between devices: 32.3 us -> 24.5 us  [across(): return lax.ppermute(value, 'chip', [(i, i ^ bit) for i in range(4)])]
    ppermute x18 -> x21, starting transfers between devices: 25.5 us -> 30.9 us  [shift(): return lax.ppermute(value, 'hi', [((i + step) % 4, i) for i in range(4)])]
  transfers between devices with their start and end apart: 85 -> 77, of which waited for: 26 -> 26; matrix products, arithmetic and copies ran while one was open for 4% -> 2% of each run, Pallas kernels for 44% -> 48%
where the time goes in v1:
time: 522 us; the launch traced here: 517 us
  Pallas kernels  267 us (51%)
  waiting for transfers between devices  133 us (25%)
  starting transfers between devices  74.3 us (14%)
  local copies, waits for them, and re-layouts  23.5 us (5%)
  between operations  15.3 us (3%)
    pallas_call x36, Pallas kernels, call(): pl.pallas_call(body, in_specs=ins, out_specs=out_specs, out_shape=out_sha...  267 us
    ppermute x30, waiting for transfers between devices, across(): return lax.ppermute(value, 'chip', [(i, i ^ bit) for i in range(4)])  61.9 us
    ppermute x21, waiting for transfers between devices, shift(): return lax.ppermute(value, 'hi', [((i + step) % 4, i) for i in range(4)])  60.3 us
    ppermute x21, starting transfers between devices, shift(): return lax.ppermute(value, 'hi', [((i + step) % 4, i) for i in range(4)])  30.9 us
    ppermute x30, starting transfers between devices, across(): return lax.ppermute(value, 'chip', [(i, i ^ bit) for i in range(4)])  24.5 us
    ppermute x18, starting transfers between devices, swap(): return lax.ppermute(value, 'core', [(0, 1), (1, 0)])  17.7 us
    unnamed x120, local copies, waits for them, and re-layouts  13.6 us
  transfers between devices with their start and end apart: 77, of which 26 were waited for; matrix products, arithmetic and copies ran while one was open for 2% of the time, Pallas kernels for 48%

profile of v1, /device:TPU:9, one launch (start us, length us, event | category | flops | bytes accessed | tf_op | source)
XLA Modules:
  0.0 517.2 jit_solution(15485365109280537883)
XLA Ops:
  39.6 7.3 %collective-permute-done.7.refs_1_ = bf16[256,512]{1,0:T(8,128)(2,1)S(1)} collective-permute-done((bf16[256,512]{1,0:T(8,128)(2,1)}, bf16[256,512]{1,0:T(8,128)(2,1)S(1)}, u32[]{:S(2)}, u32[]{:S(2)}) %collective-permute-start.7) | collective-permute-done | bytes 262176 | tf_op jit(solution)/shard_map/ppermute | solution.py:1646
  46.9 5.6 %collective-permute-done.8.refs_2_ = bf16[256,512]{1,0:T(8,128)(2,1)S(1)} collective-permute-done((bf16[256,512]{1,0:T(8,128)(2,1)}, bf16[256,512]{1,0:T(8,128)(2,1)S(1)}, u32[]{:S(2)}, u32[]{:S(2)}) %collective-permute-start.8) | collective-permute-done | bytes 262176 | tf_op jit(solution)/shard_map/ppermute | solution.py:1646
  55.8 17.5 %collective-permute-done.11.refs_6_ = bf16[768,512]{1,0:T(8,128)(2,1)S(1)} collective-permute-done((bf16[768,512]{1,0:T(8,128)(2,1)}, bf16[768,512]{1,0:T(8,128)(2,1)S(1)}, u32[]{:S(2)}, u32[]{:S(2)}) %collective-permute-start.11) | collective-permute-done | bytes 786464 | tf_op jit(solution)/shard_map/ppermute | solution.py:1643
  78.2 5.5 %collective-permute-done.15 = bf16[128,1024]{1,0:T(8,128)(2,1)S(1)} collective-permute-done((bf16[128,1024]{1,0:T(8,128)(2,1)}, bf16[128,1024]{1,0:T(8,128)(2,1)S(1)}, u32[]{:S(2)}, u32[]{:S(2)}) %collective-permute-start.15) | collective-permute-done | bytes 262176 | tf_op jit(solution)/shard_map/ppermute | solution.py:1646
  83.6 10.9 %collective-permute-done.16 = bf16[128,1024]{1,0:T(8,128)(2,1)S(1)} collective-permute-done((bf16[128,1024]{1,0:T(8,128)(2,1)}, bf16[128,1024]{1,0:T(8,128)(2,1)S(1)}, u32[]{:S(2)}, u32[]{:S(2)}) %collective-permute-start.16) | collective-permute-done | bytes 262176 | tf_op jit(solution)/shard_map/ppermute | solution.py:1646
  94.6 5.6 %collective-permute-done.17 = bf16[128,1024]{1,0:T(8,128)(2,1)S(1)} collective-permute-done((bf16[128,1024]{1,0:T(8,128)(2,1)}, bf16[128,1024]{1,0:T(8,128)(2,1)S(1)}, u32[]{:S(2)}, u32[]{:S(2)}) %collective-permute-start.17) | collective-permute-done | bytes 262176 | tf_op jit(solution)/shard_map/ppermute | solution.py:1646
  104.5 5.1 shard_map.345
  116.9 24.9 %shard_map.347 = (bf16[1024,1024]{1,0:T(8,128)(2,1)}, bf16[1024,1536]{1,0:T(8,128)(2,1)}, bf16[1024,512]{1,0:T(8,128)(2,1)}, f32[4,2,1024]{2,1,0:T(2,128)}, bf16[1024,1024]{1,0:T(8,128)(2,1)}) custom-call(s32[4]{0:T(128)} %pad_add_fusion.place, bf16[4,128,1024]{2,1,0:T(8,128)(2,1)} %shard_map.346.own.rows, bf16[4,128,1024]{2,1,0:T(8,128)(2,1)} %copy-done, ...), custom_call_target="tpu_custom_call" | custom-call | flops 1 | bytes 1 | tf_op jit(solution)/shard_map/pallas_call | solution.py:655
  149.3 8.3 %collective-permute-done.24.low = bf16[2,256,512]{2,1,0:T(8,128)(2,1)S(1)} collective-permute-done((bf16[2,256,512]{2,1,0:T(8,128)(2,1)}, bf16[2,256,512]{2,1,0:T(8,128)(2,1)S(1)}, u32[]{:S(2)}, u32[]{:S(2)}) %collective-permute-start.24) | collective-permute-done | bytes 524320 | tf_op jit(solution)/shard_map/ppermute | solution.py:1643
  169.7 15.8 %shard_map.350 = (f32[1024,1024]{1,0:T(8,128)}, bf16[1024,1024]{1,0:T(8,128)(2,1)}, bf16[1024,512]{1,0:T(8,128)(2,1)}, bf16[128,1024]{1,0:T(8,128)(2,1)}, bf16[1...) custom-call(s32[4]{0:T(128)} %pad_add_fusion.place, ...), custom_call_target="tpu_custom_call" | custom-call | flops 1 | bytes 1 | tf_op jit(solution)/shard_map/pallas_call | solution.py:655
  188.0 5.6 %collective-permute-done.29 = bf16[128,1024]{1,0:T(8,128)(2,1)} collective-permute-done((bf16[128,1024]{1,0:T(8,128)(2,1)}, bf16[128,1024]{1,0:T(8,128)(2,1)}, u32[]{:S(2)}, u32[]{:S(2)}) %collective-permute-start.29) | collective-permute-done | bytes 262176 | tf_op jit(solution)/shard_map/ppermute | solution.py:1646
  200.9 13.1 %collective-permute-done.33.low = bf16[2,256,512]{2,1,0:T(8,128)(2,1)S(1)} collective-permute-done((bf16[2,256,512]{2,1,0:T(8,128)(2,1)S(1)}, bf16[2,256,512]{2,1,0:T(8,128)(2,1)S(1)}, u32[]{:S(2)}, u32[]{:S(2)}) %collective-permute-start.33) | collective-permute-done | bytes 524320 | tf_op jit(solution)/shard_map/ppermute | solution.py:1643
  224.0 31.8 %shard_map.353 = (bf16[4,4,256,512]{3,2,1,0:T(8,128)(2,1)}, f32[1024,1024]{1,0:T(8,128)}, bf16[1024,1024]{1,0:T(8,128)(2,1)}, bf16[1024,1024]{1,0:T(8,128)(2,1)}...) custom-call(s32[4]{0:T(128)} %pad_add_fusion.place, f32[1024,1024]{1,0:T(8,128)} %get-tuple-element.941.after, ...), custom_call_target="tpu_custom_call" | custom-call | flops 1 | bytes 1 | tf_op jit(solution)/shard_map/pallas_call | solution.py:655
  256.4 27.7 %shard_map.354 = (bf16[256,2048]{1,0:T(8,128)(2,1)}, bf16[256,2048]{1,0:T(8,128)(2,1)}, bf16[256,2048]{1,0:T(8,128)(2,1)}, bf16[128,2048]{1,0:T(8,128)(2,1)}, bf...) custom-call(s32[4]{0:T(128)} %pad_add_fusion.place, ...), custom_call_target="tpu_custom_call" | custom-call | flops 1 | bytes 1 | tf_op jit(solution)/shard_map/pallas_call | solution.py:655
  284.1 4.8 collective-permute-start.37
  289.0 5.4 %collective-permute-done.36.theirs = bf16[4,128,1024]{2,1,0:T(8,128)(2,1)S(1)} collective-permute-done((bf16[4,128,1024]{2,1,0:T(8,128)(2,1)}, bf16[4,128,1024]{2,1,0:T(8,128)(2,1)S(1)}, u32[]{:S(2)}, u32[]{:S(2)}) %collective-permute-start.36) | collective-permute-done | bytes 1048608 | tf_op jit(solution)/shard_map/ppermute | solution.py:1640
  299.5 5.9 %collective-permute-start.40 = (bf16[128,1024]{1,0:T(8,128)(2,1)}, bf16[128,1024]{1,0:T(8,128)(2,1)S(1)}, u32[]{:S(2)}, u32[]{:S(2)}) collective-permute-start(bf16[128,1024]{1,0:T(8,128)(2,1)} %get-tuple-element.903), channel_id=1, source_target_pairs={{1,0},{2,1},{3,2},{0,3},{5,4},{6,5},{7,6},{4,7},{9,8},{10,9},{11,1... | collective-permute-start | bytes 786440 | tf_op jit(solution)/shard_map/ppermute | solution.py:1646
  307.5 25.2 %shard_map.355 = (f32[1024,1024]{1,0:T(8,128)}, bf16[1024,1024]{1,0:T(8,128)(2,1)}, f32[8,1024]{1,0:T(8,128)}, bf16[128,1024]{1,0:T(8,128)(2,1)}, bf16[256,2048]...) custom-call(s32[4]{0:T(128)} %pad_add_fusion.place, ...), custom_call_target="tpu_custom_call" | custom-call | flops 1 | bytes 1 | tf_op jit(solution)/shard_map/pallas_call | solution.py:655
  340.7 32.1 %shard_map.358 = (f32[4,128,1024]{2,1,0:T(8,128)}, bf16[1024,1024]{1,0:T(8,128)(2,1)}, f32[8,1024]{1,0:T(8,128)}, bf16[1024,1536]{1,0:T(8,128)(2,1)}) custom-call(s32[4]{0:T(128)} %pad_add_fusion.place, f32[1024,1024]{1,0:T(8,128)} %get-tuple-element.941.after, bf16[1024,1024]{1,0:T(8,128)(2,1)} %get-tuple-element.942.mine, bf16[1024,1024]{1,0:T(8,128)(2,1)} %copy-done.5, ...), custom_call_target="tpu_custom_call" | custom-call | flops 1 | bytes 1 | tf_op jit(solution)/shard_map/pallas_call | solution.py:655
  389.6 12.8 %shard_map.359 = (bf16[256,2048]{1,0:T(8,128)(2,1)}, bf16[256,2048]{1,0:T(8,128)(2,1)}, bf16[256,2048]{1,0:T(8,128)(2,1)}, bf16[128,2048]{1,0:T(8,128)(2,1)}, bf16[128,2048]{1,0:T(8,128)(2,1)}) custom-call(s32[4]{0:T(128)} %pad_add_fusion.place, bf16[1024,1024]{1,0:T(8,128)(2,1)} %get-tuple-element.974.normed, ...), custom_call_target="tpu_custom_call" | custom-call | flops 1 | bytes 1 | tf_op jit(solution)/shard_map/pallas_call | solution.py:655
  411.8 12.6 %shard_map.365 = (f32[4,128,1024]{2,1,0:T(8,128)}, bf16[4,128,1024]{2,1,0:T(8,128)(2,1)}) custom-call(s32[4]{0:T(128)} %pad_add_fusion.place, bf16[1024,1536]{1,0:T(8,128)(2,1)} %get-tuple-element.1018.dq.dk.dv.dqkv, bf16[1024,2048]{1,0:T(8,128)(2,1)} %get-tuple-element.1019.weights), custom_call_target="tpu_custom_call" | custom-call | flops 1 | bytes 1 | tf_op jit(solution)/shard_map/pallas_call | solution.py:655
  432.8 5.9 %shard_map.370 = (bf16[176,1024]{1,0:T(8,128)(2,1)}, bf16[176,1024]{1,0:T(8,128)(2,1)}, bf16[176,1024]{1,0:T(8,128)(2,1)}, bf16[176,1024]{1,0:T(8,128)(2,1)}) custom-call(s32[4]{0:T(128)} %pad_add_fusion.place, bf16[4,128,1024]{2,1,0:T(8,128)(2,1)} %shard_map.346.own.rows, f32[4,128,1024]{2,1,0:T(8,128)} %get-tuple-element.1055.grad_own, ...), custom_call_target="tpu_custom_call" | custom-call | flops 1 | bytes 1 | tf_op jit(solution)/shard_map/pallas_call | solution.py:655
  442.4 13.1 %collective-permute-done.55.over = bf16[256,2048]{1,0:T(8,128)(2,1)S(1)} collective-permute-done((bf16[256,2048]{1,0:T(8,128)(2,1)}, bf16[256,2048]{1,0:T(8,128)(2,1)S(1)}, u32[]{:S(2)}, u32[]{:S(2)}) %collective-permute-start.55) | collective-permute-done | bytes 1048608 | tf_op jit(solution)/shard_map/ppermute | solution.py:1643
  464.8 7.7 %collective-permute-done.61.refs_3_ = bf16[176,1024]{1,0:T(8,128)(2,1)S(1)} collective-permute-done((bf16[176,1024]{1,0:T(8,128)(2,1)}, bf16[176,1024]{1,0:T(8,128)(2,1)S(1)}, u32[]{:S(2)}, u32[]{:S(2)}) %collective-permute-start.61) | collective-permute-done | bytes 360480 | tf_op jit(solution)/shard_map/ppermute | solution.py:1646
  (322 shorter events, 191.6 us)
Async XLA Ops:
  7.2 93.7 %all-gather.9.cloned.1.call-start = ((), (), s32[]{:S(2)}) async-start(), calls=%async_computation.7 | async-start | bytes 1310720 | tf_op jit(solution)/shard_map/all_gather | solution.py:1655
  52.6 89.4 %all-gather.11.cloned.1.call-start = ((), (), s32[]{:S(2)}) async-start(), calls=%async_computation.8 | async-start | bytes 1310720 | tf_op jit(solution)/shard_map/all_gather | solution.py:1655
  104.5 81.7 %all-gather.13.cloned.1.call-start = ((), (), s32[]{:S(2)}) async-start(), calls=%async_computation.9 | async-start | bytes 1310720 | tf_op jit(solution)/shard_map/all_gather | solution.py:1655
  109.6 32.3 %collective-permute-start.19 = (bf16[4,256,512]{2,1,0:T(8,128)(2,1)}, bf16[4,256,512]{2,1,0:T(8,128)(2,1)S(1)}, u32[]{:S(2)}, u32[]{:S(2)}) collective-permute-start(bf16[4,256,512]{2,1,0:T(8,128)(2,1)} %bitcast.68), channel_id=1, source_target_pairs={{0,8},{8,0},{16,24},{24,16},{1,9},{9,1},{17,25},{25,17},{2,10},{10... | collective-permute-start | bytes 3145736 | tf_op jit(solution)/shard_map/ppermute | solution.py:1643
  111.1 30.9 %collective-permute-start.20 = (bf16[4,256,512]{2,1,0:T(8,128)(2,1)}, bf16[4,256,512]{2,1,0:T(8,128)(2,1)S(1)}, u32[]{:S(2)}, u32[]{:S(2)}) collective-permute-start(bf16[4,256,512]{2,1,0:T(8,128)(2,1)} %bitcast.69), channel_id=1, source_target_pairs={{0,16},{8,24},{16,0},{24,8},{1,17},{9,25},{17,1},{25,9},{2,18},{10... | collective-permute-start | bytes 3145736 | tf_op jit(solution)/shard_map/ppermute | solution.py:1643
  112.3 29.6 %collective-permute-start.21 = (bf16[48,1024]{1,0:T(8,128)(2,1)}, bf16[48,1024]{1,0:T(8,128)(2,1)S(1)}, u32[]{:S(2)}, u32[]{:S(2)}) collective-permute-start(bf16[48,1024]{1,0:T(8,128)(2,1)} %get-tuple-element.700), channel_id=1, source_target_pairs={{1,0},{2,1},{3,2},{0,3},{5,4},{6,5},{7,6},{4,7},{9,8},{10,9},{11,1... | collective-permute-start | bytes 294920 | tf_op jit(solution)/shard_map/ppermute | solution.py:1646
  145.4 110.4 %all-gather.15.cloned.1.call-start = ((), (), s32[]{:S(2)}) async-start(), calls=%async_computation.10 | async-start | bytes 5242880 | tf_op jit(solution)/shard_map/all_gather | solution.py:1745
  159.3 34.4 %collective-permute-start.30 = (bf16[4,256,512]{2,1,0:T(8,128)(2,1)}, bf16[4,256,512]{2,1,0:T(8,128)(2,1)S(1)}, u32[]{:S(2)}, u32[]{:S(2)}) collective-permute-start(bf16[4,256,512]{2,1,0:T(8,128)(2,1)} %bitcast.65), channel_id=1, source_target_pairs={{0,8},{8,0},{16,24},{24,16},{1,9},{9,1},{17,25},{25,17},{2,10},{10... | collective-permute-start | bytes 3145736 | tf_op jit(solution)/shard_map/ppermute | solution.py:1643
  159.5 34.2 %collective-permute-start.31 = (bf16[4,256,512]{2,1,0:T(8,128)(2,1)}, bf16[4,256,512]{2,1,0:T(8,128)(2,1)}, u32[]{:S(2)}, u32[]{:S(2)}) collective-permute-start(bf16[4,256,512]{2,1,0:T(8,128)(2,1)} %bitcast.66), channel_id=1, source_target_pairs={{0,16},{8,24},{16,0},{24,8},{1,17},{9,25},{17,1},{25,9},{2,18},{10... | collective-permute-start | bytes 3145736 | tf_op jit(solution)/shard_map/ppermute | solution.py:1643
  163.7 30.0 %collective-permute-start.29 = (bf16[128,1024]{1,0:T(8,128)(2,1)}, bf16[128,1024]{1,0:T(8,128)(2,1)}, u32[]{:S(2)}, u32[]{:S(2)}) collective-permute-start(bf16[128,1024]{1,0:T(8,128)(2,1)} %get-tuple-element.741), channel_id=1, source_target_pairs={{3,0},{0,1},{1,2},{2,3},{7,4},{4,5},{5,6},{6,7},{11,8},{8,9},{9,10... | collective-permute-start | bytes 786440 | tf_op jit(solution)/shard_map/ppermute | solution.py:1646
  193.7 143.9 %reduce-scatter.13.cloned.1.call-start = ((), (), s32[]{:S(2)}) async-start(), calls=%async_computation.11 | async-start | bytes 5242880
  255.8 119.4 %reduce-scatter.7.cloned.1.call-start = ((), (), s32[]{:S(2)}) async-start(), calls=%async_computation.4 | async-start | bytes 1310720 | tf_op jit(solution)/shard_map/reduce_scatter | solution.py:1781
  294.4 38.3 %collective-permute-start.38 = (bf16[128,2048]{1,0:T(8,128)(2,1)}, bf16[128,2048]{1,0:T(8,128)(2,1)}, u32[]{:S(2)}, u32[]{:S(2)}) collective-permute-start(bf16[128,2048]{1,0:T(8,128)(2,1)} %get-tuple-element.872), channel_id=1, source_target_pairs={{0,8},{8,0},{16,24},{24,16},{1,9},{9,1},{17,25},{25,17},{2,10},{10... | collective-permute-start | bytes 1572872 | tf_op jit(solution)/shard_map/ppermute | solution.py:1643
  296.5 36.2 %collective-permute-start.39 = (bf16[128,2048]{1,0:T(8,128)(2,1)}, bf16[128,2048]{1,0:T(8,128)(2,1)}, u32[]{:S(2)}, u32[]{:S(2)}) collective-permute-start(bf16[128,2048]{1,0:T(8,128)(2,1)} %get-tuple-element.873), channel_id=1, source_target_pairs={{0,16},{8,24},{16,0},{24,8},{1,17},{9,25},{17,1},{25,9},{2,18},{10... | collective-permute-start | bytes 1572872 | tf_op jit(solution)/shard_map/ppermute | solution.py:1643
  299.5 33.2 %collective-permute-start.40 = (bf16[128,1024]{1,0:T(8,128)(2,1)}, bf16[128,1024]{1,0:T(8,128)(2,1)S(1)}, u32[]{:S(2)}, u32[]{:S(2)}) collective-permute-start(bf16[128,1024]{1,0:T(8,128)(2,1)} %get-tuple-element.903), channel_id=1, source_target_pairs={{1,0},{2,1},{3,2},{0,3},{5,4},{6,5},{7,6},{4,7},{9,8},{10,9},{11,1... | collective-permute-start | bytes 786440 | tf_op jit(solution)/shard_map/ppermute | solution.py:1646
  305.4 27.3 %collective-permute-start.41 = (bf16[128,1024]{1,0:T(8,128)(2,1)}, bf16[128,1024]{1,0:T(8,128)(2,1)S(1)}, u32[]{:S(2)}, u32[]{:S(2)}) collective-permute-start(bf16[128,1024]{1,0:T(8,128)(2,1)} %get-tuple-element.904), channel_id=1, source_target_pairs={{2,0},{3,1},{0,2},{1,3},{6,4},{7,5},{4,6},{5,7},{10,8},{11,9},{8,1... | collective-permute-start | bytes 786440 | tf_op jit(solution)/shard_map/ppermute | solution.py:1646
  305.4 27.3 %collective-permute-start.42 = (bf16[128,1024]{1,0:T(8,128)(2,1)}, bf16[128,1024]{1,0:T(8,128)(2,1)S(1)}, u32[]{:S(2)}, u32[]{:S(2)}) collective-permute-start(bf16[128,1024]{1,0:T(8,128)(2,1)} %get-tuple-element.905), channel_id=1, source_target_pairs={{3,0},{0,1},{1,2},{2,3},{7,4},{4,5},{5,6},{6,7},{11,8},{8,9},{9,10... | collective-permute-start | bytes 786440 | tf_op jit(solution)/shard_map/ppermute | solution.py:1646
  337.7 86.8 %reduce-scatter.11.cloned.1.call-start = ((), (), s32[]{:S(2)}) async-start(), calls=%async_computation.6 | async-start | bytes 1310720 | tf_op jit(solution)/shard_map/reduce_scatter | solution.py:1790
  337.7 36.8 %collective-permute-start.46 = (bf16[256,2048]{1,0:T(8,128)(2,1)}, bf16[256,2048]{1,0:T(8,128)(2,1)S(1)}, u32[]{:S(2)}, u32[]{:S(2)}) collective-permute-start(bf16[256,2048]{1,0:T(8,128)(2,1)} %get-tuple-element.968), channel_id=1, source_target_pairs={{0,16},{8,24},{16,0},{24,8},{1,17},{9,25},{17,1},{25,9},{2,18},{10... | collective-permute-start | bytes 3145736 | tf_op jit(solution)/shard_map/ppermute | solution.py:1643
  338.5 36.7 %collective-permute-start.47 = (bf16[256,2048]{1,0:T(8,128)(2,1)}, bf16[256,2048]{1,0:T(8,128)(2,1)}, u32[]{:S(2)}, u32[]{:S(2)}) collective-permute-start(bf16[256,2048]{1,0:T(8,128)(2,1)} %get-tuple-element.969), channel_id=1, source_target_pairs={{0,8},{8,0},{16,24},{24,16},{1,9},{9,1},{17,25},{25,17},{2,10},{10... | collective-permute-start | bytes 3145736 | tf_op jit(solution)/shard_map/ppermute | solution.py:1643
  340.2 34.3 %collective-permute-start.44 = (bf16[128,2048]{1,0:T(8,128)(2,1)}, bf16[128,2048]{1,0:T(8,128)(2,1)S(1)}, u32[]{:S(2)}, u32[]{:S(2)}) collective-permute-start(bf16[128,2048]{1,0:T(8,128)(2,1)} %get-tuple-element.951), channel_id=1, source_target_pairs={{0,8},{8,0},{16,24},{24,16},{1,9},{9,1},{17,25},{25,17},{2,10},{10... | collective-permute-start | bytes 1572872 | tf_op jit(solution)/shard_map/ppermute | solution.py:1643
  340.2 34.3 %collective-permute-start.45 = (bf16[128,2048]{1,0:T(8,128)(2,1)}, bf16[128,2048]{1,0:T(8,128)(2,1)}, u32[]{:S(2)}, u32[]{:S(2)}) collective-permute-start(bf16[128,2048]{1,0:T(8,128)(2,1)} %get-tuple-element.952), channel_id=1, source_target_pairs={{0,16},{8,24},{16,0},{24,8},{1,17},{9,25},{17,1},{25,9},{2,18},{10... | collective-permute-start | bytes 1572872 | tf_op jit(solution)/shard_map/ppermute | solution.py:1643
  379.5 100.5 %reduce-scatter.9.cloned.1.call-start = ((), (), s32[]{:S(2)}) async-start(), calls=%async_computation.5 | async-start | bytes 1310720 | tf_op jit(solution)/shard_map/reduce_scatter | solution.py:1799
  441.6 30.9 %collective-permute-start.61 = (bf16[176,1024]{1,0:T(8,128)(2,1)}, bf16[176,1024]{1,0:T(8,128)(2,1)S(1)}, u32[]{:S(2)}, u32[]{:S(2)}) collective-permute-start(bf16[176,1024]{1,0:T(8,128)(2,1)} %get-tuple-element.1065), channel_id=1, source_target_pairs={{3,0},{0,1},{1,2},{2,3},{7,4},{4,5},{5,6},{6,7},{11,8},{8,9},{9,10... | collective-permute-start | bytes 1081352 | tf_op jit(solution)/shard_map/ppermute | solution.py:1646
  (113 other events, 1344.3 us)
Sparse Core Ops, SparseCore 0:
  52.7 27.4 all-gather.8
  104.6 35.4 all-gather.10
  145.5 40.5 all-gather.12
  193.8 61.4 all-gather.14
  258.1 65.1 reduce-scatter.12
  337.8 25.3 reduce-scatter.6
  379.6 25.5 reduce-scatter.10
  411.9 26.6 reduce-scatter.8

commit v2 on v1

--- a/solution.py
+++ b/solution.py
@@ -640,11 +640,72 @@
 ANY = pl.BlockSpec(memory_space=pltpu.HBM)
 SMEM = pl.BlockSpec(memory_space=pltpu.SMEM)
 VMEM = pl.BlockSpec(memory_space=pltpu.VMEM)
+LATE = object()
 MIB = 1024 * 1024
 
 
 def like(*shape, dtype=BF):
     return jax.ShapeDtypeStruct(shape, dtype)
+
+
+class Late:
+    def __init__(self, source, target, sem):
+        self.ref, self.copy = target, pltpu.make_async_copy(source, target, sem)
+        self.copy.start()
+
+    def ready(self):
+        if self.copy is not None:
+            self.copy.wait()
+            self.copy = None
+        return self.ref
+
+
+class Early:
+    def __init__(self, source, target, sem):
+        self.ref, self.copy, self.sent = source, pltpu.make_async_copy(source, target, sem), False
+
+    def send(self):
+        self.copy.start()
+        self.sent = True
+
+
+def call_overlapped(body, outs, ins, operands, scratch=(), limit=60):
+    late_ins = [i for i, spec in enumerate(ins) if spec is LATE]
+    late_outs = [i for i, (spec, _) in enumerate(outs) if spec is LATE]
+    buffers = [pltpu.VMEM(operands[i].shape, operands[i].dtype) for i in late_ins]
+    buffers += [pltpu.VMEM(outs[i][1].shape, outs[i][1].dtype) for i in late_outs]
+    count = len(buffers)
+
+    def wrapped(*refs):
+        refs = list(refs)
+        sems = refs.pop()
+        extra = refs[len(refs) - count :]
+        refs = refs[: len(refs) - count]
+        loads = [Late(refs[i], extra[n], sems.at[n]) for n, i in enumerate(late_ins)]
+        for load, i in zip(loads, late_ins):
+            refs[i] = load
+        stores = []
+        for n, i in enumerate(late_outs):
+            place = len(ins) + i
+            stores.append(Early(extra[len(late_ins) + n], refs[place], sems.at[len(late_ins) + n]))
+            refs[place] = stores[-1]
+        body(*refs)
+        for load in loads:
+            load.ready()
+        for store in stores:
+            if not store.sent:
+                store.send()
+        for store in stores:
+            store.copy.wait()
+
+    return call(
+        wrapped,
+        [(ANY if spec is LATE else spec, shape) for spec, shape in outs],
+        [ANY if spec is LATE else spec for spec in ins],
+        operands,
+        [*scratch, *buffers, pltpu.SemaphoreType.DMA((max(count, 1),))],
+        limit,
+    )
 
 
 def call(body, outs, ins, operands, scratch=(), limit=60, grid=None, flops=0, moved=0):
@@ -901,6 +962,13 @@
     return jnp.concatenate([weights[:, s * 512 + one * count : s * 512 + (one + 1) * count] for s in range(4)], 1)
 
 
+def project_into(target, rows, weights, dims=NN, step=512):
+    count = weights.shape[0] if dims == NT else weights.shape[1]
+    for low in range(0, count, step):
+        part = weights[low : low + step, :] if dims == NT else weights[:, low : low + step]
+        target[:, low : low + step] = dot(rows, part, dims).astype(target.dtype)
+
+
 def image_blocks(place, own, other):
     core, top = place[1], place[2]
     for number in range(4):
@@ -910,6 +978,25 @@
 
 def one_head(values, head):
     return jnp.where(lane_head((1, 2 * HD), 1, head), values, jnp.zeros_like(values))
+
+
+def both_heads(values):
+    return jnp.concatenate([one_head(values, 0), one_head(values, 1)], 0)
+
+
+def pick_heads(values):
+    count = values.shape[1] // 2
+    return jnp.where(lane_head((128, 1), 0, 0), values[:, :count], values[:, count:]).T
+
+
+def causal_pair(count):
+    rows = lax.broadcasted_iota(jnp.int32, (count, 2 * count), 0)
+    columns = lax.broadcasted_iota(jnp.int32, (count, 2 * count), 1)
+    return rows <= jnp.where(columns >= count, columns - count, columns)
+
+
+def twice(row):
+    return jnp.concatenate([row, row], 1)
 
 
 def softmax_mix(scores, values):
@@ -935,36 +1022,29 @@
     gain, bias = norm_row(norms, 0), norm_row(norms, 1)
     for row, half, number in image_blocks(place, own, other):
         normed[at(row, 128), :] = normalized(half[number].astype(F32), gain, bias)
-    w_in = jnp.concatenate([columns_of(weights, one) for one in range(3)], 1)
-    for low in range(0, 1024, BLOCK):
-        qkv[low : low + BLOCK, :] = dot(normed[low : low + BLOCK, :], w_in).astype(BF)
-    causal = causal_mask()
+    for one in range(3):
+        qkv[:, one * 512 : (one + 1) * 512] = dot(normed[...], columns_of(weights, one)).astype(BF)
+    causal = causal_pair(512)
 
     def pair_step(pair, carry):
         lanes = at(pair * 128, 128)
         k_lanes, v_lanes = at(512 + pair * 128, 128), at(1024 + pair * 128, 128)
-        for low in range(0, 1024, BLOCK):
-            high = low + BLOCK
-            query = qkv[low:high, lanes]
-            mixes = []
+        for low in range(0, 1024, 512):
+            high = low + 512
+            both = both_heads(qkv[low:high, lanes])
+            scores = [jnp.where(causal, dot(qkv[low:high, k_lanes], both, NT), NEG)]
+            values = [qkv[low:high, v_lanes]]
+            if low:
+                scores.append(dot(qkv[:low, k_lanes], both, NT))
+                values.append(qkv[:low, v_lanes])
+            mixed, logsum = softmax_mix(scores, values)
             for head in range(2):
-                one = one_head(query, head)
-                scores = [jnp.where(causal, dot(qkv[low:high, k_lanes], one, NT), NEG)]
-                values = [qkv[low:high, v_lanes]]
-                if low:
-                    scores.append(dot(qkv[:low, k_lanes], one, NT))
-                    values.append(qkv[:low, v_lanes])
-                mixed, logsum = softmax_mix(scores, values)
-                mixes.append(mixed)
-                lse[pair, head : head + 1, low:high] = logsum
-            both = jnp.where(lane_head((128, 1), 0, 0), mixes[0], mixes[1])
-            mix[low:high, lanes] = both.T.astype(BF)
+                lse[pair, head : head + 1, low:high] = logsum[:, head * 512 : (head + 1) * 512]
+            mix[low:high, lanes] = pick_heads(mixed).astype(BF)
         return carry
 
     lax.fori_loop(0, 4, pair_step, 0)
-    w_out = columns_of(weights, 3)
-    for low in range(0, 1024, BLOCK):
-        part[low : low + BLOCK, :] = dot(mix[low : low + BLOCK, :], w_out, NT).astype(BF)
+    project_into(part, mix[...], columns_of(weights, 3), NT)
 
 
 def fused_self_forward(place, own, other, norms, weights):
@@ -977,11 +1057,8 @@
             (VMEM, like(4, 2, 1024, dtype=F32)),
             (VMEM, like(1024, 1024)),
         ],
-        [SMEM] + [VMEM] * 4,
+        [SMEM, VMEM, VMEM, VMEM, VMEM],
         (place, own, other, norms, weights),
-        limit=60,
-        flops=10 * 2**30,
-        moved=14 * MIB,
     )
 
 
@@ -994,32 +1071,22 @@
         values = half[number].astype(F32) + (mine[rows, :].astype(F32) + theirs[rows, :].astype(F32))
         after[rows, :] = values
         normed[rows, :] = normalized(values, gain, bias)
-    w_query = columns_of(weights, 0)
-    for low in range(0, 1024, BLOCK):
-        queries[low : low + BLOCK, :] = dot(normed[low : low + BLOCK, :], w_query).astype(BF)
+    project_into(queries, normed[...], columns_of(weights, 0))
     w_text = jnp.concatenate([columns_of(weights, 1), columns_of(weights, 2)], 1)
     keys[...] = dot(text[...], w_text).astype(BF)
 
     def pair_step(pair, carry):
         lanes, v_lanes = at(pair * 128, 128), at(512 + pair * 128, 128)
-        for low in range(0, 1024, 512):
-            high = low + 512
-            query = queries[low:high, lanes]
-            seen = ids[...] == caption[:, low:high]
-            mixes = []
-            for head in range(2):
-                scores = jnp.where(seen, dot(keys[:, lanes], one_head(query, head), NT), NEG)
-                mixed, logsum = softmax_mix([scores], [keys[:, v_lanes]])
-                mixes.append(mixed)
-                lse[pair, head : head + 1, low:high] = logsum
-            both = jnp.where(lane_head((128, 1), 0, 0), mixes[0], mixes[1])
-            mix[low:high, lanes] = both.T.astype(BF)
+        seen = twice(ids[...] == caption[...])
+        scores = jnp.where(seen, dot(keys[:, lanes], both_heads(queries[:, lanes]), NT), NEG)
+        mixed, logsum = softmax_mix([scores], [keys[:, v_lanes]])
+        for head in range(2):
+            lse[pair, head : head + 1, :] = logsum[:, head * 1024 : (head + 1) * 1024]
+        mix[:, lanes] = pick_heads(mixed).astype(BF)
         return carry
 
     lax.fori_loop(0, 4, pair_step, 0)
-    w_out = columns_of(weights, 3)
-    for low in range(0, 1024, BLOCK):
-        part[low : low + BLOCK, :] = dot(mix[low : low + BLOCK, :], w_out, NT).astype(BF)
+    project_into(part, mix[...], columns_of(weights, 3), NT)
 
 
 def fused_cross_forward(place, own, other, mine, theirs, norms, text, ids, caption, weights):
@@ -1034,11 +1101,8 @@
             (VMEM, like(4, 2, 1024, dtype=F32)),
             (VMEM, like(1024, 1024)),
         ],
-        [SMEM] + [VMEM] * 9,
+        [SMEM] + [VMEM] * 8 + [VMEM],
         (place, own, other, mine, theirs, norms, text, ids, caption, weights),
-        limit=60,
-        flops=5 * 2**30,
-        moved=20 * MIB,
     )
 
 
@@ -1055,31 +1119,35 @@
 
 
 def feed_step(rows, cot, rows_t, cot_t, weights, out_sum, back_sum, grads):
-    w_in, w_out = weights[:, :256], weights[:, 256:]
+    w_in = jnp.concatenate([weights[0][:, :256], weights[1][:, :256]], 1)
+    w_out = jnp.concatenate([weights[0][:, 256:], weights[1][:, 256:]], 1)
     slope = math.sqrt(2.0 / math.pi)
-    acts, pre_grads = [], []
-    for low in range(0, 1024, BLOCK):
-        part = slice(low, low + BLOCK)
-        pre = dot(rows[part, :], w_in)
-        square = pre * pre
-        bent = jnp.tanh(pre * (slope + slope * 0.044715 * square))
-        half = 0.5 * (1.0 + bent)
-        act = (pre * half).astype(BF)
-        bend = half + pre * (0.5 * (1.0 - bent * bent)) * (slope + 3.0 * slope * 0.044715 * square)
-        pre_grad = (dot(cot[part, :], w_out) * bend).astype(BF)
-        out_sum[part, :] += dot(act, w_out, NT)
-        back_sum[part, :] += dot(pre_grad, w_in, NT)
-        acts.append(act)
-        pre_grads.append(pre_grad)
-    grads[:, :256] = dot(rows_t[...], jnp.concatenate(pre_grads, 0))
-    grads[:, 256:] = dot(cot_t[...], jnp.concatenate(acts, 0))
+    pre = dot(rows[...], w_in)
+    square = pre * pre
+    bent = jnp.tanh(pre * (slope + slope * 0.044715 * square))
+    half = 0.5 * (1.0 + bent)
+    act = (pre * half).astype(BF)
+    bend = half + pre * (0.5 * (1.0 - bent * bent)) * (slope + 3.0 * slope * 0.044715 * square)
+    pre_grad = (dot(cot[...], w_out) * bend).astype(BF)
+    for low in range(0, 1024, 512):
+        part = slice(low, low + 512)
+        out_sum[:, part] += dot(act, w_out[part, :], NT)
+        back_sum[:, part] += dot(pre_grad, w_in[part, :], NT)
+    for block in range(2):
+        part = slice(block * 256, (block + 1) * 256)
+        grads[:, block * 512 : block * 512 + 256] = dot(rows_t[...], pre_grad[:, part])
+        grads[:, block * 512 + 256 : (block + 1) * 512] = dot(cot_t[...], act[:, part])
 
 
 def feed_first_kernel(
     place, after, mine, theirs, norms, cot_own, cot_other, weights,
-    g_whole, after_cross, normed, cot, out_sum, back_sum, rows_t, cot_t, grads,
+    g_whole, after_out, normed_out, cot_out, out_sum, back, after_cross, normed, cot, back_sum, rows_t, cot_t, grads, sems,
 ):
-    @pl.when(pl.program_id(0) == 0)
+    step = pl.program_id(0)
+    pairs = ((after_cross, after_out), (normed, normed_out), (cot, cot_out))
+    stores = [pltpu.make_async_copy(a, b, sems.at[i]) for i, (a, b) in enumerate(pairs)]
+
+    @pl.when(step == 0)
     def _():
         gain, bias = norm_row(norms, 4), norm_row(norms, 5)
         for low in range(0, 1024, 128):
@@ -1089,6 +1157,8 @@
             normed[rows, :] = normalized(values, gain, bias)
         for row, half, number in image_blocks(place, cot_own, cot_other):
             cot[at(row, 128), :] = half[number]
+        for store in stores:
+            store.start()
         rows_t[...] = normed[...].T
         cot_t[...] = cot[...].T
         out_sum[...] = jnp.zeros_like(out_sum)
@@ -1097,9 +1167,19 @@
             out_sum[rows, :] = after_cross[rows, :]
         back_sum[...] = jnp.zeros_like(back_sum)
 
-    feed_step(normed, cot, rows_t, cot_t, weights, out_sum, back_sum, grads)
+    feed_step(
+        normed, cot, rows_t, cot_t, (weights[:, :512], weights[:, 512:]), out_sum, back_sum, grads
+    )
     for chip in range(4):
-        g_whole[chip, 0] = grads[chip * 256 : (chip + 1) * 256, :].astype(BF)
+        for block in range(2):
+            part = grads[chip * 256 : (chip + 1) * 256, block * 512 : (block + 1) * 512]
+            g_whole[chip, block] = part.astype(BF)
+
+    @pl.when(step == 1)
+    def _():
+        back[...] = back_sum[...].astype(BF)
+        for store in stores:
+            store.wait()
 
 
 def feed_second_kernel(
@@ -1113,12 +1193,13 @@
         rows_t[...] = normed[...].T
         cot_t[...] = cot[...].T
         out_sum[...] = out_in[...]
-        back_sum[...] = back_in[...]
-
-    feed_step(normed, cot, rows_t, cot_t, weights[:, 0].reshape(1024, 512), out_sum, back_sum, grads)
+        back_sum[...] = back_in[...].astype(F32)
+
+    blocks = [weights[:, block].reshape(1024, 512) for block in range(2)]
+    feed_step(normed, cot, rows_t, cot_t, blocks, out_sum, back_sum, grads)
     cut_grads(place, grads, slice(None), g_own, g_side, g_over, g_low, g_high)
 
-    @pl.when(step == 3)
+    @pl.when(step == 1)
     def _():
         back[...] = back_sum[...].astype(BF)
         for block in range(4):
@@ -1131,8 +1212,8 @@
     return pl.BlockSpec(shape, lambda i: zeros, pipeline_mode=pl.Buffered(1))
 
 
-def grad_outs():
-    return [(pl.BlockSpec((rows, 512), lambda i: (0, i)), like(rows, n)) for rows, n in GRAD_SHAPES]
+def grad_outs(width=512):
+    return [(pl.BlockSpec((rows, width), lambda i: (0, i)), like(rows, n)) for rows, n in GRAD_SHAPES]
 
 
 FEED_FLOPS = 13 * 2**30
@@ -1142,20 +1223,24 @@
     square = once(1024, 1024)
     return call(
         feed_first_kernel,
-        [(pl.BlockSpec((4, 1, 256, 512), lambda i: (0, i, 0, 0)), like(4, 4, 256, 512))]
+        [(pl.BlockSpec((4, 2, 256, 512), lambda i: (0, i, 0, 0)), like(4, 4, 256, 512))]
         + [
+            (ANY, like(1024, 1024, dtype=F32)),
+            (ANY, like(1024, 1024)),
+            (ANY, like(1024, 1024)),
             (square, like(1024, 1024, dtype=F32)),
             (square, like(1024, 1024)),
-            (square, like(1024, 1024)),
-            (square, like(1024, 1024, dtype=F32)),
-            (square, like(1024, 1024, dtype=F32)),
         ],
         [SMEM, square, square, square, once(16, 1024), once(4, 128, 1024), once(4, 128, 1024)]
-        + [pl.BlockSpec((1024, 512), lambda i: (0, i))],
+        + [pl.BlockSpec((1024, 1024), lambda i: (0, i))],
         (place, after, mine, theirs, norms, cot_own, cot_other, weights),
-        [pltpu.VMEM((1024, 1024), BF)] * 2 + [pltpu.VMEM((1024, 512), F32)],
+        [pltpu.VMEM((1024, 1024), F32)]
+        + [pltpu.VMEM((1024, 1024), BF)] * 2
+        + [pltpu.VMEM((1024, 1024), F32)]
+        + [pltpu.VMEM((1024, 1024), BF)] * 2
+        + [pltpu.VMEM((1024, 1024), F32), pltpu.SemaphoreType.DMA((3,))],
         limit=60,
-        grid=(4,),
+        grid=(2,),
         flops=FEED_FLOPS,
         moved=30 * MIB,
     )
@@ -1165,19 +1250,19 @@
     square = once(1024, 1024)
     return call(
         feed_second_kernel,
-        grad_outs()
+        grad_outs(1024)
         + [
             (once(4, 128, 1024), like(4, 128, 1024, dtype=F32)),
             (once(4, 128, 1024), like(4, 128, 1024)),
             (square, like(1024, 1024)),
         ],
-        [SMEM, square, square, square, square, pl.BlockSpec((4, 1, 256, 512), lambda i: (0, i, 0, 0))],
+        [SMEM, square, square, square, square, pl.BlockSpec((4, 2, 256, 512), lambda i: (0, i, 0, 0))],
         (place, normed, cot, out_in, back_in, weights),
         [pltpu.VMEM((1024, 1024), F32)] * 2
         + [pltpu.VMEM((1024, 1024), BF)] * 2
-        + [pltpu.VMEM((1024, 512), F32)],
+        + [pltpu.VMEM((1024, 1024), F32)],
         limit=60,
-        grid=(4,),
+        grid=(2,),
         flops=FEED_FLOPS,
         moved=26 * MIB,
     )
@@ -1208,6 +1293,15 @@
     norms[1:2, :] = jnp.sum(bias_sum, 0, keepdims=True)
 
 
+def pair_row(lse, pair, low, high):
+    return jnp.concatenate([lse[pair, 0:1, low:high], lse[pair, 1:2, low:high]], 1)
+
+
+def pair_delta(grad, mix):
+    product = (grad.astype(F32) * mix.astype(F32)).T
+    return jnp.concatenate([jnp.sum(product[:HD], 0, keepdims=True), jnp.sum(product[HD:], 0, keepdims=True)], 1)
+
+
 def head_grads(keys, values, one, one_grad, lse, delta, mask):
     weights = jnp.exp2(dot(keys, one, NT) * (LOG2E * HD**-0.5) - lse)
     if mask is not None:
@@ -1218,45 +1312,41 @@
 
 def cross_bwd_kernel(
     place, after, mine, theirs, cot, gain, weights, normed, text, queries, keys, mix, lse, ids, caption,
-    grad_cross, part, norms, text_part, g_own, g_side, g_over, g_low, g_high, low_grad, mix_grad, dq, dkv, grads,
+    grad_out, part_out, norms, text_part, g_own, g_side, g_over, g_low, g_high, low_grad, mix_grad, dq, dkv, grads,
 ):
+    grad_cross, part = grad_out.ref, part_out.ref
+
     def keep(rows, value):
         grad_cross[rows, :] = value
         low_grad[rows, :] = value.astype(BF)
 
     norm_block(lambda rows: after[rows, :], mine, theirs, lambda rows: cot[rows, :].astype(F32), (gain, 4), norms, keep)
-    w_out = columns_of(weights, 3)
-    for low in range(0, 1024, BLOCK):
-        mix_grad[low : low + BLOCK, :] = dot(low_grad[low : low + BLOCK, :], w_out).astype(BF)
+    grad_out.send()
+    weights, queries, keys, mix = weights.ready(), queries.ready(), keys.ready(), mix.ready()
+    project_into(mix_grad, low_grad[...], columns_of(weights, 3))
 
     def pair_step(pair, carry):
         lanes, v_lanes = at(pair * 128, 128), at(512 + pair * 128, 128)
-        dk_sum, dv_sum = jnp.zeros((128, 128), F32), jnp.zeros((128, 128), F32)
-        for low in range(0, 1024, 512):
-            high = low + 512
-            query, grad = queries[low:high, lanes], mix_grad[low:high, lanes]
-            product = (grad.astype(F32) * mix[low:high, lanes].astype(F32)).T
-            seen = ids[...] == caption[:, low:high]
-            back = []
-            for head in range(2):
-                one, one_grad = one_head(query, head), one_head(grad, head)
-                delta = jnp.sum(product[head * HD : (head + 1) * HD], 0, keepdims=True)
-                prob, score_grad = head_grads(
-                    keys[:, lanes], keys[:, v_lanes], one, one_grad, lse[pair, head : head + 1, low:high], delta, seen
-                )
-                dv_sum = dv_sum + dot(prob, one_grad)
-                dk_sum = dk_sum + dot(score_grad, one)
-                back.append(dot(keys[:, lanes], score_grad, TN))
-            both = jnp.where(lane_head((128, 1), 0, 0), back[0], back[1])
-            dq[low:high, lanes] = (both.T * HD**-0.5).astype(BF)
+        query, grad = both_heads(queries[:, lanes]), both_heads(mix_grad[:, lanes])
+        prob, score_grad = head_grads(
+            keys[:, lanes],
+            keys[:, v_lanes],
+            query,
+            grad,
+            pair_row(lse, pair, 0, 1024),
+            pair_delta(mix_grad[:, lanes], mix[:, lanes]),
+            twice(ids[...] == caption[...]),
+        )
+        dv_sum, dk_sum = dot(prob, grad), dot(score_grad, query)
+        dq[:, lanes] = (pick_heads(dot(keys[:, lanes], score_grad, TN)) * HD**-0.5).astype(BF)
         dkv[:, lanes] = (dk_sum * HD**-0.5).astype(BF)
         dkv[:, v_lanes] = dv_sum.astype(BF)
         return carry
 
     lax.fori_loop(0, 4, pair_step, 0)
-    w_query = columns_of(weights, 0)
-    for low in range(0, 1024, BLOCK):
-        part[low : low + BLOCK, :] = dot(dq[low : low + BLOCK, :], w_query, NT).astype(BF)
+    project_into(part, dq[...], columns_of(weights, 0), NT)
+    part_out.send()
+    normed = normed.ready()
     w_text = jnp.concatenate([columns_of(weights, 1), columns_of(weights, 2)], 1)
     text_part[...] = dot(dkv[...], w_text, NT).astype(BF)
     for one, (left, right) in enumerate(
@@ -1271,16 +1361,16 @@
 
 
 def fused_cross_backward(place, after, mine, theirs, cot, gain, weights, normed, text, queries, keys, mix, lse, ids, caption):
-    return call(
+    return call_overlapped(
         cross_bwd_kernel,
         [
-            (VMEM, like(1024, 1024, dtype=F32)),
-            (VMEM, like(1024, 1024)),
+            (LATE, like(1024, 1024, dtype=F32)),
+            (LATE, like(1024, 1024)),
             (VMEM, like(8, 1024, dtype=F32)),
             (VMEM, like(128, 1024)),
         ]
         + [(VMEM, like(*shape)) for shape in GRAD_SHAPES],
-        [SMEM] + [VMEM] * 14,
+        [SMEM] + [VMEM] * 5 + [LATE, LATE, VMEM, LATE, LATE, LATE, VMEM, VMEM, VMEM],
         (place, after, mine, theirs, cot, gain, weights, normed, text, queries, keys, mix, lse, ids, caption),
         [
             pltpu.VMEM((1024, 1024), BF),
@@ -1289,17 +1379,15 @@
             pltpu.VMEM((128, 1024), BF),
             pltpu.VMEM((1024, 512), F32),
         ],
-        limit=60,
-        flops=9 * 2**30,
-        moved=32 * MIB,
     )
 
 
 def self_bwd_kernel(
     place, after, mine, theirs, base, gain, weights, qkv, mix, lse,
-    grad_own, low_grad, norms, dqkv, mix_grad, dk_sum, dv_sum,
+    grad_out, low_out, norms, dqkv, mix_grad, dk_sum, dv_sum,
 ):
     core = place[1]
+    grad_own, low_grad = grad_out.ref, low_out.ref
 
     def keep(rows, value):
         low_grad[rows, :] = value.astype(BF)
@@ -1309,43 +1397,35 @@
             grad_own[rows.start // 256] = value
 
     norm_block(lambda rows: after[rows, :], mine, theirs, lambda rows: base[rows, :], (gain, 2), norms, keep)
-    w_out = columns_of(weights, 3)
-    for low in range(0, 1024, BLOCK):
-        mix_grad[low : low + BLOCK, :] = dot(low_grad[low : low + BLOCK, :], w_out).astype(BF)
-    causal = causal_mask()
+    grad_out.send()
+    low_out.send()
+    weights, qkv, mix = weights.ready(), qkv.ready(), mix.ready()
+    project_into(mix_grad, low_grad[...], columns_of(weights, 3))
+    causal = causal_pair(512)
 
     def pair_step(pair, carry):
         lanes = at(pair * 128, 128)
         k_lanes, v_lanes = at(512 + pair * 128, 128), at(1024 + pair * 128, 128)
-        dk_sum[...] = jnp.zeros_like(dk_sum)
-        dv_sum[...] = jnp.zeros_like(dv_sum)
-        for low in range(0, 1024, BLOCK):
-            high = low + BLOCK
-            query, grad = qkv[low:high, lanes], mix_grad[low:high, lanes]
-            product = (grad.astype(F32) * mix[low:high, lanes].astype(F32)).T
-            back = []
-            for head in range(2):
-                one, one_grad = one_head(query, head), one_head(grad, head)
-                delta = jnp.sum(product[head * HD : (head + 1) * HD], 0, keepdims=True)
-                total = jnp.zeros((128, BLOCK), F32)
-                for start, stop in ((0, low), (low, high)):
-                    if start == stop:
-                        continue
-                    prob, score_grad = head_grads(
-                        qkv[start:stop, k_lanes],
-                        qkv[start:stop, v_lanes],
-                        one,
-                        one_grad,
-                        lse[pair, head : head + 1, low:high],
-                        delta,
-                        causal if start == low else None,
-                    )
-                    dv_sum[start:stop, :] += dot(prob, one_grad)
-                    dk_sum[start:stop, :] += dot(score_grad, one)
-                    total = total + dot(qkv[start:stop, k_lanes], score_grad, TN)
-                back.append(total)
-            both = jnp.where(lane_head((128, 1), 0, 0), back[0], back[1])
-            dqkv[low:high, lanes] = (both.T * HD**-0.5).astype(BF)
+        for low in range(0, 1024, 512):
+            high = low + 512
+            query, grad = both_heads(qkv[low:high, lanes]), both_heads(mix_grad[low:high, lanes])
+            delta = pair_delta(mix_grad[low:high, lanes], mix[low:high, lanes])
+            logsum = pair_row(lse, pair, low, high)
+            total = 0.0
+            for start in range(0, high, 512):
+                rows = slice(start, start + 512)
+                keys = qkv[rows, k_lanes]
+                prob, score_grad = head_grads(
+                    keys, qkv[rows, v_lanes], query, grad, logsum, delta, causal if start == low else None
+                )
+                dv, dk = dot(prob, grad), dot(score_grad, query)
+                if start == low:
+                    dv_sum[rows, :], dk_sum[rows, :] = dv, dk
+                else:
+                    dv_sum[rows, :] += dv
+                    dk_sum[rows, :] += dk
+                total = total + dot(keys, score_grad, TN)
+            dqkv[low:high, lanes] = (pick_heads(total) * HD**-0.5).astype(BF)
         dqkv[:, k_lanes] = (dk_sum[...] * HD**-0.5).astype(BF)
         dqkv[:, v_lanes] = dv_sum[...].astype(BF)
         return carry
@@ -1354,20 +1434,17 @@
 
 
 def fused_self_backward(place, after, mine, theirs, base, gain, weights, qkv, mix, lse):
-    return call(
+    return call_overlapped(
         self_bwd_kernel,
         [
-            (VMEM, like(4, 128, 1024, dtype=F32)),
-            (VMEM, like(1024, 1024)),
+            (LATE, like(4, 128, 1024, dtype=F32)),
+            (LATE, like(1024, 1024)),
             (VMEM, like(8, 1024, dtype=F32)),
             (VMEM, like(1024, 1536)),
         ],
-        [SMEM] + [VMEM] * 9,
+        [SMEM] + [VMEM] * 5 + [LATE] * 3 + [VMEM],
         (place, after, mine, theirs, base, gain, weights, qkv, mix, lse),
         [pltpu.VMEM((1024, 512), BF), pltpu.VMEM((1024, 128), F32), pltpu.VMEM((1024, 128), F32)],
-        limit=60,
-        flops=9 * 2**30,
-        moved=32 * MIB,
     )
 
 
@@ -1404,10 +1481,11 @@
 def self_back_kernel(place, dqkv, weights, kept, sent):
     core = place[1]
     w_in = jnp.concatenate([columns_of(weights, one) for one in range(3)], 1)
-    for block in range(4):
-        for target, half in ((sent, 1 - core), (kept, core)):
-            value = dot(dqkv[at(block * 256 + half * 128, 128), :], w_in, NT)
-            target[block] = value.astype(target.dtype)
+    for target, half in ((sent, 1 - core), (kept, core)):
+        rows = jnp.concatenate([dqkv[at(block * 256 + half * 128, 128), :] for block in range(4)], 0)
+        for low in range(0, 1024, 512):
+            value = dot(rows, w_in[low : low + 512, :], NT).astype(target.dtype)
+            target[:, :, low : low + 512] = value.reshape(4, 128, 512)
 
 
 def self_back(place, dqkv, weights):

time: 522 us -> 508 us (0.973)
  Pallas kernels: 267 us -> 239 us
  waiting for transfers between devices: 133 us -> 146 us
    pallas_call x36, Pallas kernels: 267 us -> 239 us  [call(): pl.pallas_call(body, in_specs=ins, out_specs=out_specs, out_shape=out_sha...]
  transfers between devices with their start and end apart: 77 -> 77, of which waited for: 26 -> 28; matrix products, arithmetic and copies ran while one was open for 2% -> 2% of each run, Pallas kernels for 48% -> 44%
where the time goes in v2:
time: 508 us; the launch traced here: 499 us
  Pallas kernels  239 us (47%)
  waiting for transfers between devices  146 us (29%)
  starting transfers between devices  71.1 us (14%)
  local copies, waits for them, and re-layouts  23.4 us (5%)
  between operations  15.3 us (3%)
    pallas_call x36, Pallas kernels, call(): pl.pallas_call(body, in_specs=ins, out_specs=out_specs, out_shape=out_sha...  239 us
    ppermute x30, waiting for transfers between devices, across(): return lax.ppermute(value, 'chip', [(i, i ^ bit) for i in range(4)])  66.1 us
    ppermute x21, waiting for transfers between devices, shift(): return lax.ppermute(value, 'hi', [((i + step) % 4, i) for i in range(4)])  60.8 us
    ppermute x21, starting transfers between devices, shift(): return lax.ppermute(value, 'hi', [((i + step) % 4, i) for i in range(4)])  31.2 us
    ppermute x30, starting transfers between devices, across(): return lax.ppermute(value, 'chip', [(i, i ^ bit) for i in range(4)])  25.4 us
    ppermute x18, starting transfers between devices, swap(): return lax.ppermute(value, 'core', [(0, 1), (1, 0)])  13.8 us
    unnamed x120, local copies, waits for them, and re-layouts  13.5 us
  transfers between devices with their start and end apart: 77, of which 28 were waited for; matrix products, arithmetic and copies ran while one was open for 2% of the time, Pallas kernels for 44%

profile of v2, /device:TPU:9, one launch (start us, length us, event | category | flops | bytes accessed | tf_op | source)
XLA Modules:
  0.0 499.2 jit_solution(10697478448727841542)
XLA Ops:
  39.4 7.4 %collective-permute-done.7.refs_1_ = bf16[256,512]{1,0:T(8,128)(2,1)S(1)} collective-permute-done((bf16[256,512]{1,0:T(8,128)(2,1)}, bf16[256,512]{1,0:T(8,128)(2,1)S(1)}, u32[]{:S(2)}, u32[]{:S(2)}) %collective-permute-start.7) | collective-permute-done | bytes 262176 | tf_op jit(solution)/shard_map/ppermute | solution.py:1724
  46.8 5.6 %collective-permute-done.8.refs_2_ = bf16[256,512]{1,0:T(8,128)(2,1)S(1)} collective-permute-done((bf16[256,512]{1,0:T(8,128)(2,1)}, bf16[256,512]{1,0:T(8,128)(2,1)S(1)}, u32[]{:S(2)}, u32[]{:S(2)}) %collective-permute-start.8) | collective-permute-done | bytes 262176 | tf_op jit(solution)/shard_map/ppermute | solution.py:1724
  55.7 17.5 %collective-permute-done.11.refs_6_ = bf16[768,512]{1,0:T(8,128)(2,1)S(1)} collective-permute-done((bf16[768,512]{1,0:T(8,128)(2,1)}, bf16[768,512]{1,0:T(8,128)(2,1)S(1)}, u32[]{:S(2)}, u32[]{:S(2)}) %collective-permute-start.11) | collective-permute-done | bytes 786464 | tf_op jit(solution)/shard_map/ppermute | solution.py:1721
  78.1 5.5 %collective-permute-done.15 = bf16[128,1024]{1,0:T(8,128)(2,1)S(1)} collective-permute-done((bf16[128,1024]{1,0:T(8,128)(2,1)}, bf16[128,1024]{1,0:T(8,128)(2,1)S(1)}, u32[]{:S(2)}, u32[]{:S(2)}) %collective-permute-start.15) | collective-permute-done | bytes 262176 | tf_op jit(solution)/shard_map/ppermute | solution.py:1724
  83.6 10.9 %collective-permute-done.16 = bf16[128,1024]{1,0:T(8,128)(2,1)S(1)} collective-permute-done((bf16[128,1024]{1,0:T(8,128)(2,1)}, bf16[128,1024]{1,0:T(8,128)(2,1)S(1)}, u32[]{:S(2)}, u32[]{:S(2)}) %collective-permute-start.16) | collective-permute-done | bytes 262176 | tf_op jit(solution)/shard_map/ppermute | solution.py:1724
  94.5 5.6 %collective-permute-done.17 = bf16[128,1024]{1,0:T(8,128)(2,1)S(1)} collective-permute-done((bf16[128,1024]{1,0:T(8,128)(2,1)}, bf16[128,1024]{1,0:T(8,128)(2,1)S(1)}, u32[]{:S(2)}, u32[]{:S(2)}) %collective-permute-start.17) | collective-permute-done | bytes 262176 | tf_op jit(solution)/shard_map/ppermute | solution.py:1724
  104.4 5.1 %shard_map.345 = (bf16[1024,2048]{1,0:T(8,128)(2,1)}, bf16[16,1024]{1,0:T(8,128)(2,1)}) custom-call(s32[4]{0:T(128)} %pad_add_fusion.place.refs_0_, bf16[288,512]{1,0:T(8,128)(2,1)} %get-tuple-element.662.refs_0_, bf16[288,512]{1,0:T(8,128)(2,1)} %copy-done.18, bf16[288,512]{1,0:T(8,128)(2,1)} %copy-done.17, bf16[128,512]{1,0:T(8,128)(2,1)} %copy-done.52, ...), custom_call_target="tpu_custom_call" | custom-call | flops 1 | bytes 1 | tf_op jit(solution)/shard_map/pallas_call | solution.py:716
  116.7 19.6 %shard_map.347 = (bf16[1024,1024]{1,0:T(8,128)(2,1)}, bf16[1024,1536]{1,0:T(8,128)(2,1)}, bf16[1024,512]{1,0:T(8,128)(2,1)}, f32[4,2,1024]{2,1,0:T(2,128)}, bf16[1024,1024]{1,0:T(8,128)(2,1)}) custom-call(s32[4]{0:T(128)} %pad_add_fusion.place.refs_0_, bf16[4,128,1024]{2,1,0:T(8,128)(2,1)} %shard_map.346.own.rows, bf16[4,128,1024]{2,1,0:T(8,128)(2,1)} %copy-done, ...), custom_call_target="tpu_custom_call" | custom-call | flops 1 | bytes 1 | tf_op jit(solution)/shard_map/pallas_call | solution.py:716
  149.1 6.8 %collective-permute-done.24.low = bf16[2,256,512]{2,1,0:T(8,128)(2,1)S(1)} collective-permute-done((bf16[2,256,512]{2,1,0:T(8,128)(2,1)}, bf16[2,256,512]{2,1,0:T(8,128)(2,1)S(1)}, u32[]{:S(2)}, u32[]{:S(2)}) %collective-permute-start.24) | collective-permute-done | bytes 524320 | tf_op jit(solution)/shard_map/ppermute | solution.py:1721
  169.5 14.3 %shard_map.350 = (f32[1024,1024]{1,0:T(8,128)}, bf16[1024,1024]{1,0:T(8,128)(2,1)}, bf16[1024,512]{1,0:T(8,128)(2,1)}, bf16[128,1024]{1,0:T(8,128)(2,1)}, bf16[1...) custom-call(s32[4]{0:T(128)} %pad_add_fusion.place.refs_0_, ...), custom_call_target="tpu_custom_call" | custom-call | flops 1 | bytes 1 | tf_op jit(solution)/shard_map/pallas_call | solution.py:716
  186.3 5.6 %collective-permute-done.29 = bf16[128,1024]{1,0:T(8,128)(2,1)} collective-permute-done((bf16[128,1024]{1,0:T(8,128)(2,1)}, bf16[128,1024]{1,0:T(8,128)(2,1)}, u32[]{:S(2)}, u32[]{:S(2)}) %collective-permute-start.29) | collective-permute-done | bytes 262176 | tf_op jit(solution)/shard_map/ppermute | solution.py:1724
  199.0 13.5 %collective-permute-done.33.low = bf16[2,256,512]{2,1,0:T(8,128)(2,1)S(1)} collective-permute-done((bf16[2,256,512]{2,1,0:T(8,128)(2,1)S(1)}, bf16[2,256,512]{2,1,0:T(8,128)(2,1)S(1)}, u32[]{:S(2)}, u32[]{:S(2)}) %collective-permute-start.33) | collective-permute-done | bytes 524320 | tf_op jit(solution)/shard_map/ppermute | solution.py:1721
  222.4 25.9 %shard_map.353 = (bf16[4,4,256,512]{3,2,1,0:T(8,128)(2,1)}, f32[1024,1024]{1,0:T(8,128)}, bf16[1024,1024]{1,0:T(8,128)(2,1)}, bf16[1024,1024]{1,0:T(8,128)(2,1)}...) custom-call(s32[4]{0:T(128)} %pad_add_fusion.place.refs_0_, f32[1024,1024]{1,0:T(8,128)} %get-tuple-element.941.after.refs_1_, ...), custom_call_target="tpu_custom_call" | custom-call | flops 1 | bytes 1 | tf_op jit(solution)/shard_map/pallas_call | solution.py:716
  248.3 5.1 %all-gather.15.cloned.1.call-done = bf16[16,256,512]{2,1,0:T(8,128)(2,1)} async-done(((bf16[4,256,512]{2,1,0:T(8,128)(2,1)}), bf16[16,256,512]{2,1,0:T(8,128)(2,1)}) %all-gather.15.cloned.1.call-update) | async-done | bytes 4194320 | tf_op jit(solution)/shard_map/all_gather | solution.py:1823
  253.9 24.0 %shard_map.354 = (bf16[256,2048]{1,0:T(8,128)(2,1)}, bf16[256,2048]{1,0:T(8,128)(2,1)}, bf16[256,2048]{1,0:T(8,128)(2,1)}, bf16[128,2048]{1,0:T(8,128)(2,1)}, bf...) custom-call(s32[4]{0:T(128)} %pad_add_fusion.place.refs_0_, ...), custom_call_target="tpu_custom_call" | custom-call | flops 1 | bytes 1 | tf_op jit(solution)/shard_map/pallas_call | solution.py:716
  278.7 5.4 %collective-permute-done.36.theirs = bf16[4,128,1024]{2,1,0:T(8,128)(2,1)S(1)} collective-permute-done((bf16[4,128,1024]{2,1,0:T(8,128)(2,1)}, bf16[4,128,1024]{2,1,0:T(8,128)(2,1)S(1)}, u32[]{:S(2)}, u32[]{:S(2)}) %collective-permute-start.36) | collective-permute-done | bytes 1048608 | tf_op jit(solution)/shard_map/ppermute | solution.py:1718
  295.2 22.3 %shard_map.355 = (f32[1024,1024]{1,0:T(8,128)}, bf16[1024,1024]{1,0:T(8,128)(2,1)}, f32[8,1024]{1,0:T(8,128)}, bf16[128,1024]{1,0:T(8,128)(2,1)}, bf16[256,2048]...) custom-call(s32[4]{0:T(128)} %pad_add_fusion.place.refs_0_, ...), custom_call_target="tpu_custom_call" | custom-call | flops 1 | bytes 1 | tf_op jit(solution)/shard_map/pallas_call | solution.py:716
  325.7 28.5 %shard_map.358 = (f32[4,128,1024]{2,1,0:T(8,128)}, bf16[1024,1024]{1,0:T(8,128)(2,1)}, f32[8,1024]{1,0:T(8,128)}, bf16[1024,1536]{1,0:T(8,128)(2,1)}) custom-call(s32[4]{0:T(128)} %pad_add_fusion.place.refs_0_, f32[1024,1024]{1,0:T(8,128)} %get-tuple-element.941.after.refs_1_, bf16[1024,1024]{1,0:T(8,128)(2,1)} %get-tuple-element.942.refs_2_, ...), custom_call_target="tpu_custom_call" | custom-call | flops 1 | bytes 1 | tf_op jit(solution)/shard_map/pallas_call | solution.py:716
  354.2 5.5 %collective-permute-done.44.from_side = bf16[128,2048]{1,0:T(8,128)(2,1)S(1)} collective-permute-done((bf16[128,2048]{1,0:T(8,128)(2,1)}, bf16[128,2048]{1,0:T(8,128)(2,1)S(1)}, u32[]{:S(2)}, u32[]{:S(2)}) %collective-permute-start.44) | collective-permute-done | bytes 524320 | tf_op jit(solution)/shard_map/ppermute | solution.py:1721
  374.9 12.7 %shard_map.359 = (bf16[256,2048]{1,0:T(8,128)(2,1)}, bf16[256,2048]{1,0:T(8,128)(2,1)}, bf16[256,2048]{1,0:T(8,128)(2,1)}, bf16[128,2048]{1,0:T(8,128)(2,1)}, bf16[128,2048]{1,0:T(8,128)(2,1)}) custom-call(s32[4]{0:T(128)} %pad_add_fusion.place.refs_0_, bf16[1024,1024]{1,0:T(8,128)(2,1)} %get-tuple-element.974.normed, ...), custom_call_target="tpu_custom_call" | custom-call | flops 1 | bytes 1 | tf_op jit(solution)/shard_map/pallas_call | solution.py:716
  397.2 7.9 %shard_map.365 = (f32[4,128,1024]{2,1,0:T(8,128)}, bf16[4,128,1024]{2,1,0:T(8,128)(2,1)}) custom-call(s32[4]{0:T(128)} %pad_add_fusion.place.refs_0_, bf16[1024,1536]{1,0:T(8,128)(2,1)} %get-tuple-element.1018.dq.dk.dv.dqkv, bf16[1024,2048]{1,0:T(8,128)(2,1)} %get-tuple-element.1019.weights.refs_6_), custom_call_target="tpu_custom_call" | custom-call | flops 1 | bytes 1 | tf_op jit(solution)/shard_map/pallas_call | solution.py:716
  413.5 5.8 %shard_map.370 = (bf16[176,1024]{1,0:T(8,128)(2,1)}, bf16[176,1024]{1,0:T(8,128)(2,1)}, bf16[176,1024]{1,0:T(8,128)(2,1)}, bf16[176,1024]{1,0:T(8,128)(2,1)}) custom-call(s32[4]{0:T(128)} %pad_add_fusion.place.refs_0_, bf16[4,128,1024]{2,1,0:T(8,128)(2,1)} %shard_map.346.own.rows, f32[4,128,1024]{2,1,0:T(8,128)} %get-tuple-element.1055.grad_own, ...), custom_call_target="tpu_custom_call" | custom-call | flops 1 | bytes 1 | tf_op jit(solution)/shard_map/pallas_call | solution.py:716
  422.9 13.2 %collective-permute-done.55.over = bf16[256,2048]{1,0:T(8,128)(2,1)S(1)} collective-permute-done((bf16[256,2048]{1,0:T(8,128)(2,1)}, bf16[256,2048]{1,0:T(8,128)(2,1)S(1)}, u32[]{:S(2)}, u32[]{:S(2)}) %collective-permute-start.55) | collective-permute-done | bytes 1048608 | tf_op jit(solution)/shard_map/ppermute | solution.py:1721
  445.5 7.7 %collective-permute-done.61.refs_3_ = bf16[176,1024]{1,0:T(8,128)(2,1)S(1)} collective-permute-done((bf16[176,1024]{1,0:T(8,128)(2,1)}, bf16[176,1024]{1,0:T(8,128)(2,1)S(1)}, u32[]{:S(2)}, u32[]{:S(2)}) %collective-permute-start.61) | collective-permute-done | bytes 360480 | tf_op jit(solution)/shard_map/ppermute | solution.py:1724
  (322 shorter events, 202.4 us)
Async XLA Ops:
  7.2 93.6 %all-gather.9.cloned.1.call-start = ((), (), s32[]{:S(2)}) async-start(), calls=%async_computation.7 | async-start | bytes 1310720 | tf_op jit(solution)/shard_map/all_gather | solution.py:1733
  52.5 87.4 %all-gather.11.cloned.1.call-start = ((), (), s32[]{:S(2)}) async-start(), calls=%async_computation.8 | async-start | bytes 1310720 | tf_op jit(solution)/shard_map/all_gather | solution.py:1733
  73.3 26.8 %collective-permute-start.13 = (bf16[384,512]{1,0:T(8,128)(2,1)S(1)}, bf16[384,512]{1,0:T(8,128)(2,1)S(1)}, u32[]{:S(2)}, u32[]{:S(2)}) collective-permute-start(bf16[384,512]{1,0:T(8,128)(2,1)S(1)} %slice.47), channel_id=1, source_target_pairs={{0,16},{8,24},{16,0},{24,8},{1,17},{9,25},{17,1},{25,9},{2,18},{10... | collective-permute-start | bytes 1179656 | tf_op jit(solution)/shard_map/ppermute | solution.py:1721
  73.6 27.2 %collective-permute-start.14 = (bf16[384,512]{1,0:T(8,128)(2,1)S(1)}, bf16[384,512]{1,0:T(8,128)(2,1)S(1)}, u32[]{:S(2)}, u32[]{:S(2)}) collective-permute-start(bf16[384,512]{1,0:T(8,128)(2,1)S(1)} %slice.48), channel_id=1, source_target_pairs={{0,8},{8,0},{16,24},{24,16},{1,9},{9,1},{17,25},{25,17},{2,10},{10... | collective-permute-start | bytes 1179656 | tf_op jit(solution)/shard_map/ppermute | solution.py:1721
  104.3 79.8 %all-gather.13.cloned.1.call-start = ((), (), s32[]{:S(2)}) async-start(), calls=%async_computation.9 | async-start | bytes 1310720 | tf_op jit(solution)/shard_map/all_gather | solution.py:1733
  109.5 30.4 %collective-permute-start.19 = (bf16[4,256,512]{2,1,0:T(8,128)(2,1)}, bf16[4,256,512]{2,1,0:T(8,128)(2,1)S(1)}, u32[]{:S(2)}, u32[]{:S(2)}) collective-permute-start(bf16[4,256,512]{2,1,0:T(8,128)(2,1)} %bitcast.68), channel_id=1, source_target_pairs={{0,8},{8,0},{16,24},{24,16},{1,9},{9,1},{17,25},{25,17},{2,10},{10... | collective-permute-start | bytes 3145736 | tf_op jit(solution)/shard_map/ppermute | solution.py:1721
  111.0 28.9 %collective-permute-start.20 = (bf16[4,256,512]{2,1,0:T(8,128)(2,1)}, bf16[4,256,512]{2,1,0:T(8,128)(2,1)S(1)}, u32[]{:S(2)}, u32[]{:S(2)}) collective-permute-start(bf16[4,256,512]{2,1,0:T(8,128)(2,1)} %bitcast.69), channel_id=1, source_target_pairs={{0,16},{8,24},{16,0},{24,8},{1,17},{9,25},{17,1},{25,9},{2,18},{10... | collective-permute-start | bytes 3145736 | tf_op jit(solution)/shard_map/ppermute | solution.py:1721
  145.2 108.2 %all-gather.15.cloned.1.call-start = ((), (), s32[]{:S(2)}) async-start(), calls=%async_computation.10 | async-start | bytes 5242880 | tf_op jit(solution)/shard_map/all_gather | solution.py:1823
  158.7 33.2 %collective-permute-start.30 = (bf16[4,256,512]{2,1,0:T(8,128)(2,1)}, bf16[4,256,512]{2,1,0:T(8,128)(2,1)S(1)}, u32[]{:S(2)}, u32[]{:S(2)}) collective-permute-start(bf16[4,256,512]{2,1,0:T(8,128)(2,1)} %bitcast.65), channel_id=1, source_target_pairs={{0,8},{8,0},{16,24},{24,16},{1,9},{9,1},{17,25},{25,17},{2,10},{10... | collective-permute-start | bytes 3145736 | tf_op jit(solution)/shard_map/ppermute | solution.py:1721
  159.3 32.6 %collective-permute-start.31 = (bf16[4,256,512]{2,1,0:T(8,128)(2,1)}, bf16[4,256,512]{2,1,0:T(8,128)(2,1)}, u32[]{:S(2)}, u32[]{:S(2)}) collective-permute-start(bf16[4,256,512]{2,1,0:T(8,128)(2,1)} %bitcast.66), channel_id=1, source_target_pairs={{0,16},{8,24},{16,0},{24,8},{1,17},{9,25},{17,1},{25,9},{2,18},{10... | collective-permute-start | bytes 3145736 | tf_op jit(solution)/shard_map/ppermute | solution.py:1721
  162.0 30.0 %collective-permute-start.29 = (bf16[128,1024]{1,0:T(8,128)(2,1)}, bf16[128,1024]{1,0:T(8,128)(2,1)}, u32[]{:S(2)}, u32[]{:S(2)}) collective-permute-start(bf16[128,1024]{1,0:T(8,128)(2,1)} %get-tuple-element.741), channel_id=1, source_target_pairs={{3,0},{0,1},{1,2},{2,3},{7,4},{4,5},{5,6},{6,7},{11,8},{8,9},{9,10... | collective-permute-start | bytes 786440 | tf_op jit(solution)/shard_map/ppermute | solution.py:1724
  191.9 130.7 %reduce-scatter.13.cloned.1.call-start = ((), (), s32[]{:S(2)}) async-start(), calls=%async_computation.11 | async-start | bytes 5242880
  253.5 107.0 %reduce-scatter.7.cloned.1.call-start = ((), (), s32[]{:S(2)}) async-start(), calls=%async_computation.4 | async-start | bytes 1310720 | tf_op jit(solution)/shard_map/reduce_scatter | solution.py:1859
  284.2 33.5 %collective-permute-start.38 = (bf16[128,2048]{1,0:T(8,128)(2,1)}, bf16[128,2048]{1,0:T(8,128)(2,1)}, u32[]{:S(2)}, u32[]{:S(2)}) collective-permute-start(bf16[128,2048]{1,0:T(8,128)(2,1)} %get-tuple-element.872), channel_id=1, source_target_pairs={{0,8},{8,0},{16,24},{24,16},{1,9},{9,1},{17,25},{25,17},{2,10},{10... | collective-permute-start | bytes 1572872 | tf_op jit(solution)/shard_map/ppermute | solution.py:1721
  285.3 32.3 %collective-permute-start.39 = (bf16[128,2048]{1,0:T(8,128)(2,1)}, bf16[128,2048]{1,0:T(8,128)(2,1)}, u32[]{:S(2)}, u32[]{:S(2)}) collective-permute-start(bf16[128,2048]{1,0:T(8,128)(2,1)} %get-tuple-element.873), channel_id=1, source_target_pairs={{0,16},{8,24},{16,0},{24,8},{1,17},{9,25},{17,1},{25,9},{2,18},{10... | collective-permute-start | bytes 1572872 | tf_op jit(solution)/shard_map/ppermute | solution.py:1721
  288.6 28.9 %collective-permute-start.40 = (bf16[128,1024]{1,0:T(8,128)(2,1)}, bf16[128,1024]{1,0:T(8,128)(2,1)S(1)}, u32[]{:S(2)}, u32[]{:S(2)}) collective-permute-start(bf16[128,1024]{1,0:T(8,128)(2,1)} %get-tuple-element.903), channel_id=1, source_target_pairs={{1,0},{2,1},{3,2},{0,3},{5,4},{6,5},{7,6},{4,7},{9,8},{10,9},{11,1... | collective-permute-start | bytes 786440 | tf_op jit(solution)/shard_map/ppermute | solution.py:1724
  322.7 82.5 %reduce-scatter.11.cloned.1.call-start = ((), (), s32[]{:S(2)}) async-start(), calls=%async_computation.6 | async-start | bytes 1310720 | tf_op jit(solution)/shard_map/reduce_scatter | solution.py:1868
  322.7 37.0 %collective-permute-start.46 = (bf16[256,2048]{1,0:T(8,128)(2,1)}, bf16[256,2048]{1,0:T(8,128)(2,1)S(1)}, u32[]{:S(2)}, u32[]{:S(2)}) collective-permute-start(bf16[256,2048]{1,0:T(8,128)(2,1)} %get-tuple-element.968), channel_id=1, source_target_pairs={{0,16},{8,24},{16,0},{24,8},{1,17},{9,25},{17,1},{25,9},{2,18},{10... | collective-permute-start | bytes 3145736 | tf_op jit(solution)/shard_map/ppermute | solution.py:1721
  323.6 36.8 %collective-permute-start.47 = (bf16[256,2048]{1,0:T(8,128)(2,1)}, bf16[256,2048]{1,0:T(8,128)(2,1)}, u32[]{:S(2)}, u32[]{:S(2)}) collective-permute-start(bf16[256,2048]{1,0:T(8,128)(2,1)} %get-tuple-element.969), channel_id=1, source_target_pairs={{0,8},{8,0},{16,24},{24,16},{1,9},{9,1},{17,25},{25,17},{2,10},{10... | collective-permute-start | bytes 3145736 | tf_op jit(solution)/shard_map/ppermute | solution.py:1721
  325.3 34.3 %collective-permute-start.44 = (bf16[128,2048]{1,0:T(8,128)(2,1)}, bf16[128,2048]{1,0:T(8,128)(2,1)S(1)}, u32[]{:S(2)}, u32[]{:S(2)}) collective-permute-start(bf16[128,2048]{1,0:T(8,128)(2,1)} %get-tuple-element.951), channel_id=1, source_target_pairs={{0,8},{8,0},{16,24},{24,16},{1,9},{9,1},{17,25},{25,17},{2,10},{10... | collective-permute-start | bytes 1572872 | tf_op jit(solution)/shard_map/ppermute | solution.py:1721
  325.4 34.3 %collective-permute-start.45 = (bf16[128,2048]{1,0:T(8,128)(2,1)}, bf16[128,2048]{1,0:T(8,128)(2,1)}, u32[]{:S(2)}, u32[]{:S(2)}) collective-permute-start(bf16[128,2048]{1,0:T(8,128)(2,1)} %get-tuple-element.952), channel_id=1, source_target_pairs={{0,16},{8,24},{16,0},{24,8},{1,17},{9,25},{17,1},{25,9},{2,18},{10... | collective-permute-start | bytes 1572872 | tf_op jit(solution)/shard_map/ppermute | solution.py:1721
  364.7 97.3 %reduce-scatter.9.cloned.1.call-start = ((), (), s32[]{:S(2)}) async-start(), calls=%async_computation.5 | async-start | bytes 1310720 | tf_op jit(solution)/shard_map/reduce_scatter | solution.py:1877
  419.4 26.0 %collective-permute-start.60 = (bf16[176,1024]{1,0:T(8,128)(2,1)}, bf16[176,1024]{1,0:T(8,128)(2,1)S(1)}, u32[]{:S(2)}, u32[]{:S(2)}) collective-permute-start(bf16[176,1024]{1,0:T(8,128)(2,1)} %get-tuple-element.1064), channel_id=1, source_target_pairs={{2,0},{3,1},{0,2},{1,3},{6,4},{7,5},{4,6},{5,7},{10,8},{11,9},{8,1... | collective-permute-start | bytes 1081352 | tf_op jit(solution)/shard_map/ppermute | solution.py:1724
  422.2 31.0 %collective-permute-start.61 = (bf16[176,1024]{1,0:T(8,128)(2,1)}, bf16[176,1024]{1,0:T(8,128)(2,1)S(1)}, u32[]{:S(2)}, u32[]{:S(2)}) collective-permute-start(bf16[176,1024]{1,0:T(8,128)(2,1)} %get-tuple-element.1065), channel_id=1, source_target_pairs={{3,0},{0,1},{1,2},{2,3},{7,4},{4,5},{5,6},{6,7},{11,8},{8,9},{9,10... | collective-permute-start | bytes 1081352 | tf_op jit(solution)/shard_map/ppermute | solution.py:1724
  (113 other events, 1334.4 us)
Sparse Core Ops, SparseCore 0:
  52.6 27.4 all-gather.8
  104.5 35.4 all-gather.10
  145.3 38.7 all-gather.12
  192.1 61.3 all-gather.14
  256.2 55.8 reduce-scatter.12
  322.8 25.5 reduce-scatter.6
  364.8 25.5 reduce-scatter.10
  397.3 26.6 reduce-scatter.8

commit v3 on v2

--- a/solution.py
+++ b/solution.py
@@ -637,7 +637,8 @@
 
 
 BLOCK = 256
-ANY = pl.BlockSpec(memory_space=pltpu.HBM)
+ANY = pl.BlockSpec(memory_space=pl.ANY)
+HBM = pl.BlockSpec(memory_space=pltpu.HBM)
 SMEM = pl.BlockSpec(memory_space=pltpu.SMEM)
 VMEM = pl.BlockSpec(memory_space=pltpu.VMEM)
 LATE = object()
@@ -700,7 +701,7 @@
 
     return call(
         wrapped,
-        [(ANY if spec is LATE else spec, shape) for spec, shape in outs],
+        [(HBM if spec is LATE else spec, shape) for spec, shape in outs],
         [ANY if spec is LATE else spec for spec in ins],
         operands,
         [*scratch, *buffers, pltpu.SemaphoreType.DMA((max(count, 1),))],
@@ -737,8 +738,7 @@
     return pl.ds(pl.multiple_of(offset, unit), count)
 
 
-def prepare_kernel(place, image, text, ids, cot, norms, wq, wk, wv, wo, cq, ck, cv, co, win, wout, *outs):
-    keep, sent, rows_keep, rows_sent, cot_keep, cot_sent, text_pair, sems = outs
+def prepare_kernel(place, norms, wq, wk, wv, wo, cq, ck, cv, co, win, wout, keep, sent, sems):
     core = place[1]
     copies = []
     for target, which in ((sent, 1 - core), (keep, core)):
@@ -758,24 +758,43 @@
                         target.at[256 + part * 128 : 384 + part * 128, one * 256 : (one + 1) * 256],
                     )
                 )
-        copies.append((norms, target.at[512:528, :]))
+        rows = jnp.concatenate([norms[...], jnp.zeros((10, 128), F32)], 0).astype(BF)
+        target[512:528, :] = jnp.concatenate([rows] * 4, 1)
+    run_copies(copies, sems)
+
+
+def prepare(place, norms, weights):
+    return call(
+        prepare_kernel,
+        [(VMEM, like(528, 512))] * 2,
+        [SMEM, VMEM] + [ANY] * 10,
+        (place, norms, *weights),
+        [pltpu.SemaphoreType.DMA((24,))],
+    )
+
+
+def prepare_rows_kernel(place, ids, image, text, cot, *outs):
+    rows_keep, rows_sent, cot_keep, cot_sent, text_pair, sems = outs
+    core = place[1]
+    copies = []
     for target, cots, which in ((rows_sent, cot_sent, 1 - core), (rows_keep, cot_keep, core)):
         for one in range(2):
             copies.append((image.at[one, at(which * 128, 128), :], target.at[one]))
             copies.append((cot.at[one, at(which * 128, 128), :], cots.at[one]))
     for one in range(2):
         copies.append((text.at[one], text_pair.at[one, 0:32, :]))
-        copies.append((ids.at[one], text_pair.at[one, 32:48, :]))
+        row = jnp.concatenate([ids[one : one + 1, :].astype(F32), jnp.zeros((1, 896), F32)], 1)
+        text_pair[one, 32:48, :] = jnp.concatenate([row] * 16, 0).astype(BF)
     run_copies(copies, sems)
 
 
-def prepare(place, image, text, ids, cot, norms, weights):
-    return call(
-        prepare_kernel,
-        [(VMEM, like(528, 512))] * 2 + [(VMEM, like(2, 128, 1024))] * 4 + [(VMEM, like(2, 48, 1024))],
-        [SMEM] + [ANY] * 15,
-        (place, image, text, ids, cot, norms, *weights),
-        [pltpu.SemaphoreType.DMA((42,))],
+def prepare_rows(place, ids, image, text, cot):
+    return call(
+        prepare_rows_kernel,
+        [(VMEM, like(2, 128, 1024))] * 4 + [(VMEM, like(2, 48, 1024))],
+        [SMEM, VMEM] + [ANY] * 3,
+        (place, ids, image, text, cot),
+        [pltpu.SemaphoreType.DMA((10,))],
     )
 
 
@@ -846,6 +865,21 @@
     )[0]
 
 
+def join_pieces_kernel(place, *refs):
+    pieces, whole, sems = refs[:4], refs[4], refs[5]
+    run_copies([(piece, whole.at[i]) for i, piece in enumerate(pieces)], sems)
+
+
+def join_pieces(place, pieces):
+    return call(
+        join_pieces_kernel,
+        [(VMEM, like(4, *pieces[0].shape))],
+        [SMEM] + [ANY] * 4,
+        (place, *pieces),
+        [pltpu.SemaphoreType.DMA((4,))],
+    )[0]
+
+
 def arrange_kernel(place, *refs):
     messages, text, sems = refs[:4], refs[4], refs[5]
     run_copies(
@@ -863,89 +897,48 @@
     )[0]
 
 
-def gather_copies(batches, buffer, whole, rows_of, loads, stores, extra=()):
-    started = []
-    for i, batch in enumerate(batches):
-        copies = [pltpu.make_async_copy(a, b, loads.at[i * 8 + j]) for j, (a, b) in enumerate(batch)]
-        for copy in copies:
-            copy.start()
-        started.append(copies)
-    stored = [pltpu.make_async_copy(a, b, stores.at[4 + i]) for i, (a, b) in enumerate(extra)]
-    for copy in stored:
+def started(pairs, sems):
+    copies = [pltpu.make_async_copy(source, target, sems.at[i]) for i, (source, target) in enumerate(pairs)]
+    for copy in copies:
         copy.start()
-    for i, copies in enumerate(started):
-        for copy in copies:
-            copy.wait()
-        rows = rows_of(i)
-        stored.append(pltpu.make_async_copy(buffer.at[rows, :], whole.at[rows, :], stores.at[i]))
-        stored[-1].start()
-    for copy in stored:
+    return copies
+
+
+def wait_all(copies):
+    for copy in copies:
         copy.wait()
 
 
-def assemble_first_kernel(place, *refs):
-    near, far = refs[:5], refs[5:10]
-    whole, norms, buffer, loads, stores = refs[10:]
+def first_pieces(place, near, far, buffer, norms):
     chip, top = place[0], place[2]
-    batches, extra = [], []
+    weights, rows = [], []
     for source in range(4):
-        batch = []
         for half in range(2):
             row = at((chip ^ source) * 256 + half * 128, 128)
             piece, first = (near[source], half * 128) if source < 3 else (near[3 + half], 0)
-            batch.append((piece.at[first : first + 128, :], buffer.at[row, at(top * 512, 512, 512)]))
+            weights.append((piece.at[first : first + 128, :], buffer.at[row, at(top * 512, 512, 512)]))
             low = 256 + half * 16 if source < 3 else 128 + half * 16
             piece = near[source] if source < 3 else near[4]
             column = at((chip ^ source) * 256 + half * 128, 128)
-            extra.append((piece.at[low : low + 16, 0:128], norms.at[:, column]))
+            rows.append((piece.at[low : low + 16, 0:128], norms.at[:, column]))
             for step in range(3):
                 first = step * 256 + half * 128
                 piece = far[source] if source < 3 else far[3 + first // 384]
                 first = first if source < 3 else first % 384
                 columns = at((top + 1 + step) % 4 * 512, 512, 512)
-                batch.append((piece.at[first : first + 128, :], buffer.at[row, columns]))
-        batches.append(batch)
-    gather_copies(batches, buffer, whole, lambda i: at((chip ^ i) * 256, 256), loads, stores, extra)
-
-
-ASSEMBLE_SCRATCH = [
-    pltpu.VMEM((1024, 2048), BF),
-    pltpu.SemaphoreType.DMA((32,)),
-    pltpu.SemaphoreType.DMA((12,)),
-]
-
-
-def assemble_first(place, near, far):
-    return call(
-        assemble_first_kernel,
-        [(ANY, like(1024, 2048)), (VMEM, like(16, 1024))],
-        [SMEM] + [ANY] * 10,
-        (place, *near, *far),
-        ASSEMBLE_SCRATCH,
-    )
-
-
-def assemble_kernel(place, own, side, over, low, high, whole, buffer, loads, stores):
+                weights.append((piece.at[first : first + 128, :], buffer.at[row, columns]))
+    return weights, rows
+
+
+def later_pieces(place, own, side, over, low, high, buffer):
     chip = place[0]
-    batches = []
+    weights = []
     for source in range(4):
-        batch = []
         for top in range(4):
             piece = (own, side, over, low if top < 2 else high)[source]
             rows, columns = at((chip ^ source) * 256, 256), slice(top * 512, (top + 1) * 512)
-            batch.append((piece.at[top % 2 if source == 3 else top], buffer.at[rows, columns]))
-        batches.append(batch)
-    gather_copies(batches, buffer, whole, lambda i: at((chip ^ i) * 256, 256), loads, stores)
-
-
-def assemble(place, own, others):
-    return call(
-        assemble_kernel,
-        [(ANY, like(1024, 2048))],
-        [SMEM] + [ANY] * 5,
-        (place, own, *others),
-        ASSEMBLE_SCRATCH,
-    )[0]
+            weights.append((piece.at[top % 2 if source == 3 else top], buffer.at[rows, columns]))
+    return weights
 
 
 def norm_row(norms, one):
@@ -1018,10 +1011,17 @@
     )
 
 
-def self_fwd_kernel(place, own, other, norms, weights, normed, qkv, mix, lse, part):
+def self_fwd_kernel(place, own, other, *refs):
+    near, far = refs[:5], refs[5:10]
+    whole, norms, normed, qkv, mix, lse, part, weights, loads, store = refs[10:]
+    pieces, rows = first_pieces(place, near, far, weights, norms)
+    copies = started(rows + pieces, loads)
+    wait_all(copies[: len(rows)])
     gain, bias = norm_row(norms, 0), norm_row(norms, 1)
     for row, half, number in image_blocks(place, own, other):
         normed[at(row, 128), :] = normalized(half[number].astype(F32), gain, bias)
+    wait_all(copies[len(rows) :])
+    (stored,) = started([(weights, whole)], store)
     for one in range(3):
         qkv[:, one * 512 : (one + 1) * 512] = dot(normed[...], columns_of(weights, one)).astype(BF)
     causal = causal_pair(512)
@@ -1045,32 +1045,41 @@
 
     lax.fori_loop(0, 4, pair_step, 0)
     project_into(part, mix[...], columns_of(weights, 3), NT)
-
-
-def fused_self_forward(place, own, other, norms, weights):
+    stored.wait()
+
+
+def fused_self_forward(place, own, other, near, far):
     return call(
         self_fwd_kernel,
         [
+            (HBM, like(1024, 2048)),
+            (VMEM, like(16, 1024)),
             (VMEM, like(1024, 1024)),
             (VMEM, like(1024, 1536)),
             (VMEM, like(1024, 512)),
             (VMEM, like(4, 2, 1024, dtype=F32)),
             (VMEM, like(1024, 1024)),
         ],
-        [SMEM, VMEM, VMEM, VMEM, VMEM],
-        (place, own, other, norms, weights),
+        [SMEM, VMEM, VMEM] + [ANY] * 10,
+        (place, own, other, *near, *far),
+        [pltpu.VMEM((1024, 2048), BF), pltpu.SemaphoreType.DMA((40,)), pltpu.SemaphoreType.DMA((1,))],
     )
 
 
 def cross_fwd_kernel(
-    place, own, other, mine, theirs, norms, text, ids, caption, weights, after, normed, queries, keys, mix, lse, part
+    place, own, other, mine, theirs, norms, text, ids, caption, *refs
 ):
+    pieces = refs[:5]
+    whole, after, normed, queries, keys, mix, lse, part, weights, loads, store = refs[5:]
+    copies = started(later_pieces(place, *pieces, weights), loads)
     gain, bias = norm_row(norms, 2), norm_row(norms, 3)
     for row, half, number in image_blocks(place, own, other):
         rows = at(row, 128)
         values = half[number].astype(F32) + (mine[rows, :].astype(F32) + theirs[rows, :].astype(F32))
         after[rows, :] = values
         normed[rows, :] = normalized(values, gain, bias)
+    wait_all(copies)
+    (stored,) = started([(weights, whole)], store)
     project_into(queries, normed[...], columns_of(weights, 0))
     w_text = jnp.concatenate([columns_of(weights, 1), columns_of(weights, 2)], 1)
     keys[...] = dot(text[...], w_text).astype(BF)
@@ -1087,12 +1096,14 @@
 
     lax.fori_loop(0, 4, pair_step, 0)
     project_into(part, mix[...], columns_of(weights, 3), NT)
-
-
-def fused_cross_forward(place, own, other, mine, theirs, norms, text, ids, caption, weights):
+    stored.wait()
+
+
+def fused_cross_forward(place, own, other, mine, theirs, norms, text, ids, caption, pieces):
     return call(
         cross_fwd_kernel,
         [
+            (HBM, like(1024, 2048)),
             (VMEM, like(1024, 1024, dtype=F32)),
             (VMEM, like(1024, 1024)),
             (VMEM, like(1024, 512)),
@@ -1101,8 +1112,9 @@
             (VMEM, like(4, 2, 1024, dtype=F32)),
             (VMEM, like(1024, 1024)),
         ],
-        [SMEM] + [VMEM] * 8 + [VMEM],
-        (place, own, other, mine, theirs, norms, text, ids, caption, weights),
+        [SMEM] + [VMEM] * 8 + [ANY] * 5,
+        (place, own, other, mine, theirs, norms, text, ids, caption, *pieces),
+        [pltpu.VMEM((1024, 2048), BF), pltpu.SemaphoreType.DMA((16,)), pltpu.SemaphoreType.DMA((1,))],
     )
 
 
@@ -1140,8 +1152,9 @@
 
 
 def feed_first_kernel(
-    place, after, mine, theirs, norms, cot_own, cot_other, weights,
-    g_whole, after_out, normed_out, cot_out, out_sum, back, after_cross, normed, cot, back_sum, rows_t, cot_t, grads, sems,
+    place, after, mine, theirs, norms, cot_own, cot_other, p_own, p_side, p_over, p_low, p_high,
+    g_whole, after_out, normed_out, cot_out, out_sum, back, after_cross, normed, cot, back_sum, rows_t, cot_t, grads,
+    weights, sems, loads,
 ):
     step = pl.program_id(0)
     pairs = ((after_cross, after_out), (normed, normed_out), (cot, cot_out))
@@ -1149,6 +1162,7 @@
 
     @pl.when(step == 0)
     def _():
+        copies = started(later_pieces(place, p_own, p_side, p_over, p_low, p_high, weights), loads)
         gain, bias = norm_row(norms, 4), norm_row(norms, 5)
         for low in range(0, 1024, 128):
             rows = slice(low, low + 128)
@@ -1166,10 +1180,10 @@
             rows = at(block * 256 + place[1] * 128, 128)
             out_sum[rows, :] = after_cross[rows, :]
         back_sum[...] = jnp.zeros_like(back_sum)
-
-    feed_step(
-        normed, cot, rows_t, cot_t, (weights[:, :512], weights[:, 512:]), out_sum, back_sum, grads
-    )
+        wait_all(copies)
+
+    blocks = [weights[:, at(step * 1024 + block * 512, 512, 512)] for block in range(2)]
+    feed_step(normed, cot, rows_t, cot_t, blocks, out_sum, back_sum, grads)
     for chip in range(4):
         for block in range(2):
             part = grads[chip * 256 : (chip + 1) * 256, block * 512 : (block + 1) * 512]
@@ -1219,26 +1233,27 @@
 FEED_FLOPS = 13 * 2**30
 
 
-def feed_first(place, after, mine, theirs, norms, cot_own, cot_other, weights):
+def feed_first(place, after, mine, theirs, norms, cot_own, cot_other, pieces):
     square = once(1024, 1024)
     return call(
         feed_first_kernel,
         [(pl.BlockSpec((4, 2, 256, 512), lambda i: (0, i, 0, 0)), like(4, 4, 256, 512))]
         + [
-            (ANY, like(1024, 1024, dtype=F32)),
-            (ANY, like(1024, 1024)),
-            (ANY, like(1024, 1024)),
+            (HBM, like(1024, 1024, dtype=F32)),
+            (HBM, like(1024, 1024)),
+            (HBM, like(1024, 1024)),
             (square, like(1024, 1024, dtype=F32)),
             (square, like(1024, 1024)),
         ],
         [SMEM, square, square, square, once(16, 1024), once(4, 128, 1024), once(4, 128, 1024)]
-        + [pl.BlockSpec((1024, 1024), lambda i: (0, i))],
-        (place, after, mine, theirs, norms, cot_own, cot_other, weights),
+        + [ANY] * 5,
+        (place, after, mine, theirs, norms, cot_own, cot_other, *pieces),
         [pltpu.VMEM((1024, 1024), F32)]
         + [pltpu.VMEM((1024, 1024), BF)] * 2
         + [pltpu.VMEM((1024, 1024), F32)]
         + [pltpu.VMEM((1024, 1024), BF)] * 2
-        + [pltpu.VMEM((1024, 1024), F32), pltpu.SemaphoreType.DMA((3,))],
+        + [pltpu.VMEM((1024, 1024), F32), pltpu.VMEM((1024, 2048), BF)]
+        + [pltpu.SemaphoreType.DMA((3,)), pltpu.SemaphoreType.DMA((16,))],
         limit=60,
         grid=(2,),
         flops=FEED_FLOPS,
@@ -1741,25 +1756,24 @@
     def grad_corners(grads):
         return [across(grads[3], 1), across(grads[4], 2)]
 
-    def grad_sides(grads, got):
-        to_over, to_side = relay(grads[2], grads[1], *got)
-        return [across(to_over, 2), across(to_side, 1)]
+    def grad_sides(grads, got, later):
+        to_over, to_side, later = tie((*relay(grads[2], grads[1], *got), later))
+        return [across(to_over, 2), across(to_side, 1)], later
 
     def halves(total):
         cut = total.reshape(2, 128, 512)
         sent = lax.dynamic_index_in_dim(cut, 1 - core, 0, False)
         return lax.dynamic_index_in_dim(cut, core, 0, False), swap(sent)
 
-    ids_wide = jnp.pad(segment_ids.astype(BF)[:, None, :], ((0, 0), (0, 15), (0, 896)))
-    norms_wide = jnp.pad(jnp.stack(norms).astype(BF), ((0, 10), (0, 384)))
-    keep, sent, rows_keep, rows_sent, cot_keep, cot_sent, text_pair = prepare(
-        place, image_rows, text_rows, ids_wide, cotangent, norms_wide, weights
-    )
-    v = {"rows_keep": rows_keep, "cot_keep": cot_keep, "text_pair": text_pair}
-    v["taken"], v["rows_taken"], v["cot_taken"] = swap(sent), swap(rows_sent), swap(cot_sent)
-    v["text_taken"] = swap(text_pair)
+    keep, sent = prepare(place, jnp.stack(norms), weights)
+    v = {"taken": swap(sent)}
+    v["rows_keep"], v["rows_sent"], v["cot_keep"], v["cot_sent"], v["text_pair"] = prepare_rows(
+        place, segment_ids, image_rows, text_rows, cotangent
+    )
     v = tie(v)
     *v["singles"], v["near"] = join(place, keep, v.pop("taken"))
+    v["rows_taken"], v["cot_taken"] = swap(v.pop("rows_sent")), swap(v.pop("cot_sent"))
+    v["text_taken"] = swap(v["text_pair"])
     v = tie(v)
 
     v["near"] = [v["near"], *sides(v["near"])]
@@ -1774,30 +1788,35 @@
 
     rest = stack(v.pop("line"))
     v["far_self"] = [rest, *sides(rest)]
-    pieces = exchange(v.pop("pieces"))
+    v["two_on"] = shift(v["pieces"][2], 2)
     line_cross = gather_line(v["singles"][1])
     v = tie(v)
     v["far_self"] += corners(v["far_self"][1:], 384)
-    v["pieces"], v["line_cross"] = pieces, line_cross
+    pieces = v.pop("pieces")
+    v["pieces"] = [pieces[0], shift(pieces[1], 1), v.pop("two_on"), shift(pieces[3], 3)]
+    v["line_cross"] = line_cross
     v = tie(v)
     v["rows_own"] = stack([piece[None] for piece in v.pop("pieces")])
     v["rows_other"] = swap(v["rows_own"])
-    v["w_self"], v["norms"] = assemble_first(place, v.pop("near"), v.pop("far_self"))
     line_one = gather_line(v["singles"][2])
     v = tie(v)
 
     v["far_cross"] = sides(v["line_cross"])
-    v["text_pieces"] = exchange(v["text_pieces"])
+    text_pieces, cot_pieces = v.pop("text_pieces"), v.pop("cot_pieces")
+    v["text_near"] = [text_pieces[0], shift(text_pieces[1], 1), shift(text_pieces[3], 3)]
+    v["text_two"], v["cot_two"] = text_pieces[2], shift(cot_pieces[2], 2)
+    v["cot_near"] = [cot_pieces[0], cot_pieces[1], cot_pieces[3]]
     v["line_one"] = line_one
-    v["normed_one"], v["qkv"], v["self_mix"], v["self_lse"], v["mine"] = fused_self_forward(
-        place, v["rows_own"], v["rows_other"], v["norms"], v["w_self"]
+    v["w_self"], v["norms"], v["normed_one"], v["qkv"], v["self_mix"], v["self_lse"], v["mine"] = (
+        fused_self_forward(place, v["rows_own"], v["rows_other"], v.pop("near"), v.pop("far_self"))
     )
     v = tie(v)
 
     v["theirs"] = swap(v["mine"])
     v["far_cross"] += corners(v["far_cross"], 2)
     line_two = gather_line(v.pop("singles")[3])
-    text_pieces = v.pop("text_pieces")
+    text_near, text_two = v.pop("text_near"), shift(v.pop("text_two"), 2)
+    text_pieces = [text_near[0], text_near[1], text_two, text_near[2]]
     v["text"] = arrange(place, text_pieces)
     ids = text_pieces[0][32, :128].astype(jnp.int32)
     v["caption"] = jnp.repeat(ids, 8)[None, :]
@@ -1805,28 +1824,29 @@
     v = tie(v)
 
     v["far_one"] = sides(v["line_one"])
+    near, one_on, three_on = v.pop("cot_near")
+    cot_pieces = [near, shift(one_on, 1), v.pop("cot_two"), shift(three_on, 3)]
     v["line_two"] = line_two
-    v["cot_pieces"] = exchange(v["cot_pieces"])
-    v["w_cross"] = assemble(place, v.pop("line_cross"), v.pop("far_cross"))
-    v["after_attn"], v["normed_two"], v["queries"], v["keys"], v["cross_mix"], v["cross_lse"], v["mine"] = (
+    v["w_cross"], v["after_attn"], v["normed_two"], v["queries"], v["keys"], v["cross_mix"], v["cross_lse"], v["mine"] = (
         fused_cross_forward(
             place, v["rows_own"], v.pop("rows_other"), v["mine"], v["theirs"], v["norms"], v["text"], v["ids"],
-            v["caption"], v["w_cross"],
+            v["caption"], (v.pop("line_cross"), *v.pop("far_cross")),
         )
     )
+    v["cot_own"] = join_pieces(place, cot_pieces)
     v = tie(v)
 
     v["theirs"] = swap(v["mine"])
-    v["far_one"] += corners(v["far_one"], 2)
-    v["cot_own"] = stack([piece[None] for piece in v.pop("cot_pieces")])
+    low, high, line_two = tie((v["far_one"][0][:2], v["far_one"][1][2:], v.pop("line_two")))
+    v["far_one"] += [across(low, 2), across(high, 1)]
     v["cot_other"] = swap(v["cot_own"])
-    w_two = lax.all_gather(v.pop("line_two"), "chip")
+    w_two = lax.all_gather(line_two, "chip")
     v = tie(v)
 
     v["w_two"] = w_two
-    w_one = assemble(place, v.pop("line_one"), v.pop("far_one"))
+    pieces = (v.pop("line_one"), *v.pop("far_one"))
     v["grads_one"], v["after_cross"], v["normed_three"], v["cot"], v["out_sum"], v["back_sum"] = feed_first(
-        place, v["after_attn"], v["mine"], v["theirs"], v["norms"], v.pop("cot_own"), v.pop("cot_other"), w_one
+        place, v["after_attn"], v["mine"], v["theirs"], v["norms"], v.pop("cot_own"), v.pop("cot_other"), pieces
     )
     v = tie(v)
 
@@ -1863,8 +1883,8 @@
     )
     v = tie(v)
 
-    v["sides_three"] = grad_sides(v["grads_three"], v.pop("got_three"))
-    total_two = plane_sum_whole(v.pop("grads_two")[0], *v.pop("sides_two"))
+    v["sides_three"], sides_two = grad_sides(v["grads_three"], v.pop("got_three"), v.pop("sides_two"))
+    total_two = plane_sum_whole(v.pop("grads_two")[0], *sides_two)
     line_two = lax.psum_scatter(total_two, "hi", scatter_dimension=0, tiled=True)
     v["grads_four"] = self_grads(place, v.pop("normed_one"), v.pop("low_grad"), v["dqkv"], v.pop("self_mix"))
     mine, sent = part_images(place, v.pop("pieces"))
@@ -1879,7 +1899,7 @@
     v["kept"], v["sent"] = self_back(place, dqkv, v.pop("w_self"))
     v = tie(v)
 
-    v["sides_four"] = grad_sides(v["grads_four"], v.pop("got_four"))
+    v["sides_four"], _ = grad_sides(v["grads_four"], v.pop("got_four"), place)
     pieces = last_norm(
         place, v.pop("rows_own"), v.pop("grad_own"), v.pop("kept"), swap(v.pop("sent")), v.pop("norms"),
         v.pop("text_part"), v.pop("norms_two"), v.pop("norms_three"),

time: 508 us -> 496 us (0.976)
  waiting for transfers between devices: 146 us -> 132 us
    ppermute x30, waiting for transfers between devices: 66.1 us -> 51.1 us  [across(): return lax.ppermute(value, 'chip', [(i, i ^ bit) for i in range(4)])]
    pallas_call x36 -> x34, Pallas kernels: 239 us -> 237 us  [call(): pl.pallas_call(body, in_specs=ins, out_specs=out_specs, out_shape=out_sha...]
    unnamed x120 -> x122, local copies, waits for them, and re-layouts: 13.5 us -> 13.7 us
  transfers between devices with their start and end apart: 77 -> 77, of which waited for: 28 -> 28; matrix products, arithmetic and copies ran while one was open for 2% -> 2% of each run, Pallas kernels for 44% -> 45%
where the time goes in v3:
time: 496 us; the launch traced here: 487 us
  Pallas kernels  237 us (48%)
  waiting for transfers between devices  132 us (27%)
  starting transfers between devices  74.5 us (15%)
  local copies, waits for them, and re-layouts  26.4 us (5%)
  between operations  15.3 us (3%)
    pallas_call x34, Pallas kernels, call(): pl.pallas_call(body, in_specs=ins, out_specs=out_specs, out_shape=out_sha...  237 us
    ppermute x21, waiting for transfers between devices, shift(): return lax.ppermute(value, 'hi', [((i + step) % 4, i) for i in range(4)])  63.4 us
    ppermute x30, waiting for transfers between devices, across(): return lax.ppermute(value, 'chip', [(i, i ^ bit) for i in range(4)])  51.1 us
    ppermute x21, starting transfers between devices, shift(): return lax.ppermute(value, 'hi', [((i + step) % 4, i) for i in range(4)])  35.2 us
    ppermute x30, starting transfers between devices, across(): return lax.ppermute(value, 'chip', [(i, i ^ bit) for i in range(4)])  23.1 us
    ppermute x18, starting transfers between devices, swap(): return lax.ppermute(value, 'core', [(0, 1), (1, 0)])  15.3 us
    unnamed x122, local copies, waits for them, and re-layouts  13.7 us
  transfers between devices with their start and end apart: 77, of which 28 were waited for; matrix products, arithmetic and copies ran while one was open for 2% of the time, Pallas kernels for 45%

profile of v3, /device:TPU:9, one launch (start us, length us, event | category | flops | bytes accessed | tf_op | source)
XLA Modules:
  0.0 487.2 jit_solution(1836855215699741998)
XLA Ops:
  35.8 7.0 %collective-permute-done.7.refs_1_ = bf16[256,512]{1,0:T(8,128)(2,1)S(1)} collective-permute-done((bf16[256,512]{1,0:T(8,128)(2,1)}, bf16[256,512]{1,0:T(8,128)(2,1)S(1)}, u32[]{:S(2)}, u32[]{:S(2)}) %collective-permute-start.7) | collective-permute-done | bytes 262176 | tf_op jit(solution)/shard_map/ppermute | solution.py:1739
  42.8 5.6 %collective-permute-done.8.refs_2_ = bf16[256,512]{1,0:T(8,128)(2,1)S(1)} collective-permute-done((bf16[256,512]{1,0:T(8,128)(2,1)}, bf16[256,512]{1,0:T(8,128)(2,1)S(1)}, u32[]{:S(2)}, u32[]{:S(2)}) %collective-permute-start.8) | collective-permute-done | bytes 262176 | tf_op jit(solution)/shard_map/ppermute | solution.py:1739
  51.7 6.9 %collective-permute-done.13 = bf16[128,1024]{1,0:T(8,128)(2,1)S(1)} collective-permute-done((bf16[128,1024]{1,0:T(8,128)(2,1)S(1)}, bf16[128,1024]{1,0:T(8,128)(2,1)S(1)}, u32[]{:S(2)}, u32[]{:S(2)}) %collective-permute-start.13) | collective-permute-done | bytes 262176 | tf_op jit(solution)/shard_map/ppermute | solution.py:1739
  58.6 10.5 %collective-permute-done.11.refs_6_ = bf16[768,512]{1,0:T(8,128)(2,1)S(1)} collective-permute-done((bf16[768,512]{1,0:T(8,128)(2,1)}, bf16[768,512]{1,0:T(8,128)(2,1)S(1)}, u32[]{:S(2)}, u32[]{:S(2)}) %collective-permute-start.11) | collective-permute-done | bytes 786464 | tf_op jit(solution)/shard_map/ppermute | solution.py:1736
  71.3 11.2 %collective-permute-start.16 = (bf16[128,1024]{1,0:T(8,128)(2,1)S(1)}, bf16[128,1024]{1,0:T(8,128)(2,1)S(1)}, u32[]{:S(2)}, u32[]{:S(2)}) collective-permute-start(bf16[128,1024]{1,0:T(8,128)(2,1)S(1)} %copy-done.58), channel_id=1, source_target_pairs={{1,0},{2,1},{3,2},{0,3},{5,4},{6,5},{7,6},{4,7},{9,8},{10,9},{11,1... | collective-permute-start | bytes 786440 | tf_op jit(solution)/shard_map/ppermute | solution.py:1739
  82.5 7.2 %collective-permute-done.16 = bf16[128,1024]{1,0:T(8,128)(2,1)S(1)} collective-permute-done((bf16[128,1024]{1,0:T(8,128)(2,1)S(1)}, bf16[128,1024]{1,0:T(8,128)(2,1)S(1)}, u32[]{:S(2)}, u32[]{:S(2)}) %collective-permute-start.16) | collective-permute-done | bytes 262176 | tf_op jit(solution)/shard_map/ppermute | solution.py:1739
  106.0 21.3 %shard_map.347 = (bf16[1024,2048]{1,0:T(8,128)(2,1)}, bf16[16,1024]{1,0:T(8,128)(2,1)}, bf16[1024,1024]{1,0:T(8,128)(2,1)}, bf16[1024,1536]{1,0:T(8,128)(2,1)}, ...) custom-call(s32[4]{0:T(128)} %pad_add_fusion.place.refs_0_, ...), custom_call_target="tpu_custom_call" | custom-call | flops 1 | bytes 1 | tf_op jit(solution)/shard_map/pallas_call | solution.py:717
  127.3 10.8 %collective-permute-done.22.refs_1_ = bf16[48,1024]{1,0:T(8,128)(2,1)} collective-permute-done((bf16[48,1024]{1,0:T(8,128)(2,1)}, bf16[48,1024]{1,0:T(8,128)(2,1)}, u32[]{:S(2)}, u32[]{:S(2)}) %collective-permute-start.22) | collective-permute-done | bytes 98336 | tf_op jit(solution)/shard_map/ppermute | solution.py:1739
  149.3 4.1 collective-permute-done.24.refs_3_
  158.7 17.1 %shard_map.349 = (bf16[1024,2048]{1,0:T(8,128)(2,1)}, f32[1024,1024]{1,0:T(8,128)}, bf16[1024,1024]{1,0:T(8,128)(2,1)}, bf16[1024,512]{1,0:T(8,128)(2,1)}, bf16[...) custom-call(s32[4]{0:T(128)} %pad_add_fusion.place.refs_0_, ...), custom_call_target="tpu_custom_call" | custom-call | flops 1 | bytes 1 | tf_op jit(solution)/shard_map/pallas_call | solution.py:717
  188.9 12.5 %collective-permute-done.33.p_low = bf16[2,256,512]{2,1,0:T(8,128)(2,1)S(1)} collective-permute-done((bf16[2,256,512]{2,1,0:T(8,128)(2,1)}, bf16[2,256,512]{2,1,0:T(8,128)(2,1)S(1)}, u32[]{:S(2)}, u32[]{:S(2)}) %collective-permute-start.33) | collective-permute-done | bytes 524320 | tf_op jit(solution)/shard_map/ppermute | solution.py:1736
  205.6 29.8 %shard_map.351 = (bf16[4,4,256,512]{3,2,1,0:T(8,128)(2,1)}, f32[1024,1024]{1,0:T(8,128)}, bf16[1024,1024]{1,0:T(8,128)(2,1)}, bf16[1024,1024]{1,0:T(8,128)(2,1)}...) custom-call(s32[4]{0:T(128)} %pad_add_fusion.place.refs_0_, f32[1024,1024]{1,0:T(8,128)} %get-tuple-element.971.after.refs_1_, ...), custom_call_target="tpu_custom_call" | custom-call | flops 1 | bytes 1 | tf_op jit(solution)/shard_map/pallas_call | solution.py:717
  235.5 7.8 %all-gather.15.cloned.1.call-done = bf16[16,256,512]{2,1,0:T(8,128)(2,1)} async-done(((bf16[4,256,512]{2,1,0:T(8,128)(2,1)}), bf16[16,256,512]{2,1,0:T(8,128)(2,1)}) %all-gather.15.cloned.1.call-update) | async-done | bytes 4194320 | tf_op jit(solution)/shard_map/all_gather | solution.py:1843
  243.8 24.0 %shard_map.352 = (bf16[256,2048]{1,0:T(8,128)(2,1)}, bf16[256,2048]{1,0:T(8,128)(2,1)}, bf16[256,2048]{1,0:T(8,128)(2,1)}, bf16[128,2048]{1,0:T(8,128)(2,1)}, bf...) custom-call(s32[4]{0:T(128)} %pad_add_fusion.place.refs_0_, ...), custom_call_target="tpu_custom_call" | custom-call | flops 1 | bytes 1 | tf_op jit(solution)/shard_map/pallas_call | solution.py:717
  268.5 5.4 %collective-permute-done.36.theirs = bf16[4,128,1024]{2,1,0:T(8,128)(2,1)S(1)} collective-permute-done((bf16[4,128,1024]{2,1,0:T(8,128)(2,1)}, bf16[4,128,1024]{2,1,0:T(8,128)(2,1)S(1)}, u32[]{:S(2)}, u32[]{:S(2)}) %collective-permute-start.36) | collective-permute-done | bytes 1048608 | tf_op jit(solution)/shard_map/ppermute | solution.py:1733
  283.8 22.9 %shard_map.353 = (f32[1024,1024]{1,0:T(8,128)}, bf16[1024,1024]{1,0:T(8,128)(2,1)}, f32[8,1024]{1,0:T(8,128)}, bf16[128,1024]{1,0:T(8,128)(2,1)}, bf16[256,2048]...) custom-call(s32[4]{0:T(128)} %pad_add_fusion.place.refs_0_, ...), custom_call_target="tpu_custom_call" | custom-call | flops 1 | bytes 1 | tf_op jit(solution)/shard_map/pallas_call | solution.py:717
  315.2 28.5 %shard_map.356 = (f32[4,128,1024]{2,1,0:T(8,128)}, bf16[1024,1024]{1,0:T(8,128)(2,1)}, f32[8,1024]{1,0:T(8,128)}, bf16[1024,1536]{1,0:T(8,128)(2,1)}) custom-call(s32[4]{0:T(128)} %pad_add_fusion.place.refs_0_, f32[1024,1024]{1,0:T(8,128)} %get-tuple-element.971.after.refs_1_, bf16[1024,1024]{1,0:T(8,128)(2,1)} %get-tuple-element.972.refs_2_, ...), custom_call_target="tpu_custom_call" | custom-call | flops 1 | bytes 1 | tf_op jit(solution)/shard_map/pallas_call | solution.py:717
  343.6 5.3 %collective-permute-done.44.from_side = bf16[128,2048]{1,0:T(8,128)(2,1)S(1)} collective-permute-done((bf16[128,2048]{1,0:T(8,128)(2,1)}, bf16[128,2048]{1,0:T(8,128)(2,1)S(1)}, u32[]{:S(2)}, u32[]{:S(2)}) %collective-permute-start.44) | collective-permute-done | bytes 524320 | tf_op jit(solution)/shard_map/ppermute | solution.py:1736
  363.6 12.7 %shard_map.357 = (bf16[256,2048]{1,0:T(8,128)(2,1)}, bf16[256,2048]{1,0:T(8,128)(2,1)}, bf16[256,2048]{1,0:T(8,128)(2,1)}, bf16[128,2048]{1,0:T(8,128)(2,1)}, bf16[128,2048]{1,0:T(8,128)(2,1)}) custom-call(s32[4]{0:T(128)} %pad_add_fusion.place.refs_0_, bf16[1024,1024]{1,0:T(8,128)(2,1)} %get-tuple-element.1004.normed, ...), custom_call_target="tpu_custom_call" | custom-call | flops 1 | bytes 1 | tf_op jit(solution)/shard_map/pallas_call | solution.py:717
  385.7 7.9 %shard_map.363 = (f32[4,128,1024]{2,1,0:T(8,128)}, bf16[4,128,1024]{2,1,0:T(8,128)(2,1)}) custom-call(s32[4]{0:T(128)} %pad_add_fusion.place.refs_0_, bf16[1024,1536]{1,0:T(8,128)(2,1)} %get-tuple-element.1052.dq.dk.dv.dqkv, bf16[1024,2048]{1,0:T(8,128)(2,1)} %get-tuple-element.1053.refs_6_.weights), custom_call_target="tpu_custom_call" | custom-call | flops 1 | bytes 1 | tf_op jit(solution)/shard_map/pallas_call | solution.py:717
  402.0 5.8 %shard_map.368 = (bf16[176,1024]{1,0:T(8,128)(2,1)}, bf16[176,1024]{1,0:T(8,128)(2,1)}, bf16[176,1024]{1,0:T(8,128)(2,1)}, bf16[176,1024]{1,0:T(8,128)(2,1)}) custom-call(s32[4]{0:T(128)} %pad_add_fusion.place.refs_0_, bf16[4,128,1024]{2,1,0:T(8,128)(2,1)} %shard_map.346.own.rows, f32[4,128,1024]{2,1,0:T(8,128)} %get-tuple-element.1091.grad_own, ...), custom_call_target="tpu_custom_call" | custom-call | flops 1 | bytes 1 | tf_op jit(solution)/shard_map/pallas_call | solution.py:717
  411.5 12.9 %collective-permute-done.55.over = bf16[256,2048]{1,0:T(8,128)(2,1)S(1)} collective-permute-done((bf16[256,2048]{1,0:T(8,128)(2,1)}, bf16[256,2048]{1,0:T(8,128)(2,1)S(1)}, u32[]{:S(2)}, u32[]{:S(2)}) %collective-permute-start.55) | collective-permute-done | bytes 1048608 | tf_op jit(solution)/shard_map/ppermute | solution.py:1736
  429.5 4.5 collective-permute-done.60.refs_2_
  434.0 7.7 %collective-permute-done.61.refs_3_ = bf16[176,1024]{1,0:T(8,128)(2,1)S(1)} collective-permute-done((bf16[176,1024]{1,0:T(8,128)(2,1)}, bf16[176,1024]{1,0:T(8,128)(2,1)S(1)}, u32[]{:S(2)}, u32[]{:S(2)}) %collective-permute-start.61) | collective-permute-done | bytes 360480 | tf_op jit(solution)/shard_map/ppermute | solution.py:1739
  (315 shorter events, 182.4 us)
Async XLA Ops:
  7.2 86.3 %all-gather.9.cloned.1.call-start = ((), (), s32[]{:S(2)}) async-start(), calls=%async_computation.7 | async-start | bytes 1310720 | tf_op jit(solution)/shard_map/all_gather | solution.py:1748
  48.4 89.7 %all-gather.11.cloned.1.call-start = ((), (), s32[]{:S(2)}) async-start(), calls=%async_computation.8 | async-start | bytes 1310720 | tf_op jit(solution)/shard_map/all_gather | solution.py:1748
  98.4 82.6 %all-gather.13.cloned.1.call-start = ((), (), s32[]{:S(2)}) async-start(), calls=%async_computation.9 | async-start | bytes 1310720 | tf_op jit(solution)/shard_map/all_gather | solution.py:1748
  100.9 37.2 %collective-permute-start.20 = (bf16[4,256,512]{2,1,0:T(8,128)(2,1)}, bf16[4,256,512]{2,1,0:T(8,128)(2,1)S(1)}, u32[]{:S(2)}, u32[]{:S(2)}) collective-permute-start(bf16[4,256,512]{2,1,0:T(8,128)(2,1)} %bitcast.10.refs_0_), channel_id=1, source_target_pairs={{0,8},{8,0},{16,24},{24,16},{1,9},{9,1},{17,25},{25,17},{2,10},{10... | collective-permute-start | bytes 3145736 | tf_op jit(solution)/shard_map/ppermute | solution.py:1736
  101.5 36.6 %collective-permute-start.21 = (bf16[4,256,512]{2,1,0:T(8,128)(2,1)}, bf16[4,256,512]{2,1,0:T(8,128)(2,1)S(1)}, u32[]{:S(2)}, u32[]{:S(2)}) collective-permute-start(bf16[4,256,512]{2,1,0:T(8,128)(2,1)} %bitcast.10.refs_0_), channel_id=1, source_target_pairs={{0,16},{8,24},{16,0},{24,8},{1,17},{9,25},{17,1},{25,9},{2,18},{10... | collective-permute-start | bytes 3145736 | tf_op jit(solution)/shard_map/ppermute | solution.py:1736
  102.7 35.3 %collective-permute-start.19 = (bf16[128,1024]{1,0:T(8,128)(2,1)}, bf16[128,1024]{1,0:T(8,128)(2,1)}, u32[]{:S(2)}, u32[]{:S(2)}) collective-permute-start(bf16[128,1024]{1,0:T(8,128)(2,1)} %get-tuple-element.706), channel_id=1, source_target_pairs={{2,0},{3,1},{0,2},{1,3},{6,4},{7,5},{4,6},{5,7},{10,8},{11,9},{8,1... | collective-permute-start | bytes 786440 | tf_op jit(solution)/shard_map/ppermute | solution.py:1739
  102.7 35.3 %collective-permute-start.22 = (bf16[48,1024]{1,0:T(8,128)(2,1)}, bf16[48,1024]{1,0:T(8,128)(2,1)}, u32[]{:S(2)}, u32[]{:S(2)}) collective-permute-start(bf16[48,1024]{1,0:T(8,128)(2,1)} %get-tuple-element.728), channel_id=1, source_target_pairs={{1,0},{2,1},{3,2},{0,3},{5,4},{6,5},{7,6},{4,7},{9,8},{10,9},{11,1... | collective-permute-start | bytes 294920 | tf_op jit(solution)/shard_map/ppermute | solution.py:1739
  104.8 33.3 %collective-permute-start.23 = (bf16[48,1024]{1,0:T(8,128)(2,1)}, bf16[48,1024]{1,0:T(8,128)(2,1)}, u32[]{:S(2)}, u32[]{:S(2)}) collective-permute-start(bf16[48,1024]{1,0:T(8,128)(2,1)} %get-tuple-element.729), channel_id=1, source_target_pairs={{3,0},{0,1},{1,2},{2,3},{7,4},{4,5},{5,6},{6,7},{11,8},{8,9},{9,10... | collective-permute-start | bytes 294920 | tf_op jit(solution)/shard_map/ppermute | solution.py:1739
  141.5 101.7 %all-gather.15.cloned.1.call-start = ((), (), s32[]{:S(2)}) async-start(), calls=%async_computation.10 | async-start | bytes 5242880 | tf_op jit(solution)/shard_map/all_gather | solution.py:1843
  153.9 27.0 %collective-permute-start.30 = (bf16[4,256,512]{2,1,0:T(8,128)(2,1)}, bf16[4,256,512]{2,1,0:T(8,128)(2,1)}, u32[]{:S(2)}, u32[]{:S(2)}) collective-permute-start(bf16[4,256,512]{2,1,0:T(8,128)(2,1)} %bitcast.15.p_own), channel_id=1, source_target_pairs={{0,8},{8,0},{16,24},{24,16},{1,9},{9,1},{17,25},{25,17},{2,10},{10... | collective-permute-start | bytes 3145736 | tf_op jit(solution)/shard_map/ppermute | solution.py:1736
  154.9 26.1 %collective-permute-start.31 = (bf16[4,256,512]{2,1,0:T(8,128)(2,1)}, bf16[4,256,512]{2,1,0:T(8,128)(2,1)}, u32[]{:S(2)}, u32[]{:S(2)}) collective-permute-start(bf16[4,256,512]{2,1,0:T(8,128)(2,1)} %bitcast.15.p_own), channel_id=1, source_target_pairs={{0,16},{8,24},{16,0},{24,8},{1,17},{9,25},{17,1},{25,9},{2,18},{10... | collective-permute-start | bytes 3145736 | tf_op jit(solution)/shard_map/ppermute | solution.py:1736
  184.9 127.2 %reduce-scatter.13.cloned.1.call-start = ((), (), s32[]{:S(2)}) async-start(), calls=%async_computation.11 | async-start | bytes 5242880
  243.3 106.4 %reduce-scatter.7.cloned.1.call-start = ((), (), s32[]{:S(2)}) async-start(), calls=%async_computation.4 | async-start | bytes 1310720 | tf_op jit(solution)/shard_map/reduce_scatter | solution.py:1879
  274.0 32.8 %collective-permute-start.38 = (bf16[128,2048]{1,0:T(8,128)(2,1)}, bf16[128,2048]{1,0:T(8,128)(2,1)}, u32[]{:S(2)}, u32[]{:S(2)}) collective-permute-start(bf16[128,2048]{1,0:T(8,128)(2,1)} %get-tuple-element.902), channel_id=1, source_target_pairs={{0,8},{8,0},{16,24},{24,16},{1,9},{9,1},{17,25},{25,17},{2,10},{10... | collective-permute-start | bytes 1572872 | tf_op jit(solution)/shard_map/ppermute | solution.py:1736
  275.2 31.7 %collective-permute-start.39 = (bf16[128,2048]{1,0:T(8,128)(2,1)}, bf16[128,2048]{1,0:T(8,128)(2,1)}, u32[]{:S(2)}, u32[]{:S(2)}) collective-permute-start(bf16[128,2048]{1,0:T(8,128)(2,1)} %get-tuple-element.903), channel_id=1, source_target_pairs={{0,16},{8,24},{16,0},{24,8},{1,17},{9,25},{17,1},{25,9},{2,18},{10... | collective-permute-start | bytes 1572872 | tf_op jit(solution)/shard_map/ppermute | solution.py:1736
  278.4 28.3 %collective-permute-start.40 = (bf16[128,1024]{1,0:T(8,128)(2,1)}, bf16[128,1024]{1,0:T(8,128)(2,1)S(1)}, u32[]{:S(2)}, u32[]{:S(2)}) collective-permute-start(bf16[128,1024]{1,0:T(8,128)(2,1)} %get-tuple-element.933), channel_id=1, source_target_pairs={{1,0},{2,1},{3,2},{0,3},{5,4},{6,5},{7,6},{4,7},{9,8},{10,9},{11,1... | collective-permute-start | bytes 786440 | tf_op jit(solution)/shard_map/ppermute | solution.py:1739
  312.1 81.5 %reduce-scatter.11.cloned.1.call-start = ((), (), s32[]{:S(2)}) async-start(), calls=%async_computation.6 | async-start | bytes 1310720 | tf_op jit(solution)/shard_map/reduce_scatter | solution.py:1888
  312.2 36.8 %collective-permute-start.46 = (bf16[256,2048]{1,0:T(8,128)(2,1)}, bf16[256,2048]{1,0:T(8,128)(2,1)S(1)}, u32[]{:S(2)}, u32[]{:S(2)}) collective-permute-start(bf16[256,2048]{1,0:T(8,128)(2,1)} %get-tuple-element.998), channel_id=1, source_target_pairs={{0,16},{8,24},{16,0},{24,8},{1,17},{9,25},{17,1},{25,9},{2,18},{10... | collective-permute-start | bytes 3145736 | tf_op jit(solution)/shard_map/ppermute | solution.py:1736
  313.4 36.3 %collective-permute-start.47 = (bf16[256,2048]{1,0:T(8,128)(2,1)}, bf16[256,2048]{1,0:T(8,128)(2,1)}, u32[]{:S(2)}, u32[]{:S(2)}) collective-permute-start(bf16[256,2048]{1,0:T(8,128)(2,1)} %get-tuple-element.999), channel_id=1, source_target_pairs={{0,8},{8,0},{16,24},{24,16},{1,9},{9,1},{17,25},{25,17},{2,10},{10... | collective-permute-start | bytes 3145736 | tf_op jit(solution)/shard_map/ppermute | solution.py:1736
  314.3 34.7 %collective-permute-start.44 = (bf16[128,2048]{1,0:T(8,128)(2,1)}, bf16[128,2048]{1,0:T(8,128)(2,1)S(1)}, u32[]{:S(2)}, u32[]{:S(2)}) collective-permute-start(bf16[128,2048]{1,0:T(8,128)(2,1)} %get-tuple-element.981), channel_id=1, source_target_pairs={{0,8},{8,0},{16,24},{24,16},{1,9},{9,1},{17,25},{25,17},{2,10},{10... | collective-permute-start | bytes 1572872 | tf_op jit(solution)/shard_map/ppermute | solution.py:1736
  314.9 34.1 %collective-permute-start.45 = (bf16[128,2048]{1,0:T(8,128)(2,1)}, bf16[128,2048]{1,0:T(8,128)(2,1)}, u32[]{:S(2)}, u32[]{:S(2)}) collective-permute-start(bf16[128,2048]{1,0:T(8,128)(2,1)} %get-tuple-element.982), channel_id=1, source_target_pairs={{0,16},{8,24},{16,0},{24,8},{1,17},{9,25},{17,1},{25,9},{2,18},{10... | collective-permute-start | bytes 1572872 | tf_op jit(solution)/shard_map/ppermute | solution.py:1736
  356.7 93.3 %reduce-scatter.9.cloned.1.call-start = ((), (), s32[]{:S(2)}) async-start(), calls=%async_computation.5 | async-start | bytes 1310720 | tf_op jit(solution)/shard_map/reduce_scatter | solution.py:1897
  407.9 26.1 %collective-permute-start.60 = (bf16[176,1024]{1,0:T(8,128)(2,1)}, bf16[176,1024]{1,0:T(8,128)(2,1)S(1)}, u32[]{:S(2)}, u32[]{:S(2)}) collective-permute-start(bf16[176,1024]{1,0:T(8,128)(2,1)} %get-tuple-element.1100), channel_id=1, source_target_pairs={{2,0},{3,1},{0,2},{1,3},{6,4},{7,5},{4,6},{5,7},{10,8},{11,9},{8,1... | collective-permute-start | bytes 1081352 | tf_op jit(solution)/shard_map/ppermute | solution.py:1739
  410.1 31.6 %collective-permute-start.61 = (bf16[176,1024]{1,0:T(8,128)(2,1)}, bf16[176,1024]{1,0:T(8,128)(2,1)S(1)}, u32[]{:S(2)}, u32[]{:S(2)}) collective-permute-start(bf16[176,1024]{1,0:T(8,128)(2,1)} %get-tuple-element.1101), channel_id=1, source_target_pairs={{3,0},{0,1},{1,2},{2,3},{7,4},{4,5},{5,6},{6,7},{11,8},{8,9},{9,10... | collective-permute-start | bytes 1081352 | tf_op jit(solution)/shard_map/ppermute | solution.py:1739
  (114 other events, 1260.1 us)
Sparse Core Ops, SparseCore 0:
  48.5 34.2 all-gather.8
  98.5 37.4 all-gather.10
  141.7 36.7 all-gather.12
  185.0 58.2 all-gather.14
  246.1 55.8 reduce-scatter.12
  312.2 24.0 reduce-scatter.6
  356.8 25.0 reduce-scatter.10
  385.8 26.1 reduce-scatter.8

commit v4 on v3

--- a/solution.py
+++ b/solution.py
@@ -641,7 +641,7 @@
 HBM = pl.BlockSpec(memory_space=pltpu.HBM)
 SMEM = pl.BlockSpec(memory_space=pltpu.SMEM)
 VMEM = pl.BlockSpec(memory_space=pltpu.VMEM)
-LATE = object()
+LATE, ROWS = object(), object()
 MIB = 1024 * 1024
 
 
@@ -650,15 +650,34 @@
 
 
 class Late:
-    def __init__(self, source, target, sem):
-        self.ref, self.copy = target, pltpu.make_async_copy(source, target, sem)
-        self.copy.start()
+    def __init__(self, source, target, sems, chunks=1):
+        self.ref, self.rows, self.waited = target, target.shape[0] // chunks, [False] * chunks
+        self.copies = []
+        for i in range(chunks):
+            part = slice(i * self.rows, (i + 1) * self.rows)
+            self.copies.append(pltpu.make_async_copy(source.at[part], target.at[part], sems.at[i]))
+
+    def start(self, chunk):
+        self.copies[chunk].start()
+
+    def need(self, row):
+        chunk = row // self.rows
+        if not self.waited[chunk]:
+            self.copies[chunk].wait()
+            self.waited[chunk] = True
+        return self.ref
 
     def ready(self):
-        if self.copy is not None:
-            self.copy.wait()
-            self.copy = None
+        for chunk in range(len(self.copies)):
+            self.need(chunk * self.rows)
         return self.ref
+
+
+def start_chunks(loads):
+    for chunk in range(max((len(load.copies) for load in loads), default=0)):
+        for load in loads:
+            if chunk < len(load.copies):
+                load.start(chunk)
 
 
 class Early:
@@ -671,7 +690,7 @@
 
 
 def call_overlapped(body, outs, ins, operands, scratch=(), limit=60):
-    late_ins = [i for i, spec in enumerate(ins) if spec is LATE]
+    late_ins = [i for i, spec in enumerate(ins) if spec in (LATE, ROWS)]
     late_outs = [i for i, (spec, _) in enumerate(outs) if spec is LATE]
     buffers = [pltpu.VMEM(operands[i].shape, operands[i].dtype) for i in late_ins]
     buffers += [pltpu.VMEM(outs[i][1].shape, outs[i][1].dtype) for i in late_outs]
@@ -679,16 +698,21 @@
 
     def wrapped(*refs):
         refs = list(refs)
-        sems = refs.pop()
+        sems, load_sems = refs.pop(), refs.pop()
         extra = refs[len(refs) - count :]
         refs = refs[: len(refs) - count]
-        loads = [Late(refs[i], extra[n], sems.at[n]) for n, i in enumerate(late_ins)]
+        loads = [
+            Late(refs[i], extra[n], load_sems.at[n], 4 if ins[i] is ROWS else 1)
+            for n, i in enumerate(late_ins)
+        ]
+        start_chunks([load for load in loads if len(load.copies) > 1])
+        start_chunks([load for load in loads if len(load.copies) == 1])
         for load, i in zip(loads, late_ins):
             refs[i] = load
         stores = []
         for n, i in enumerate(late_outs):
             place = len(ins) + i
-            stores.append(Early(extra[len(late_ins) + n], refs[place], sems.at[len(late_ins) + n]))
+            stores.append(Early(extra[len(late_ins) + n], refs[place], sems.at[n]))
             refs[place] = stores[-1]
         body(*refs)
         for load in loads:
@@ -702,9 +726,14 @@
     return call(
         wrapped,
         [(HBM if spec is LATE else spec, shape) for spec, shape in outs],
-        [ANY if spec is LATE else spec for spec in ins],
+        [ANY if spec in (LATE, ROWS) else spec for spec in ins],
         operands,
-        [*scratch, *buffers, pltpu.SemaphoreType.DMA((max(count, 1),))],
+        [
+            *scratch,
+            *buffers,
+            pltpu.SemaphoreType.DMA((max(len(late_ins), 1), 4)),
+            pltpu.SemaphoreType.DMA((max(len(late_outs), 1),)),
+        ],
         limit,
     )
 
@@ -930,14 +959,15 @@
     return weights, rows
 
 
-def later_pieces(place, own, side, over, low, high, buffer):
+def later_pieces(place, pieces, buffer):
+    groups = (pieces[:1], pieces[1:-3], pieces[-3:-2], pieces[-2:])
     chip = place[0]
     weights = []
-    for source in range(4):
+    for source, parts in enumerate(groups):
         for top in range(4):
-            piece = (own, side, over, low if top < 2 else high)[source]
+            part, each = parts[top * len(parts) // 4], 4 // len(parts)
             rows, columns = at((chip ^ source) * 256, 256), slice(top * 512, (top + 1) * 512)
-            weights.append((piece.at[top % 2 if source == 3 else top], buffer.at[rows, columns]))
+            weights.append((part.at[top % each], buffer.at[rows, columns]))
     return weights
 
 
@@ -1067,17 +1097,27 @@
 
 
 def cross_fwd_kernel(
-    place, own, other, mine, theirs, norms, text, ids, caption, *refs
+    place, own, other, mine_in, theirs_in, norms, text, ids, caption, *refs
 ):
     pieces = refs[:5]
-    whole, after, normed, queries, keys, mix, lse, part, weights, loads, store = refs[5:]
-    copies = started(later_pieces(place, *pieces, weights), loads)
+    whole, after, normed, queries, keys, mix, lse, part, weights, mine, theirs, loads, store, row_sems = refs[5:]
+    late = [
+        Late(source, target, row_sems.at[i], 4)
+        for i, (source, target) in enumerate(((mine_in, mine), (theirs_in, theirs)))
+    ]
+    start_chunks(late)
+    copies = started(later_pieces(place, pieces, weights), loads)
     gain, bias = norm_row(norms, 2), norm_row(norms, 3)
-    for row, half, number in image_blocks(place, own, other):
-        rows = at(row, 128)
-        values = half[number].astype(F32) + (mine[rows, :].astype(F32) + theirs[rows, :].astype(F32))
-        after[rows, :] = values
-        normed[rows, :] = normalized(values, gain, bias)
+    core, top = place[1], place[2]
+    for block in range(4):
+        for load in late:
+            load.need(block * 256)
+        for half, which in ((own, core), (other, 1 - core)):
+            rows = at(block * 256 + which * 128, 128)
+            values = half[(block + 4 - top) % 4].astype(F32)
+            values = values + (mine[rows, :].astype(F32) + theirs[rows, :].astype(F32))
+            after[rows, :] = values
+            normed[rows, :] = normalized(values, gain, bias)
     wait_all(copies)
     (stored,) = started([(weights, whole)], store)
     project_into(queries, normed[...], columns_of(weights, 0))
@@ -1112,9 +1152,11 @@
             (VMEM, like(4, 2, 1024, dtype=F32)),
             (VMEM, like(1024, 1024)),
         ],
-        [SMEM] + [VMEM] * 8 + [ANY] * 5,
+        [SMEM, VMEM, VMEM, ANY, ANY] + [VMEM] * 4 + [ANY] * 5,
         (place, own, other, mine, theirs, norms, text, ids, caption, *pieces),
-        [pltpu.VMEM((1024, 2048), BF), pltpu.SemaphoreType.DMA((16,)), pltpu.SemaphoreType.DMA((1,))],
+        [pltpu.VMEM((1024, 2048), BF)]
+        + [pltpu.VMEM((1024, 1024), BF)] * 2
+        + [pltpu.SemaphoreType.DMA((16,)), pltpu.SemaphoreType.DMA((1,)), pltpu.SemaphoreType.DMA((2, 4))],
     )
 
 
@@ -1152,19 +1194,25 @@
 
 
 def feed_first_kernel(
-    place, after, mine, theirs, norms, cot_own, cot_other, p_own, p_side, p_over, p_low, p_high,
-    g_whole, after_out, normed_out, cot_out, out_sum, back, after_cross, normed, cot, back_sum, rows_t, cot_t, grads,
-    weights, sems, loads,
+    place, after_in, mine_in, theirs_in, norms, cot_own, cot_other, *refs
 ):
+    pieces = refs[:6]
+    g_whole, after_out, normed_out, cot_out, out_sum, back = refs[6:12]
+    after_cross, normed, cot, back_sum, rows_t, cot_t, grads, weights, after, mine, theirs, sems, loads, row_sems = refs[12:]
     step = pl.program_id(0)
     pairs = ((after_cross, after_out), (normed, normed_out), (cot, cot_out))
     stores = [pltpu.make_async_copy(a, b, sems.at[i]) for i, (a, b) in enumerate(pairs)]
 
     @pl.when(step == 0)
     def _():
-        copies = started(later_pieces(place, p_own, p_side, p_over, p_low, p_high, weights), loads)
+        arrays = ((after_in, after), (mine_in, mine), (theirs_in, theirs))
+        late = [Late(source, target, row_sems.at[i], 4) for i, (source, target) in enumerate(arrays)]
+        start_chunks(late)
+        copies = started(later_pieces(place, pieces, weights), loads)
         gain, bias = norm_row(norms, 4), norm_row(norms, 5)
         for low in range(0, 1024, 128):
+            for load in late:
+                load.need(low)
             rows = slice(low, low + 128)
             values = after[rows, :] + (mine[rows, :].astype(F32) + theirs[rows, :].astype(F32))
             after_cross[rows, :] = values
@@ -1245,15 +1293,16 @@
             (square, like(1024, 1024, dtype=F32)),
             (square, like(1024, 1024)),
         ],
-        [SMEM, square, square, square, once(16, 1024), once(4, 128, 1024), once(4, 128, 1024)]
-        + [ANY] * 5,
+        [SMEM, ANY, ANY, ANY, once(16, 1024), once(4, 128, 1024), once(4, 128, 1024)]
+        + [ANY] * 6,
         (place, after, mine, theirs, norms, cot_own, cot_other, *pieces),
         [pltpu.VMEM((1024, 1024), F32)]
         + [pltpu.VMEM((1024, 1024), BF)] * 2
         + [pltpu.VMEM((1024, 1024), F32)]
         + [pltpu.VMEM((1024, 1024), BF)] * 2
         + [pltpu.VMEM((1024, 1024), F32), pltpu.VMEM((1024, 2048), BF)]
-        + [pltpu.SemaphoreType.DMA((3,)), pltpu.SemaphoreType.DMA((16,))],
+        + [pltpu.VMEM((1024, 1024), F32), pltpu.VMEM((1024, 1024), BF), pltpu.VMEM((1024, 1024), BF)]
+        + [pltpu.SemaphoreType.DMA((3,)), pltpu.SemaphoreType.DMA((16,)), pltpu.SemaphoreType.DMA((3, 4))],
         limit=60,
         grid=(2,),
         flops=FEED_FLOPS,
@@ -1299,7 +1348,7 @@
     gain_sum, bias_sum = jnp.zeros((8, 1024), F32), jnp.zeros((8, 1024), F32)
     for low in range(0, 1024, 128):
         rows = slice(low, low + 128)
-        grad = mine[rows, :].astype(F32) + theirs[rows, :].astype(F32)
+        grad = mine.need(low)[rows, :].astype(F32) + theirs.need(low)[rows, :].astype(F32)
         back, term = norm_backward(values_of(rows), gain, grad)
         keep(rows, base_of(rows) + back)
         gain_sum = gain_sum + jnp.sum(term.reshape(16, 8, 1024), 0)
@@ -1335,7 +1384,7 @@
         grad_cross[rows, :] = value
         low_grad[rows, :] = value.astype(BF)
 
-    norm_block(lambda rows: after[rows, :], mine, theirs, lambda rows: cot[rows, :].astype(F32), (gain, 4), norms, keep)
+    norm_block(lambda rows: after.need(rows.start)[rows, :], mine, theirs, lambda rows: cot.need(rows.start)[rows, :].astype(F32), (gain, 4), norms, keep)
     grad_out.send()
     weights, queries, keys, mix = weights.ready(), queries.ready(), keys.ready(), mix.ready()
     project_into(mix_grad, low_grad[...], columns_of(weights, 3))
@@ -1385,7 +1434,7 @@
             (VMEM, like(128, 1024)),
         ]
         + [(VMEM, like(*shape)) for shape in GRAD_SHAPES],
-        [SMEM] + [VMEM] * 5 + [LATE, LATE, VMEM, LATE, LATE, LATE, VMEM, VMEM, VMEM],
+        [SMEM] + [ROWS] * 4 + [VMEM] + [LATE, LATE, VMEM, LATE, LATE, LATE, VMEM, VMEM, VMEM],
         (place, after, mine, theirs, cot, gain, weights, normed, text, queries, keys, mix, lse, ids, caption),
         [
             pltpu.VMEM((1024, 1024), BF),
@@ -1411,7 +1460,7 @@
         def _():
             grad_own[rows.start // 256] = value
 
-    norm_block(lambda rows: after[rows, :], mine, theirs, lambda rows: base[rows, :], (gain, 2), norms, keep)
+    norm_block(lambda rows: after.need(rows.start)[rows, :], mine, theirs, lambda rows: base.need(rows.start)[rows, :], (gain, 2), norms, keep)
     grad_out.send()
     low_out.send()
     weights, qkv, mix = weights.ready(), qkv.ready(), mix.ready()
@@ -1457,7 +1506,7 @@
             (VMEM, like(8, 1024, dtype=F32)),
             (VMEM, like(1024, 1536)),
         ],
-        [SMEM] + [VMEM] * 5 + [LATE] * 3 + [VMEM],
+        [SMEM] + [ROWS] * 4 + [VMEM] + [LATE] * 3 + [VMEM],
         (place, after, mine, theirs, base, gain, weights, qkv, mix, lse),
         [pltpu.VMEM((1024, 512), BF), pltpu.VMEM((1024, 128), F32), pltpu.VMEM((1024, 128), F32)],
     )
@@ -1821,12 +1870,13 @@
     ids = text_pieces[0][32, :128].astype(jnp.int32)
     v["caption"] = jnp.repeat(ids, 8)[None, :]
     v["ids"] = ids[:, None]
+    v["one_low"], v["one_high"] = v["line_one"][:2], v["line_one"][2:]
     v = tie(v)
 
-    v["far_one"] = sides(v["line_one"])
+    low, high = v.pop("one_low"), v.pop("one_high")
+    v["far_one"] = [across(low, 1), across(high, 1), across(v["line_one"], 2)]
     near, one_on, three_on = v.pop("cot_near")
     cot_pieces = [near, shift(one_on, 1), v.pop("cot_two"), shift(three_on, 3)]
-    v["line_two"] = line_two
     v["w_cross"], v["after_attn"], v["normed_two"], v["queries"], v["keys"], v["cross_mix"], v["cross_lse"], v["mine"] = (
         fused_cross_forward(
             place, v["rows_own"], v.pop("rows_other"), v["mine"], v["theirs"], v["norms"], v["text"], v["ids"],
@@ -1834,13 +1884,13 @@
         )
     )
     v["cot_own"] = join_pieces(place, cot_pieces)
+    v["line_two"] = line_two
     v = tie(v)
 
     v["theirs"] = swap(v["mine"])
-    low, high, line_two = tie((v["far_one"][0][:2], v["far_one"][1][2:], v.pop("line_two")))
-    v["far_one"] += [across(low, 2), across(high, 1)]
+    v["far_one"] += [across(v["far_one"][0], 2), across(v["far_one"][2][2:], 1)]
+    w_two = lax.all_gather(v.pop("line_two"), "chip")
     v["cot_other"] = swap(v["cot_own"])
-    w_two = lax.all_gather(line_two, "chip")
     v = tie(v)
 
     v["w_two"] = w_two
@@ -1856,9 +1906,9 @@
     )
     v = tie(v)
 
-    v["theirs"] = swap(v["mine"])
     v["out_theirs"] = swap(v.pop("out_sent"))
     v = tie(v)
+    v["theirs"] = swap(v["mine"])
     v["got_two"] = grad_corners(v["grads_two"])
     v["pieces"] = exchange(finish(place, v.pop("out_keep"), v.pop("out_theirs")))
     v["grad_cross"], v["part"], v["norms_three"], v["text_part"], *v["grads_three"] = fused_cross_backward(
@@ -1870,10 +1920,8 @@
 
     v["theirs"] = swap(v["part"])
     v["total_one"] = total_one
-    v["to_two"] = relay(v["grads_two"][2], v["grads_two"][1], *v.pop("got_two"))
-    v = tie(v)
-
-    to_two = v.pop("to_two")
+    to_two = relay(v["grads_two"][2], v["grads_two"][1], *v.pop("got_two"))
+
     v["sides_two"] = [across(to_two[0], 2), across(to_two[1], 1)]
     v["got_three"] = grad_corners(v["grads_three"])
     v["line_one"] = lax.psum_scatter(v.pop("total_one"), "hi", scatter_dimension=0, tiled=False)

time: 496 us -> 490 us (0.988)
  Pallas kernels: 237 us -> 232 us
    pallas_call x34, Pallas kernels: 237 us -> 232 us  [call(): pl.pallas_call(body, in_specs=ins, out_specs=out_specs, out_shape=out_sha...]
    ppermute x30 -> x31, starting transfers between devices: 23.1 us -> 24 us  [across(): return lax.ppermute(value, 'chip', [(i, i ^ bit) for i in range(4)])]
    ppermute x30 -> x31, waiting for transfers between devices: 51.1 us -> 51.8 us  [across(): return lax.ppermute(value, 'chip', [(i, i ^ bit) for i in range(4)])]
    unnamed x122 -> x120, local copies, waits for them, and re-layouts: 13.7 us -> 13.9 us
  transfers between devices with their start and end apart: 77 -> 78, of which waited for: 28 -> 27; matrix products, arithmetic and copies ran while one was open for 2% -> 2% of each run, Pallas kernels for 45% -> 45%
where the time goes in v4:
time: 490 us; the launch traced here: 481 us
  Pallas kernels  232 us (47%)
  waiting for transfers between devices  132 us (27%)
  starting transfers between devices  75.3 us (15%)
  local copies, waits for them, and re-layouts  23.8 us (5%)
  between operations  15.3 us (3%)
    pallas_call x34, Pallas kernels, call(): pl.pallas_call(body, in_specs=ins, out_specs=out_specs, out_shape=out_sha...  232 us
    ppermute x21, waiting for transfers between devices, shift(): return lax.ppermute(value, 'hi', [((i + step) % 4, i) for i in range(4)])  62.1 us
    ppermute x31, waiting for transfers between devices, across(): return lax.ppermute(value, 'chip', [(i, i ^ bit) for i in range(4)])  51.8 us
    ppermute x21, starting transfers between devices, shift(): return lax.ppermute(value, 'hi', [((i + step) % 4, i) for i in range(4)])  34.1 us
    ppermute x31, starting transfers between devices, across(): return lax.ppermute(value, 'chip', [(i, i ^ bit) for i in range(4)])  24 us
    ppermute x18, starting transfers between devices, swap(): return lax.ppermute(value, 'core', [(0, 1), (1, 0)])  16 us
    unnamed x120, local copies, waits for them, and re-layouts  13.9 us
    all_gather x1, waiting for transfers between devices, packed_layer(): w_two = lax.all_gather(v.pop('line_two'), 'chip')  12.3 us
  transfers between devices with their start and end apart: 78, of which 27 were waited for; matrix products, arithmetic and copies ran while one was open for 2% of the time, Pallas kernels for 45%

profile of v4, /device:TPU:9, one launch (start us, length us, event | category | flops | bytes accessed | tf_op | source)
XLA Modules:
  0.0 480.7 jit_solution(11342413125085708511)
XLA Ops:
  35.7 7.0 %collective-permute-done.7.refs_1_ = bf16[256,512]{1,0:T(8,128)(2,1)S(1)} collective-permute-done((bf16[256,512]{1,0:T(8,128)(2,1)}, bf16[256,512]{1,0:T(8,128)(2,1)S(1)}, u32[]{:S(2)}, u32[]{:S(2)}) %collective-permute-start.7) | collective-permute-done | bytes 262176 | tf_op jit(solution)/shard_map/ppermute | solution.py:1788
  42.7 5.6 %collective-permute-done.8.refs_2_ = bf16[256,512]{1,0:T(8,128)(2,1)S(1)} collective-permute-done((bf16[256,512]{1,0:T(8,128)(2,1)}, bf16[256,512]{1,0:T(8,128)(2,1)S(1)}, u32[]{:S(2)}, u32[]{:S(2)}) %collective-permute-start.8) | collective-permute-done | bytes 262176 | tf_op jit(solution)/shard_map/ppermute | solution.py:1788
  51.6 6.9 %collective-permute-done.13 = bf16[128,1024]{1,0:T(8,128)(2,1)S(1)} collective-permute-done((bf16[128,1024]{1,0:T(8,128)(2,1)S(1)}, bf16[128,1024]{1,0:T(8,128)(2,1)S(1)}, u32[]{:S(2)}, u32[]{:S(2)}) %collective-permute-start.13) | collective-permute-done | bytes 262176 | tf_op jit(solution)/shard_map/ppermute | solution.py:1788
  58.5 10.5 %collective-permute-done.11.refs_6_ = bf16[768,512]{1,0:T(8,128)(2,1)S(1)} collective-permute-done((bf16[768,512]{1,0:T(8,128)(2,1)}, bf16[768,512]{1,0:T(8,128)(2,1)S(1)}, u32[]{:S(2)}, u32[]{:S(2)}) %collective-permute-start.11) | collective-permute-done | bytes 786464 | tf_op jit(solution)/shard_map/ppermute | solution.py:1785
  71.2 11.1 %collective-permute-start.16 = (bf16[128,1024]{1,0:T(8,128)(2,1)S(1)}, bf16[128,1024]{1,0:T(8,128)(2,1)S(1)}, u32[]{:S(2)}, u32[]{:S(2)}) collective-permute-start(bf16[128,1024]{1,0:T(8,128)(2,1)S(1)} %copy-done.58), channel_id=1, source_target_pairs={{1,0},{2,1},{3,2},{0,3},{5,4},{6,5},{7,6},{4,7},{9,8},{10,9},{11,1... | collective-permute-start | bytes 786440 | tf_op jit(solution)/shard_map/ppermute | solution.py:1788
  82.4 7.3 %collective-permute-done.16 = bf16[128,1024]{1,0:T(8,128)(2,1)S(1)} collective-permute-done((bf16[128,1024]{1,0:T(8,128)(2,1)S(1)}, bf16[128,1024]{1,0:T(8,128)(2,1)S(1)}, u32[]{:S(2)}, u32[]{:S(2)}) %collective-permute-start.16) | collective-permute-done | bytes 262176 | tf_op jit(solution)/shard_map/ppermute | solution.py:1788
  105.9 21.3 %shard_map.347 = (bf16[1024,2048]{1,0:T(8,128)(2,1)}, bf16[16,1024]{1,0:T(8,128)(2,1)}, bf16[1024,1024]{1,0:T(8,128)(2,1)}, bf16[1024,1536]{1,0:T(8,128)(2,1)}, ...) custom-call(s32[4]{0:T(128)} %pad_add_fusion.place.refs_0_, ...), custom_call_target="tpu_custom_call" | custom-call | flops 1 | bytes 1 | tf_op jit(solution)/shard_map/pallas_call | solution.py:746
  127.2 10.7 %collective-permute-done.22.refs_1_ = bf16[48,1024]{1,0:T(8,128)(2,1)S(1)} collective-permute-done((bf16[48,1024]{1,0:T(8,128)(2,1)}, bf16[48,1024]{1,0:T(8,128)(2,1)S(1)}, u32[]{:S(2)}, u32[]{:S(2)}) %collective-permute-start.22) | collective-permute-done | bytes 98336 | tf_op jit(solution)/shard_map/ppermute | solution.py:1788
  149.0 4.3 collective-permute-done.24.refs_3_
  159.7 15.8 %shard_map.349 = (bf16[1024,2048]{1,0:T(8,128)(2,1)}, f32[1024,1024]{1,0:T(8,128)}, bf16[1024,1024]{1,0:T(8,128)(2,1)}, bf16[1024,512]{1,0:T(8,128)(2,1)}, bf16[...) custom-call(s32[4]{0:T(128)} %pad_add_fusion.place.refs_0_, ...), custom_call_target="tpu_custom_call" | custom-call | flops 1 | bytes 1 | tf_op jit(solution)/shard_map/pallas_call | solution.py:746
  184.8 12.6 %collective-permute-done.35.refs_5_ = bf16[2,256,512]{2,1,0:T(8,128)(2,1)S(1)} collective-permute-done((bf16[2,256,512]{2,1,0:T(8,128)(2,1)S(1)}, bf16[2,256,512]{2,1,0:T(8,128)(2,1)S(1)}, u32[]{:S(2)}, u32[]{:S(2)}) %collective-permute-start.35) | collective-permute-done | bytes 524320 | tf_op jit(solution)/shard_map/ppermute | solution.py:1785
  200.6 26.0 %shard_map.351 = (bf16[4,4,256,512]{3,2,1,0:T(8,128)(2,1)}, f32[1024,1024]{1,0:T(8,128)}, bf16[1024,1024]{1,0:T(8,128)(2,1)}, bf16[1024,1024]{1,0:T(8,128)(2,1)}...) custom-call(s32[4]{0:T(128)} %pad_add_fusion.place.refs_0_, f32[1024,1024]{1,0:T(8,128)} %get-tuple-element.916.after_in.refs_1_, ...), custom_call_target="tpu_custom_call" | custom-call | flops 1 | bytes 1 | tf_op jit(solution)/shard_map/pallas_call | solution.py:746
  226.7 12.3 %all-gather.15.cloned.1.call-done = bf16[16,256,512]{2,1,0:T(8,128)(2,1)} async-done(((bf16[4,256,512]{2,1,0:T(8,128)(2,1)}), bf16[16,256,512]{2,1,0:T(8,128)(2,1)}) %all-gather.15.cloned.1.call-update) | async-done | bytes 4194320 | tf_op jit(solution)/shard_map/all_gather | solution.py:1892
  239.5 23.9 %shard_map.352 = (bf16[256,2048]{1,0:T(8,128)(2,1)}, bf16[256,2048]{1,0:T(8,128)(2,1)}, bf16[256,2048]{1,0:T(8,128)(2,1)}, bf16[128,2048]{1,0:T(8,128)(2,1)}, bf...) custom-call(s32[4]{0:T(128)} %pad_add_fusion.place.refs_0_, ...), custom_call_target="tpu_custom_call" | custom-call | flops 1 | bytes 1 | tf_op jit(solution)/shard_map/pallas_call | solution.py:746
  276.9 23.3 %shard_map.353 = (f32[1024,1024]{1,0:T(8,128)}, bf16[1024,1024]{1,0:T(8,128)(2,1)}, f32[8,1024]{1,0:T(8,128)}, bf16[128,1024]{1,0:T(8,128)(2,1)}, bf16[256,2048]...) custom-call(s32[4]{0:T(128)} %pad_add_fusion.place.refs_0_, ...), custom_call_target="tpu_custom_call" | custom-call | flops 1 | bytes 1 | tf_op jit(solution)/shard_map/pallas_call | solution.py:746
  310.3 28.0 %shard_map.355 = (f32[4,128,1024]{2,1,0:T(8,128)}, bf16[1024,1024]{1,0:T(8,128)(2,1)}, f32[8,1024]{1,0:T(8,128)}, bf16[1024,1536]{1,0:T(8,128)(2,1)}) custom-call(s32[4]{0:T(128)} %pad_add_fusion.place.refs_0_, f32[1024,1024]{1,0:T(8,128)} %get-tuple-element.916.after_in.refs_1_, bf16[1024,1024]{1,0:T(8,128)(2,1)} %get-tuple-element.917.refs_2_, ...), custom_call_target="tpu_custom_call" | custom-call | flops 1 | bytes 1 | tf_op jit(solution)/shard_map/pallas_call | solution.py:746
  338.3 4.8 %collective-permute-done.45.from_side = bf16[128,2048]{1,0:T(8,128)(2,1)S(1)} collective-permute-done((bf16[128,2048]{1,0:T(8,128)(2,1)}, bf16[128,2048]{1,0:T(8,128)(2,1)S(1)}, u32[]{:S(2)}, u32[]{:S(2)}) %collective-permute-start.45) | collective-permute-done | bytes 524320 | tf_op jit(solution)/shard_map/ppermute | solution.py:1785
  343.9 3.7 shard_map.360
  357.4 12.8 %shard_map.357 = (bf16[256,2048]{1,0:T(8,128)(2,1)}, bf16[256,2048]{1,0:T(8,128)(2,1)}, bf16[256,2048]{1,0:T(8,128)(2,1)}, bf16[128,2048]{1,0:T(8,128)(2,1)}, bf16[128,2048]{1,0:T(8,128)(2,1)}) custom-call(s32[4]{0:T(128)} %pad_add_fusion.place.refs_0_, bf16[1024,1024]{1,0:T(8,128)(2,1)} %get-tuple-element.952.normed, ...), custom_call_target="tpu_custom_call" | custom-call | flops 1 | bytes 1 | tf_op jit(solution)/shard_map/pallas_call | solution.py:746
  379.7 7.9 %shard_map.363 = (f32[4,128,1024]{2,1,0:T(8,128)}, bf16[4,128,1024]{2,1,0:T(8,128)(2,1)}) custom-call(s32[4]{0:T(128)} %pad_add_fusion.place.refs_0_, bf16[1024,1536]{1,0:T(8,128)(2,1)} %get-tuple-element.1000.dq.dk.dv.dqkv, bf16[1024,2048]{1,0:T(8,128)(2,1)} %get-tuple-element.1001.refs_6_.weights), custom_call_target="tpu_custom_call" | custom-call | flops 1 | bytes 1 | tf_op jit(solution)/shard_map/pallas_call | solution.py:746
  396.3 5.8 %shard_map.368 = (bf16[176,1024]{1,0:T(8,128)(2,1)}, bf16[176,1024]{1,0:T(8,128)(2,1)}, bf16[176,1024]{1,0:T(8,128)(2,1)}, bf16[176,1024]{1,0:T(8,128)(2,1)}) custom-call(s32[4]{0:T(128)} %pad_add_fusion.place.refs_0_, bf16[4,128,1024]{2,1,0:T(8,128)(2,1)} %shard_map.346.own.rows, f32[4,128,1024]{2,1,0:T(8,128)} %get-tuple-element.1039.grad_own, ...), custom_call_target="tpu_custom_call" | custom-call | flops 1 | bytes 1 | tf_op jit(solution)/shard_map/pallas_call | solution.py:746
  404.6 13.7 %collective-permute-done.56.over = bf16[256,2048]{1,0:T(8,128)(2,1)S(1)} collective-permute-done((bf16[256,2048]{1,0:T(8,128)(2,1)}, bf16[256,2048]{1,0:T(8,128)(2,1)S(1)}, u32[]{:S(2)}, u32[]{:S(2)}) %collective-permute-start.56) | collective-permute-done | bytes 1048608 | tf_op jit(solution)/shard_map/ppermute | solution.py:1785
  423.4 3.7 collective-permute-done.61.refs_2_
  427.1 7.7 %collective-permute-done.62.refs_3_ = bf16[176,1024]{1,0:T(8,128)(2,1)S(1)} collective-permute-done((bf16[176,1024]{1,0:T(8,128)(2,1)}, bf16[176,1024]{1,0:T(8,128)(2,1)S(1)}, u32[]{:S(2)}, u32[]{:S(2)}) %collective-permute-start.62) | collective-permute-done | bytes 360480 | tf_op jit(solution)/shard_map/ppermute | solution.py:1788
  (315 shorter events, 178.3 us)
Async XLA Ops:
  7.2 86.1 %all-gather.9.cloned.1.call-start = ((), (), s32[]{:S(2)}) async-start(), calls=%async_computation.7 | async-start | bytes 1310720 | tf_op jit(solution)/shard_map/all_gather | solution.py:1797
  48.3 89.6 %all-gather.11.cloned.1.call-start = ((), (), s32[]{:S(2)}) async-start(), calls=%async_computation.8 | async-start | bytes 1310720 | tf_op jit(solution)/shard_map/all_gather | solution.py:1797
  98.3 82.3 %all-gather.13.cloned.1.call-start = ((), (), s32[]{:S(2)}) async-start(), calls=%async_computation.9 | async-start | bytes 1310720 | tf_op jit(solution)/shard_map/all_gather | solution.py:1797
  100.8 37.2 %collective-permute-start.20 = (bf16[4,256,512]{2,1,0:T(8,128)(2,1)}, bf16[4,256,512]{2,1,0:T(8,128)(2,1)S(1)}, u32[]{:S(2)}, u32[]{:S(2)}) collective-permute-start(bf16[4,256,512]{2,1,0:T(8,128)(2,1)} %bitcast.10.refs_0_), channel_id=1, source_target_pairs={{0,8},{8,0},{16,24},{24,16},{1,9},{9,1},{17,25},{25,17},{2,10},{10... | collective-permute-start | bytes 3145736 | tf_op jit(solution)/shard_map/ppermute | solution.py:1785
  101.5 36.5 %collective-permute-start.21 = (bf16[4,256,512]{2,1,0:T(8,128)(2,1)}, bf16[4,256,512]{2,1,0:T(8,128)(2,1)S(1)}, u32[]{:S(2)}, u32[]{:S(2)}) collective-permute-start(bf16[4,256,512]{2,1,0:T(8,128)(2,1)} %bitcast.10.refs_0_), channel_id=1, source_target_pairs={{0,16},{8,24},{16,0},{24,8},{1,17},{9,25},{17,1},{25,9},{2,18},{10... | collective-permute-start | bytes 3145736 | tf_op jit(solution)/shard_map/ppermute | solution.py:1785
  102.7 35.2 %collective-permute-start.19 = (bf16[128,1024]{1,0:T(8,128)(2,1)}, bf16[128,1024]{1,0:T(8,128)(2,1)S(1)}, u32[]{:S(2)}, u32[]{:S(2)}) collective-permute-start(bf16[128,1024]{1,0:T(8,128)(2,1)} %get-tuple-element.680), channel_id=1, source_target_pairs={{2,0},{3,1},{0,2},{1,3},{6,4},{7,5},{4,6},{5,7},{10,8},{11,9},{8,1... | collective-permute-start | bytes 786440 | tf_op jit(solution)/shard_map/ppermute | solution.py:1788
  102.7 35.2 %collective-permute-start.22 = (bf16[48,1024]{1,0:T(8,128)(2,1)}, bf16[48,1024]{1,0:T(8,128)(2,1)S(1)}, u32[]{:S(2)}, u32[]{:S(2)}) collective-permute-start(bf16[48,1024]{1,0:T(8,128)(2,1)} %get-tuple-element.702), channel_id=1, source_target_pairs={{1,0},{2,1},{3,2},{0,3},{5,4},{6,5},{7,6},{4,7},{9,8},{10,9},{11,1... | collective-permute-start | bytes 294920 | tf_op jit(solution)/shard_map/ppermute | solution.py:1788
  104.7 33.2 %collective-permute-start.23 = (bf16[48,1024]{1,0:T(8,128)(2,1)}, bf16[48,1024]{1,0:T(8,128)(2,1)}, u32[]{:S(2)}, u32[]{:S(2)}) collective-permute-start(bf16[48,1024]{1,0:T(8,128)(2,1)} %get-tuple-element.703), channel_id=1, source_target_pairs={{3,0},{0,1},{1,2},{2,3},{7,4},{4,5},{5,6},{6,7},{11,8},{8,9},{9,10... | collective-permute-start | bytes 294920 | tf_op jit(solution)/shard_map/ppermute | solution.py:1788
  141.3 97.7 %all-gather.15.cloned.1.call-start = ((), (), s32[]{:S(2)}) async-start(), calls=%async_computation.10 | async-start | bytes 5242880 | tf_op jit(solution)/shard_map/all_gather | solution.py:1892
  154.1 26.6 %collective-permute-start.32 = (bf16[4,256,512]{2,1,0:T(8,128)(2,1)S(1)}, bf16[4,256,512]{2,1,0:T(8,128)(2,1)S(1)}, u32[]{:S(2)}, u32[]{:S(2)}) collective-permute-start(bf16[4,256,512]{2,1,0:T(8,128)(2,1)S(1)} %bitcast.55), channel_id=1, source_target_pairs={{0,16},{8,24},{16,0},{24,8},{1,17},{9,25},{17,1},{25,9},{2,18},{10... | collective-permute-start | bytes 3145736 | tf_op jit(solution)/shard_map/ppermute | solution.py:1785
  180.7 121.7 %reduce-scatter.13.cloned.1.call-start = ((), (), s32[]{:S(2)}) async-start(), calls=%async_computation.11 | async-start | bytes 5242880
  239.0 104.9 %reduce-scatter.7.cloned.1.call-start = ((), (), s32[]{:S(2)}) async-start(), calls=%async_computation.4 | async-start | bytes 1310720 | tf_op jit(solution)/shard_map/reduce_scatter | solution.py:1927
  267.0 33.2 %collective-permute-start.38 = (bf16[128,2048]{1,0:T(8,128)(2,1)}, bf16[128,2048]{1,0:T(8,128)(2,1)}, u32[]{:S(2)}, u32[]{:S(2)}) collective-permute-start(bf16[128,2048]{1,0:T(8,128)(2,1)} %get-tuple-element.877), channel_id=1, source_target_pairs={{0,8},{8,0},{16,24},{24,16},{1,9},{9,1},{17,25},{25,17},{2,10},{10... | collective-permute-start | bytes 1572872 | tf_op jit(solution)/shard_map/ppermute | solution.py:1785
  268.2 32.1 %collective-permute-start.39 = (bf16[128,2048]{1,0:T(8,128)(2,1)}, bf16[128,2048]{1,0:T(8,128)(2,1)}, u32[]{:S(2)}, u32[]{:S(2)}) collective-permute-start(bf16[128,2048]{1,0:T(8,128)(2,1)} %get-tuple-element.878), channel_id=1, source_target_pairs={{0,16},{8,24},{16,0},{24,8},{1,17},{9,25},{17,1},{25,9},{2,18},{10... | collective-permute-start | bytes 1572872 | tf_op jit(solution)/shard_map/ppermute | solution.py:1785
  271.5 28.7 %collective-permute-start.41 = (bf16[128,1024]{1,0:T(8,128)(2,1)}, bf16[128,1024]{1,0:T(8,128)(2,1)S(1)}, u32[]{:S(2)}, u32[]{:S(2)}) collective-permute-start(bf16[128,1024]{1,0:T(8,128)(2,1)} %get-tuple-element.907), channel_id=1, source_target_pairs={{1,0},{2,1},{3,2},{0,3},{5,4},{6,5},{7,6},{4,7},{9,8},{10,9},{11,1... | collective-permute-start | bytes 786440 | tf_op jit(solution)/shard_map/ppermute | solution.py:1788
  271.8 28.5 %collective-permute-start.42 = (bf16[128,1024]{1,0:T(8,128)(2,1)}, bf16[128,1024]{1,0:T(8,128)(2,1)S(1)}, u32[]{:S(2)}, u32[]{:S(2)}) collective-permute-start(bf16[128,1024]{1,0:T(8,128)(2,1)} %get-tuple-element.908), channel_id=1, source_target_pairs={{2,0},{3,1},{0,2},{1,3},{6,4},{7,5},{4,6},{5,7},{10,8},{11,9},{8,1... | collective-permute-start | bytes 786440 | tf_op jit(solution)/shard_map/ppermute | solution.py:1788
  273.9 26.3 %collective-permute-start.43 = (bf16[128,1024]{1,0:T(8,128)(2,1)}, bf16[128,1024]{1,0:T(8,128)(2,1)S(1)}, u32[]{:S(2)}, u32[]{:S(2)}) collective-permute-start(bf16[128,1024]{1,0:T(8,128)(2,1)} %get-tuple-element.909), channel_id=1, source_target_pairs={{3,0},{0,1},{1,2},{2,3},{7,4},{4,5},{5,6},{6,7},{11,8},{8,9},{9,10... | collective-permute-start | bytes 786440 | tf_op jit(solution)/shard_map/ppermute | solution.py:1788
  302.4 85.3 %reduce-scatter.11.cloned.1.call-start = ((), (), s32[]{:S(2)}) async-start(), calls=%async_computation.6 | async-start | bytes 1310720 | tf_op jit(solution)/shard_map/reduce_scatter | solution.py:1936
  306.0 37.1 %collective-permute-start.47 = (bf16[256,2048]{1,0:T(8,128)(2,1)}, bf16[256,2048]{1,0:T(8,128)(2,1)S(1)}, u32[]{:S(2)}, u32[]{:S(2)}) collective-permute-start(bf16[256,2048]{1,0:T(8,128)(2,1)} %get-tuple-element.946), channel_id=1, source_target_pairs={{0,16},{8,24},{16,0},{24,8},{1,17},{9,25},{17,1},{25,9},{2,18},{10... | collective-permute-start | bytes 3145736 | tf_op jit(solution)/shard_map/ppermute | solution.py:1785
  307.3 36.7 %collective-permute-start.48 = (bf16[256,2048]{1,0:T(8,128)(2,1)}, bf16[256,2048]{1,0:T(8,128)(2,1)}, u32[]{:S(2)}, u32[]{:S(2)}) collective-permute-start(bf16[256,2048]{1,0:T(8,128)(2,1)} %get-tuple-element.947), channel_id=1, source_target_pairs={{0,8},{8,0},{16,24},{24,16},{1,9},{9,1},{17,25},{25,17},{2,10},{10... | collective-permute-start | bytes 3145736 | tf_op jit(solution)/shard_map/ppermute | solution.py:1785
  307.5 35.7 %collective-permute-start.45 = (bf16[128,2048]{1,0:T(8,128)(2,1)}, bf16[128,2048]{1,0:T(8,128)(2,1)S(1)}, u32[]{:S(2)}, u32[]{:S(2)}) collective-permute-start(bf16[128,2048]{1,0:T(8,128)(2,1)} %get-tuple-element.925), channel_id=1, source_target_pairs={{0,8},{8,0},{16,24},{24,16},{1,9},{9,1},{17,25},{25,17},{2,10},{10... | collective-permute-start | bytes 1572872 | tf_op jit(solution)/shard_map/ppermute | solution.py:1785
  308.7 34.4 %collective-permute-start.46 = (bf16[128,2048]{1,0:T(8,128)(2,1)}, bf16[128,2048]{1,0:T(8,128)(2,1)}, u32[]{:S(2)}, u32[]{:S(2)}) collective-permute-start(bf16[128,2048]{1,0:T(8,128)(2,1)} %get-tuple-element.926), channel_id=1, source_target_pairs={{0,16},{8,24},{16,0},{24,8},{1,17},{9,25},{17,1},{25,9},{2,18},{10... | collective-permute-start | bytes 1572872 | tf_op jit(solution)/shard_map/ppermute | solution.py:1785
  350.9 92.6 %reduce-scatter.9.cloned.1.call-start = ((), (), s32[]{:S(2)}) async-start(), calls=%async_computation.5 | async-start | bytes 1310720 | tf_op jit(solution)/shard_map/reduce_scatter | solution.py:1945
  403.6 31.2 %collective-permute-start.62 = (bf16[176,1024]{1,0:T(8,128)(2,1)}, bf16[176,1024]{1,0:T(8,128)(2,1)S(1)}, u32[]{:S(2)}, u32[]{:S(2)}) collective-permute-start(bf16[176,1024]{1,0:T(8,128)(2,1)} %get-tuple-element.1049), channel_id=1, source_target_pairs={{3,0},{0,1},{1,2},{2,3},{7,4},{4,5},{5,6},{6,7},{11,8},{8,9},{9,10... | collective-permute-start | bytes 1081352 | tf_op jit(solution)/shard_map/ppermute | solution.py:1788
  (114 other events, 1335.8 us)
Sparse Core Ops, SparseCore 0:
  48.5 34.3 all-gather.8
  98.4 37.4 all-gather.10
  141.5 35.3 all-gather.12
  180.8 58.1 all-gather.14
  241.8 55.8 reduce-scatter.12
  302.5 22.7 reduce-scatter.6
  351.0 23.7 reduce-scatter.10
  379.8 25.3 reduce-scatter.8

commit v5 on v4

--- a/solution.py
+++ b/solution.py
@@ -738,7 +738,7 @@
     )
 
 
-def call(body, outs, ins, operands, scratch=(), limit=60, grid=None, flops=0, moved=0):
+def call(body, outs, ins, operands, scratch=(), limit=24, grid=None, flops=0, moved=0):
     single = not isinstance(outs, (list, tuple))
     extra = {} if grid is None else {"grid": grid}
     cost = pl.CostEstimate(flops=1, bytes_accessed=1, transcendentals=0)
@@ -890,7 +890,6 @@
         [ANY] * len(parts),
         parts,
         [pltpu.SemaphoreType.DMA((len(parts),))],
-        limit=60,
     )[0]
 
 
@@ -1093,6 +1092,7 @@
         [SMEM, VMEM, VMEM] + [ANY] * 10,
         (place, own, other, *near, *far),
         [pltpu.VMEM((1024, 2048), BF), pltpu.SemaphoreType.DMA((40,)), pltpu.SemaphoreType.DMA((1,))],
+        limit=60,
     )
 
 
@@ -1157,6 +1157,7 @@
         [pltpu.VMEM((1024, 2048), BF)]
         + [pltpu.VMEM((1024, 1024), BF)] * 2
         + [pltpu.SemaphoreType.DMA((16,)), pltpu.SemaphoreType.DMA((1,)), pltpu.SemaphoreType.DMA((2, 4))],
+        limit=60,
     )
 
 
@@ -1303,10 +1304,10 @@
         + [pltpu.VMEM((1024, 1024), F32), pltpu.VMEM((1024, 2048), BF)]
         + [pltpu.VMEM((1024, 1024), F32), pltpu.VMEM((1024, 1024), BF), pltpu.VMEM((1024, 1024), BF)]
         + [pltpu.SemaphoreType.DMA((3,)), pltpu.SemaphoreType.DMA((16,)), pltpu.SemaphoreType.DMA((3, 4))],
-        limit=60,
         grid=(2,),
         flops=FEED_FLOPS,
         moved=30 * MIB,
+        limit=60,
     )
 
 
@@ -1325,10 +1326,10 @@
         [pltpu.VMEM((1024, 1024), F32)] * 2
         + [pltpu.VMEM((1024, 1024), BF)] * 2
         + [pltpu.VMEM((1024, 1024), F32)],
-        limit=60,
         grid=(2,),
         flops=FEED_FLOPS,
         moved=26 * MIB,
+        limit=60,
     )
 
 
@@ -1535,10 +1536,10 @@
         [SMEM, square, square, cut(0), cut(4), cut(8), cut(0)],
         (place, normed, low_grad, dqkv, dqkv, dqkv, mix),
         [pltpu.VMEM((1024, 1024), BF)] * 2 + [pltpu.VMEM((1024, 512), F32)],
-        limit=60,
         grid=(4,),
         flops=4 * 2**30,
         moved=12 * MIB,
+        limit=60,
     )
 
 
@@ -1558,9 +1559,9 @@
         [(VMEM, like(4, 128, 1024, dtype=F32)), (VMEM, like(4, 128, 1024))],
         [SMEM, VMEM, VMEM],
         (place, dqkv, weights),
-        limit=60,
         flops=3 * 2**30,
         moved=10 * MIB,
+        limit=60,
     )
 
 
@@ -1667,7 +1668,6 @@
         [(VMEM, like(256, 2048))] * 2,
         [VMEM] * 4,
         (over, side, from_side, from_over),
-        limit=60,
         moved=5 * MIB,
     )
 
@@ -1688,7 +1688,6 @@
         [(VMEM, like(256, 512, dtype=F32))] + [(VMEM, like(256, 512))] * 3,
         [SMEM] + [VMEM] * 3,
         (place, own, over, side),
-        limit=60,
         moved=5 * MIB,
     )
 
@@ -1725,7 +1724,6 @@
         [(VMEM, like(128, 512, dtype=F32)), (VMEM, like(128, 512))],
         [SMEM] + [VMEM] * 4,
         (place, keep, *parts),
-        limit=60,
         moved=2 * MIB,
     )
 
@@ -1744,7 +1742,6 @@
         [(VMEM, like(128, 256, dtype=F32))] * 4,
         [SMEM] + [VMEM] * 2,
         (place, mine, other),
-        limit=60,
         moved=MIB,
     )
 
@@ -1764,7 +1761,6 @@
         [(VMEM, like(128, 1024, dtype=F32))] * 2,
         [SMEM] + [VMEM] * 4,
         (place, *halves),
-        limit=60,
         moved=2 * MIB,
     )
 

time: 490 us -> 482 us (0.984)
  Pallas kernels: 232 us -> 196 us
  local copies, waits for them, and re-layouts: 23.8 us -> 48.5 us
  waiting for transfers between devices: 132 us -> 140 us
    pallas_call x34, Pallas kernels: 232 us -> 196 us  [call(): pl.pallas_call(body, in_specs=ins, out_specs=out_specs, out_shape=out_sha...]
    unnamed x120 -> x176, local copies, waits for them, and re-layouts: 13.9 us -> 35.7 us
    ppermute x21, waiting for transfers between devices: 62.1 us -> 69 us  [shift(): return lax.ppermute(value, 'hi', [((i + step) % 4, i) for i in range(4)])]
  transfers between devices with their start and end apart: 78 -> 78, of which waited for: 27 -> 28; matrix products, arithmetic and copies ran while one was open for 2% -> 3% of each run, Pallas kernels for 45% -> 39%
where the time goes in v5:
time: 482 us; the launch traced here: 477 us
  Pallas kernels  196 us (41%)
  waiting for transfers between devices  140 us (29%)
  starting transfers between devices  77 us (16%)
  local copies, waits for them, and re-layouts  48.5 us (10%)
  between operations  15.4 us (3%)
    pallas_call x34, Pallas kernels, call(): pl.pallas_call(body, in_specs=ins, out_specs=out_specs, out_shape=out_sha...  196 us
    ppermute x21, waiting for transfers between devices, shift(): return lax.ppermute(value, 'hi', [((i + step) % 4, i) for i in range(4)])  69 us
    ppermute x31, waiting for transfers between devices, across(): return lax.ppermute(value, 'chip', [(i, i ^ bit) for i in range(4)])  56.1 us
    unnamed x176, local copies, waits for them, and re-layouts  35.7 us
    ppermute x21, starting transfers between devices, shift(): return lax.ppermute(value, 'hi', [((i + step) % 4, i) for i in range(4)])  35.1 us
    ppermute x31, starting transfers between devices, across(): return lax.ppermute(value, 'chip', [(i, i ^ bit) for i in range(4)])  22.8 us
    ppermute x18, starting transfers between devices, swap(): return lax.ppermute(value, 'core', [(0, 1), (1, 0)])  18.2 us
  transfers between devices with their start and end apart: 78, of which 28 were waited for; matrix products, arithmetic and copies ran while one was open for 3% of the time, Pallas kernels for 39%

profile of v5, /device:TPU:9, one launch (start us, length us, event | category | flops | bytes accessed | tf_op | source)
XLA Modules:
  0.0 477.2 jit_solution(8167584436229372968)
XLA Ops:
  41.2 8.9 %collective-permute-done.7.refs_1_ = bf16[256,512]{1,0:T(8,128)(2,1)S(1)} collective-permute-done((bf16[256,512]{1,0:T(8,128)(2,1)}, bf16[256,512]{1,0:T(8,128)(2,1)S(1)}, u32[]{:S(2)}, u32[]{:S(2)}) %collective-permute-start.7) | collective-permute-done | bytes 262176 | tf_op jit(solution)/shard_map/ppermute | solution.py:1784
  50.1 5.6 %collective-permute-done.8.refs_2_ = bf16[256,512]{1,0:T(8,128)(2,1)S(1)} collective-permute-done((bf16[256,512]{1,0:T(8,128)(2,1)}, bf16[256,512]{1,0:T(8,128)(2,1)S(1)}, u32[]{:S(2)}, u32[]{:S(2)}) %collective-permute-start.8) | collective-permute-done | bytes 262176 | tf_op jit(solution)/shard_map/ppermute | solution.py:1784
  57.1 8.5 %collective-permute-done.13 = bf16[128,1024]{1,0:T(8,128)(2,1)S(1)} collective-permute-done((bf16[128,1024]{1,0:T(8,128)(2,1)}, bf16[128,1024]{1,0:T(8,128)(2,1)S(1)}, u32[]{:S(2)}, u32[]{:S(2)}) %collective-permute-start.13) | collective-permute-done | bytes 262176 | tf_op jit(solution)/shard_map/ppermute | solution.py:1784
  65.6 8.9 %collective-permute-done.11.refs_6_ = bf16[768,512]{1,0:T(8,128)(2,1)S(1)} collective-permute-done((bf16[768,512]{1,0:T(8,128)(2,1)S(1)}, bf16[768,512]{1,0:T(8,128)(2,1)S(1)}, u32[]{:S(2)}, u32[]{:S(2)}) %collective-permute-start.11) | collective-permute-done | bytes 786464 | tf_op jit(solution)/shard_map/ppermute | solution.py:1781
  76.1 10.8 %collective-permute-start.16 = (bf16[128,1024]{1,0:T(8,128)(2,1)S(1)}, bf16[128,1024]{1,0:T(8,128)(2,1)S(1)}, u32[]{:S(2)}, u32[]{:S(2)}) collective-permute-start(bf16[128,1024]{1,0:T(8,128)(2,1)S(1)} %copy-done.67), channel_id=1, source_target_pairs={{1,0},{2,1},{3,2},{0,3},{5,4},{6,5},{7,6},{4,7},{9,8},{10,9},{11,1... | collective-permute-start | bytes 786440 | tf_op jit(solution)/shard_map/ppermute | solution.py:1784
  87.0 12.0 %collective-permute-done.16 = bf16[128,1024]{1,0:T(8,128)(2,1)S(1)} collective-permute-done((bf16[128,1024]{1,0:T(8,128)(2,1)S(1)}, bf16[128,1024]{1,0:T(8,128)(2,1)S(1)}, u32[]{:S(2)}, u32[]{:S(2)}) %collective-permute-start.16) | collective-permute-done | bytes 262176 | tf_op jit(solution)/shard_map/ppermute | solution.py:1784
  109.6 21.3 %shard_map.347 = (bf16[1024,2048]{1,0:T(8,128)(2,1)}, bf16[16,1024]{1,0:T(8,128)(2,1)}, bf16[1024,1024]{1,0:T(8,128)(2,1)}, bf16[1024,1536]{1,0:T(8,128)(2,1)}, ...) custom-call(s32[4]{0:T(128)} %copy-done.22, bf16[4,128,1024]{2,1,0:T(8,128)(2,1)} %copy-done, ...), custom_call_target="tpu_custom_call" | custom-call | flops 1 | bytes 1 | tf_op jit(solution)/shard_map/pallas_call | solution.py:746
  130.9 10.4 %collective-permute-done.22.refs_1_ = bf16[48,1024]{1,0:T(8,128)(2,1)S(1)} collective-permute-done((bf16[48,1024]{1,0:T(8,128)(2,1)}, bf16[48,1024]{1,0:T(8,128)(2,1)S(1)}, u32[]{:S(2)}, u32[]{:S(2)}) %collective-permute-start.22) | collective-permute-done | bytes 98336 | tf_op jit(solution)/shard_map/ppermute | solution.py:1784
  152.1 4.7 collective-permute-done.24.refs_3_
  164.7 15.9 %shard_map.349 = (bf16[1024,2048]{1,0:T(8,128)(2,1)}, f32[1024,1024]{1,0:T(8,128)}, bf16[1024,1024]{1,0:T(8,128)(2,1)}, bf16[1024,512]{1,0:T(8,128)(2,1)}, bf16[...) custom-call(s32[4]{0:T(128)} %copy-done.22, ...), custom_call_target="tpu_custom_call" | custom-call | flops 1 | bytes 1 | tf_op jit(solution)/shard_map/pallas_call | solution.py:746
  189.0 15.4 %collective-permute-done.35.refs_5_ = bf16[2,256,512]{2,1,0:T(8,128)(2,1)S(1)} collective-permute-done((bf16[2,256,512]{2,1,0:T(8,128)(2,1)S(1)}, bf16[2,256,512]{2,1,0:T(8,128)(2,1)S(1)}, u32[]{:S(2)}, u32[]{:S(2)}) %collective-permute-start.35) | collective-permute-done | bytes 524320 | tf_op jit(solution)/shard_map/ppermute | solution.py:1781
  207.5 26.0 %shard_map.351 = (bf16[4,4,256,512]{3,2,1,0:T(8,128)(2,1)}, f32[1024,1024]{1,0:T(8,128)}, bf16[1024,1024]{1,0:T(8,128)(2,1)}, bf16[1024,1024]{1,0:T(8,128)(2,1)}...) custom-call(s32[4]{0:T(128)} %copy-done.22, f32[1024,1024]{1,0:T(8,128)} %get-tuple-element.916.after_in.refs_1_, ...), custom_call_target="tpu_custom_call" | custom-call | flops 1 | bytes 1 | tf_op jit(solution)/shard_map/pallas_call | solution.py:746
  233.5 9.5 %all-gather.15.cloned.1.call-done = bf16[16,256,512]{2,1,0:T(8,128)(2,1)} async-done(((bf16[4,256,512]{2,1,0:T(8,128)(2,1)}), bf16[16,256,512]{2,1,0:T(8,128)(2,1)}) %all-gather.15.cloned.1.call-update) | async-done | bytes 4194320 | tf_op jit(solution)/shard_map/all_gather | solution.py:1888
  243.3 24.0 %shard_map.352 = (bf16[256,2048]{1,0:T(8,128)(2,1)}, bf16[256,2048]{1,0:T(8,128)(2,1)}, bf16[256,2048]{1,0:T(8,128)(2,1)}, bf16[128,2048]{1,0:T(8,128)(2,1)}, bf...) custom-call(s32[4]{0:T(128)} %copy-done.22, ...), custom_call_target="tpu_custom_call" | custom-call | flops 1 | bytes 1 | tf_op jit(solution)/shard_map/pallas_call | solution.py:746
  281.9 23.8 %shard_map.353 = (f32[1024,1024]{1,0:T(8,128)}, bf16[1024,1024]{1,0:T(8,128)(2,1)}, f32[8,1024]{1,0:T(8,128)}, bf16[128,1024]{1,0:T(8,128)(2,1)}, bf16[256,2048]...) custom-call(s32[4]{0:T(128)} %copy-done.22, ...), custom_call_target="tpu_custom_call" | custom-call | flops 1 | bytes 1 | tf_op jit(solution)/shard_map/pallas_call | solution.py:746
  312.2 27.9 %shard_map.355 = (f32[4,128,1024]{2,1,0:T(8,128)}, bf16[1024,1024]{1,0:T(8,128)(2,1)}, f32[8,1024]{1,0:T(8,128)}, bf16[1024,1536]{1,0:T(8,128)(2,1)}) custom-call(s32[4]{0:T(128)} %copy-done.22, f32[1024,1024]{1,0:T(8,128)} %get-tuple-element.916.after_in.refs_1_, bf16[1024,1024]{1,0:T(8,128)(2,1)} %get-tuple-element.917.refs_2_, ...), custom_call_target="tpu_custom_call" | custom-call | flops 1 | bytes 1 | tf_op jit(solution)/shard_map/pallas_call | solution.py:746
  340.1 6.2 %collective-permute-done.45.from_side = bf16[128,2048]{1,0:T(8,128)(2,1)S(1)} collective-permute-done((bf16[128,2048]{1,0:T(8,128)(2,1)}, bf16[128,2048]{1,0:T(8,128)(2,1)S(1)}, u32[]{:S(2)}, u32[]{:S(2)}) %collective-permute-start.45) | collective-permute-done | bytes 524320 | tf_op jit(solution)/shard_map/ppermute | solution.py:1781
  362.9 12.7 %shard_map.357 = (bf16[256,2048]{1,0:T(8,128)(2,1)}, bf16[256,2048]{1,0:T(8,128)(2,1)}, bf16[256,2048]{1,0:T(8,128)(2,1)}, bf16[128,2048]{1,0:T(8,128)(2,1)}, bf16[128,2048]{1,0:T(8,128)(2,1)}) custom-call(s32[4]{0:T(128)} %copy-done.22, bf16[1024,1024]{1,0:T(8,128)(2,1)} %get-tuple-element.952.normed, bf16[1024,1024]{1,0:T(8,128)(2,1)} %get-tuple-element.953.low_grad, ...), custom_call_target="tpu_custom_call" | custom-call | flops 1 | bytes 1 | tf_op jit(solution)/shard_map/pallas_call | solution.py:746
  381.4 7.9 %shard_map.363 = (f32[4,128,1024]{2,1,0:T(8,128)}, bf16[4,128,1024]{2,1,0:T(8,128)(2,1)}) custom-call(s32[4]{0:T(128)} %copy-done.22, bf16[1024,1536]{1,0:T(8,128)(2,1)} %get-tuple-element.1000.dq.dk.dv.dqkv, bf16[1024,2048]{1,0:T(8,128)(2,1)} %get-tuple-element.1001.refs_6_.weights), custom_call_target="tpu_custom_call" | custom-call | flops 1 | bytes 1 | tf_op jit(solution)/shard_map/pallas_call | solution.py:746
  390.4 3.6 collective-permute-start.59
  407.5 15.3 %collective-permute-done.56.over = bf16[256,2048]{1,0:T(8,128)(2,1)S(1)} collective-permute-done((bf16[256,2048]{1,0:T(8,128)(2,1)S(1)}, bf16[256,2048]{1,0:T(8,128)(2,1)S(1)}, u32[]{:S(2)}, u32[]{:S(2)}) %collective-permute-start.56) | collective-permute-done | bytes 1048608 | tf_op jit(solution)/shard_map/ppermute | solution.py:1781
  424.8 3.6 collective-permute-done.61.refs_2_
  428.3 7.7 %collective-permute-done.62.refs_3_ = bf16[176,1024]{1,0:T(8,128)(2,1)S(1)} collective-permute-done((bf16[176,1024]{1,0:T(8,128)(2,1)S(1)}, bf16[176,1024]{1,0:T(8,128)(2,1)S(1)}, u32[]{:S(2)}, u32[]{:S(2)}) %collective-permute-start.62) | collective-permute-done | bytes 360480 | tf_op jit(solution)/shard_map/ppermute | solution.py:1784
  456.6 7.3 %collective-permute-done.65.two = bf16[256,512]{1,0:T(8,128)(2,1)S(1)} collective-permute-done((bf16[256,512]{1,0:T(8,128)(2,1)}, bf16[256,512]{1,0:T(8,128)(2,1)S(1)}, u32[]{:S(2)}, u32[]{:S(2)}) %collective-permute-start.65) | collective-permute-done | bytes 262176 | tf_op jit(solution)/shard_map/ppermute | solution.py:1784
  (371 shorter events, 164.0 us)
Async XLA Ops:
  7.2 92.6 %all-gather.9.cloned.1.call-start = ((), (), s32[]{:S(2)}) async-start(), calls=%async_computation.7 | async-start | bytes 1310720 | tf_op jit(solution)/shard_map/all_gather | solution.py:1793
  56.5 84.8 %all-gather.11.cloned.1.call-start = ((), (), s32[]{:S(2)}) async-start(), calls=%async_computation.8 | async-start | bytes 1310720 | tf_op jit(solution)/shard_map/all_gather | solution.py:1793
  101.6 81.7 %all-gather.13.cloned.1.call-start = ((), (), s32[]{:S(2)}) async-start(), calls=%async_computation.9 | async-start | bytes 1310720 | tf_op jit(solution)/shard_map/all_gather | solution.py:1793
  104.0 37.3 %collective-permute-start.20 = (bf16[4,256,512]{2,1,0:T(8,128)(2,1)}, bf16[4,256,512]{2,1,0:T(8,128)(2,1)}, u32[]{:S(2)}, u32[]{:S(2)}) collective-permute-start(bf16[4,256,512]{2,1,0:T(8,128)(2,1)} %bitcast.57), channel_id=1, source_target_pairs={{0,8},{8,0},{16,24},{24,16},{1,9},{9,1},{17,25},{25,17},{2,10},{10... | collective-permute-start | bytes 3145736 | tf_op jit(solution)/shard_map/ppermute | solution.py:1781
  105.1 36.2 %collective-permute-start.21 = (bf16[4,256,512]{2,1,0:T(8,128)(2,1)}, bf16[4,256,512]{2,1,0:T(8,128)(2,1)}, u32[]{:S(2)}, u32[]{:S(2)}) collective-permute-start(bf16[4,256,512]{2,1,0:T(8,128)(2,1)} %bitcast.58), channel_id=1, source_target_pairs={{0,16},{8,24},{16,0},{24,8},{1,17},{9,25},{17,1},{25,9},{2,18},{10... | collective-permute-start | bytes 3145736 | tf_op jit(solution)/shard_map/ppermute | solution.py:1781
  106.3 34.9 %collective-permute-start.19 = (bf16[128,1024]{1,0:T(8,128)(2,1)S(1)}, bf16[128,1024]{1,0:T(8,128)(2,1)S(1)}, u32[]{:S(2)}, u32[]{:S(2)}) collective-permute-start(bf16[128,1024]{1,0:T(8,128)(2,1)S(1)} %copy-done.63), channel_id=1, source_target_pairs={{2,0},{3,1},{0,2},{1,3},{6,4},{7,5},{4,6},{5,7},{10,8},{11,9},{8,1... | collective-permute-start | bytes 786440 | tf_op jit(solution)/shard_map/ppermute | solution.py:1784
  106.3 34.9 %collective-permute-start.22 = (bf16[48,1024]{1,0:T(8,128)(2,1)}, bf16[48,1024]{1,0:T(8,128)(2,1)S(1)}, u32[]{:S(2)}, u32[]{:S(2)}) collective-permute-start(bf16[48,1024]{1,0:T(8,128)(2,1)} %copy-done.74), channel_id=1, source_target_pairs={{1,0},{2,1},{3,2},{0,3},{5,4},{6,5},{7,6},{4,7},{9,8},{10,9},{11,1... | collective-permute-start | bytes 294920 | tf_op jit(solution)/shard_map/ppermute | solution.py:1784
  107.9 33.4 %collective-permute-start.23 = (bf16[48,1024]{1,0:T(8,128)(2,1)S(1)}, bf16[48,1024]{1,0:T(8,128)(2,1)S(1)}, u32[]{:S(2)}, u32[]{:S(2)}) collective-permute-start(bf16[48,1024]{1,0:T(8,128)(2,1)S(1)} %copy-done.73), channel_id=1, source_target_pairs={{3,0},{0,1},{1,2},{2,3},{7,4},{4,5},{5,6},{6,7},{11,8},{8,9},{9,10... | collective-permute-start | bytes 294920 | tf_op jit(solution)/shard_map/ppermute | solution.py:1784
  145.7 97.3 %all-gather.15.cloned.1.call-start = ((), (), s32[]{:S(2)}) async-start(), calls=%async_computation.10 | async-start | bytes 5242880 | tf_op jit(solution)/shard_map/all_gather | solution.py:1888
  183.6 123.8 %reduce-scatter.13.cloned.1.call-start = ((), (), s32[]{:S(2)}) async-start(), calls=%async_computation.11 | async-start | bytes 5242880
  243.0 104.2 %reduce-scatter.7.cloned.1.call-start = ((), (), s32[]{:S(2)}) async-start(), calls=%async_computation.4 | async-start | bytes 1310720 | tf_op jit(solution)/shard_map/reduce_scatter | solution.py:1923
  270.9 34.9 %collective-permute-start.38 = (bf16[128,2048]{1,0:T(8,128)(2,1)}, bf16[128,2048]{1,0:T(8,128)(2,1)S(1)}, u32[]{:S(2)}, u32[]{:S(2)}) collective-permute-start(bf16[128,2048]{1,0:T(8,128)(2,1)} %get-tuple-element.877), channel_id=1, source_target_pairs={{0,8},{8,0},{16,24},{24,16},{1,9},{9,1},{17,25},{25,17},{2,10},{10... | collective-permute-start | bytes 1572872 | tf_op jit(solution)/shard_map/ppermute | solution.py:1781
  272.1 33.7 %collective-permute-start.39 = (bf16[128,2048]{1,0:T(8,128)(2,1)}, bf16[128,2048]{1,0:T(8,128)(2,1)S(1)}, u32[]{:S(2)}, u32[]{:S(2)}) collective-permute-start(bf16[128,2048]{1,0:T(8,128)(2,1)} %get-tuple-element.878), channel_id=1, source_target_pairs={{0,16},{8,24},{16,0},{24,8},{1,17},{9,25},{17,1},{25,9},{2,18},{10... | collective-permute-start | bytes 1572872 | tf_op jit(solution)/shard_map/ppermute | solution.py:1781
  276.2 29.6 %collective-permute-start.41 = (bf16[128,1024]{1,0:T(8,128)(2,1)}, bf16[128,1024]{1,0:T(8,128)(2,1)S(1)}, u32[]{:S(2)}, u32[]{:S(2)}) collective-permute-start(bf16[128,1024]{1,0:T(8,128)(2,1)} %get-tuple-element.907), channel_id=1, source_target_pairs={{1,0},{2,1},{3,2},{0,3},{5,4},{6,5},{7,6},{4,7},{9,8},{10,9},{11,1... | collective-permute-start | bytes 786440 | tf_op jit(solution)/shard_map/ppermute | solution.py:1784
  276.5 29.3 %collective-permute-start.42 = (bf16[128,1024]{1,0:T(8,128)(2,1)}, bf16[128,1024]{1,0:T(8,128)(2,1)}, u32[]{:S(2)}, u32[]{:S(2)}) collective-permute-start(bf16[128,1024]{1,0:T(8,128)(2,1)} %get-tuple-element.908), channel_id=1, source_target_pairs={{2,0},{3,1},{0,2},{1,3},{6,4},{7,5},{4,6},{5,7},{10,8},{11,9},{8,1... | collective-permute-start | bytes 786440 | tf_op jit(solution)/shard_map/ppermute | solution.py:1784
  278.6 27.2 %collective-permute-start.43 = (bf16[128,1024]{1,0:T(8,128)(2,1)}, bf16[128,1024]{1,0:T(8,128)(2,1)}, u32[]{:S(2)}, u32[]{:S(2)}) collective-permute-start(bf16[128,1024]{1,0:T(8,128)(2,1)} %get-tuple-element.909), channel_id=1, source_target_pairs={{3,0},{0,1},{1,2},{2,3},{7,4},{4,5},{5,6},{6,7},{11,8},{8,9},{9,10... | collective-permute-start | bytes 786440 | tf_op jit(solution)/shard_map/ppermute | solution.py:1784
  307.5 82.9 %reduce-scatter.11.cloned.1.call-start = ((), (), s32[]{:S(2)}) async-start(), calls=%async_computation.6 | async-start | bytes 1310720 | tf_op jit(solution)/shard_map/reduce_scatter | solution.py:1932
  309.3 37.9 %collective-permute-start.47 = (bf16[256,2048]{1,0:T(8,128)(2,1)}, bf16[256,2048]{1,0:T(8,128)(2,1)}, u32[]{:S(2)}, u32[]{:S(2)}) collective-permute-start(bf16[256,2048]{1,0:T(8,128)(2,1)} %get-tuple-element.946), channel_id=1, source_target_pairs={{0,16},{8,24},{16,0},{24,8},{1,17},{9,25},{17,1},{25,9},{2,18},{10... | collective-permute-start | bytes 3145736 | tf_op jit(solution)/shard_map/ppermute | solution.py:1781
  310.5 36.7 %collective-permute-start.48 = (bf16[256,2048]{1,0:T(8,128)(2,1)}, bf16[256,2048]{1,0:T(8,128)(2,1)}, u32[]{:S(2)}, u32[]{:S(2)}) collective-permute-start(bf16[256,2048]{1,0:T(8,128)(2,1)} %get-tuple-element.947), channel_id=1, source_target_pairs={{0,8},{8,0},{16,24},{24,16},{1,9},{9,1},{17,25},{25,17},{2,10},{10... | collective-permute-start | bytes 3145736 | tf_op jit(solution)/shard_map/ppermute | solution.py:1781
  310.8 35.6 %collective-permute-start.45 = (bf16[128,2048]{1,0:T(8,128)(2,1)}, bf16[128,2048]{1,0:T(8,128)(2,1)S(1)}, u32[]{:S(2)}, u32[]{:S(2)}) collective-permute-start(bf16[128,2048]{1,0:T(8,128)(2,1)} %get-tuple-element.925), channel_id=1, source_target_pairs={{0,8},{8,0},{16,24},{24,16},{1,9},{9,1},{17,25},{25,17},{2,10},{10... | collective-permute-start | bytes 1572872 | tf_op jit(solution)/shard_map/ppermute | solution.py:1781
  311.9 35.2 %collective-permute-start.46 = (bf16[128,2048]{1,0:T(8,128)(2,1)}, bf16[128,2048]{1,0:T(8,128)(2,1)}, u32[]{:S(2)}, u32[]{:S(2)}) collective-permute-start(bf16[128,2048]{1,0:T(8,128)(2,1)} %get-tuple-element.926), channel_id=1, source_target_pairs={{0,16},{8,24},{16,0},{24,8},{1,17},{9,25},{17,1},{25,9},{2,18},{10... | collective-permute-start | bytes 1572872 | tf_op jit(solution)/shard_map/ppermute | solution.py:1781
  354.3 89.3 %reduce-scatter.9.cloned.1.call-start = ((), (), s32[]{:S(2)}) async-start(), calls=%async_computation.5 | async-start | bytes 1310720 | tf_op jit(solution)/shard_map/reduce_scatter | solution.py:1941
  397.9 24.8 %collective-permute-start.56 = (bf16[256,2048]{1,0:T(8,128)(2,1)S(1)}, bf16[256,2048]{1,0:T(8,128)(2,1)S(1)}, u32[]{:S(2)}, u32[]{:S(2)}) collective-permute-start(bf16[256,2048]{1,0:T(8,128)(2,1)S(1)} %get-tuple-element.1024), channel_id=1, source_target_pairs={{0,16},{8,24},{16,0},{24,8},{1,17},{9,25},{17,1},{25,9},{2,18},{10... | collective-permute-start | bytes 3145736 | tf_op jit(solution)/shard_map/ppermute | solution.py:1781
  405.4 30.7 %collective-permute-start.62 = (bf16[176,1024]{1,0:T(8,128)(2,1)S(1)}, bf16[176,1024]{1,0:T(8,128)(2,1)S(1)}, u32[]{:S(2)}, u32[]{:S(2)}) collective-permute-start(bf16[176,1024]{1,0:T(8,128)(2,1)S(1)} %get-tuple-element.1049), channel_id=1, source_target_pairs={{3,0},{0,1},{1,2},{2,3},{7,4},{4,5},{5,6},{6,7},{11,8},{8,9},{9,10... | collective-permute-start | bytes 1081352 | tf_op jit(solution)/shard_map/ppermute | solution.py:1784
  (142 other events, 1791.9 us)
Sparse Core Ops, SparseCore 0:
  56.0 33.4 all-gather.8
  101.7 37.8 all-gather.10
  145.8 36.0 all-gather.12
  183.7 59.1 all-gather.14
  245.8 56.0 reduce-scatter.12
  307.6 23.0 reduce-scatter.6
  354.5 24.0 reduce-scatter.10
  381.4 25.6 reduce-scatter.8

commit v6 on v5

--- a/solution.py
+++ b/solution.py
@@ -1539,7 +1539,7 @@
         grid=(4,),
         flops=4 * 2**30,
         moved=12 * MIB,
-        limit=60,
+        limit=36,
     )
 
 
@@ -1561,7 +1561,7 @@
         (place, dqkv, weights),
         flops=3 * 2**30,
         moved=10 * MIB,
-        limit=60,
+        limit=36,
     )
 
 

time: 482 us -> 489 us (1.015)
  local copies, waits for them, and re-layouts: 48.5 us -> 65.2 us
  Pallas kernels: 196 us -> 190 us
    unnamed x176 -> x206, local copies, waits for them, and re-layouts: 35.7 us -> 52.4 us
    pallas_call x34, Pallas kernels: 196 us -> 190 us  [call(): pl.pallas_call(body, in_specs=ins, out_specs=out_specs, out_shape=out_sha...]
  transfers between devices with their start and end apart: 78 -> 78, of which waited for: 28 -> 25; matrix products, arithmetic and copies ran while one was open for 3% -> 2% of each run, Pallas kernels for 39% -> 38%
where the time goes in v6:
time: 489 us; the launch traced here: 484 us
  Pallas kernels  190 us (39%)
  waiting for transfers between devices  138 us (28%)
  starting transfers between devices  75.7 us (15%)
  local copies, waits for them, and re-layouts  65.2 us (13%)
  between operations  15.4 us (3%)
    pallas_call x34, Pallas kernels, call(): pl.pallas_call(body, in_specs=ins, out_specs=out_specs, out_shape=out_sha...  190 us
    ppermute x21, waiting for transfers between devices, shift(): return lax.ppermute(value, 'hi', [((i + step) % 4, i) for i in range(4)])  67.8 us
    ppermute x31, waiting for transfers between devices, across(): return lax.ppermute(value, 'chip', [(i, i ^ bit) for i in range(4)])  54.8 us
    unnamed x206, local copies, waits for them, and re-layouts  52.4 us
    ppermute x21, starting transfers between devices, shift(): return lax.ppermute(value, 'hi', [((i + step) % 4, i) for i in range(4)])  35.4 us
    ppermute x31, starting transfers between devices, across(): return lax.ppermute(value, 'chip', [(i, i ^ bit) for i in range(4)])  23.2 us
    ppermute x18, starting transfers between devices, swap(): return lax.ppermute(value, 'core', [(0, 1), (1, 0)])  16.2 us
  transfers between devices with their start and end apart: 78, of which 25 were waited for; matrix products, arithmetic and copies ran while one was open for 2% of the time, Pallas kernels for 38%

profile of v6, /device:TPU:9, one launch (start us, length us, event | category | flops | bytes accessed | tf_op | source)
XLA Modules:
  0.0 484.2 jit_solution(14707489460443265200)
XLA Ops:
  24.1 3.3 shard_map.341
  41.7 8.9 %collective-permute-done.7.refs_1_ = bf16[256,512]{1,0:T(8,128)(2,1)S(1)} collective-permute-done((bf16[256,512]{1,0:T(8,128)(2,1)}, bf16[256,512]{1,0:T(8,128)(2,1)S(1)}, u32[]{:S(2)}, u32[]{:S(2)}) %collective-permute-start.7) | collective-permute-done | bytes 262176 | tf_op jit(solution)/shard_map/ppermute | solution.py:1784
  50.7 5.6 %collective-permute-done.8.refs_2_ = bf16[256,512]{1,0:T(8,128)(2,1)S(1)} collective-permute-done((bf16[256,512]{1,0:T(8,128)(2,1)}, bf16[256,512]{1,0:T(8,128)(2,1)S(1)}, u32[]{:S(2)}, u32[]{:S(2)}) %collective-permute-start.8) | collective-permute-done | bytes 262176 | tf_op jit(solution)/shard_map/ppermute | solution.py:1784
  57.7 8.5 %collective-permute-done.13 = bf16[128,1024]{1,0:T(8,128)(2,1)S(1)} collective-permute-done((bf16[128,1024]{1,0:T(8,128)(2,1)}, bf16[128,1024]{1,0:T(8,128)(2,1)S(1)}, u32[]{:S(2)}, u32[]{:S(2)}) %collective-permute-start.13) | collective-permute-done | bytes 262176 | tf_op jit(solution)/shard_map/ppermute | solution.py:1784
  66.2 8.9 %collective-permute-done.11.refs_6_ = bf16[768,512]{1,0:T(8,128)(2,1)S(1)} collective-permute-done((bf16[768,512]{1,0:T(8,128)(2,1)S(1)}, bf16[768,512]{1,0:T(8,128)(2,1)S(1)}, u32[]{:S(2)}, u32[]{:S(2)}) %collective-permute-start.11) | collective-permute-done | bytes 786464 | tf_op jit(solution)/shard_map/ppermute | solution.py:1781
  76.7 10.8 %collective-permute-start.16 = (bf16[128,1024]{1,0:T(8,128)(2,1)S(1)}, bf16[128,1024]{1,0:T(8,128)(2,1)S(1)}, u32[]{:S(2)}, u32[]{:S(2)}) collective-permute-start(bf16[128,1024]{1,0:T(8,128)(2,1)S(1)} %copy-done.82), channel_id=1, source_target_pairs={{1,0},{2,1},{3,2},{0,3},{5,4},{6,5},{7,6},{4,7},{9,8},{10,9},{11,1... | collective-permute-start | bytes 786440 | tf_op jit(solution)/shard_map/ppermute | solution.py:1784
  87.5 12.0 %collective-permute-done.16 = bf16[128,1024]{1,0:T(8,128)(2,1)S(1)} collective-permute-done((bf16[128,1024]{1,0:T(8,128)(2,1)S(1)}, bf16[128,1024]{1,0:T(8,128)(2,1)S(1)}, u32[]{:S(2)}, u32[]{:S(2)}) %collective-permute-start.16) | collective-permute-done | bytes 262176 | tf_op jit(solution)/shard_map/ppermute | solution.py:1784
  110.1 21.3 %shard_map.347 = (bf16[1024,2048]{1,0:T(8,128)(2,1)}, bf16[16,1024]{1,0:T(8,128)(2,1)}, bf16[1024,1024]{1,0:T(8,128)(2,1)}, bf16[1024,1536]{1,0:T(8,128)(2,1)}, ...) custom-call(s32[4]{0:T(128)} %copy-done.37, bf16[4,128,1024]{2,1,0:T(8,128)(2,1)} %copy-done.1, ...), custom_call_target="tpu_custom_call" | custom-call | flops 1 | bytes 1 | tf_op jit(solution)/shard_map/pallas_call | solution.py:746
  131.5 10.3 %collective-permute-done.22.refs_1_ = bf16[48,1024]{1,0:T(8,128)(2,1)S(1)} collective-permute-done((bf16[48,1024]{1,0:T(8,128)(2,1)}, bf16[48,1024]{1,0:T(8,128)(2,1)S(1)}, u32[]{:S(2)}, u32[]{:S(2)}) %collective-permute-start.22) | collective-permute-done | bytes 98336 | tf_op jit(solution)/shard_map/ppermute | solution.py:1784
  152.7 4.7 collective-permute-done.24.refs_3_
  165.2 15.9 %shard_map.349 = (bf16[1024,2048]{1,0:T(8,128)(2,1)}, f32[1024,1024]{1,0:T(8,128)}, bf16[1024,1024]{1,0:T(8,128)(2,1)}, bf16[1024,512]{1,0:T(8,128)(2,1)}, bf16[...) custom-call(s32[4]{0:T(128)} %copy-done.37, ...), custom_call_target="tpu_custom_call" | custom-call | flops 1 | bytes 1 | tf_op jit(solution)/shard_map/pallas_call | solution.py:746
  189.6 15.4 %collective-permute-done.35.refs_5_ = bf16[2,256,512]{2,1,0:T(8,128)(2,1)S(1)} collective-permute-done((bf16[2,256,512]{2,1,0:T(8,128)(2,1)S(1)}, bf16[2,256,512]{2,1,0:T(8,128)(2,1)S(1)}, u32[]{:S(2)}, u32[]{:S(2)}) %collective-permute-start.35) | collective-permute-done | bytes 524320 | tf_op jit(solution)/shard_map/ppermute | solution.py:1781
  208.1 26.0 %shard_map.351 = (bf16[4,4,256,512]{3,2,1,0:T(8,128)(2,1)}, f32[1024,1024]{1,0:T(8,128)}, bf16[1024,1024]{1,0:T(8,128)(2,1)}, bf16[1024,1024]{1,0:T(8,128)(2,1)}...) custom-call(s32[4]{0:T(128)} %copy-done.37, f32[1024,1024]{1,0:T(8,128)} %get-tuple-element.916.after_in.refs_1_, ...), custom_call_target="tpu_custom_call" | custom-call | flops 1 | bytes 1 | tf_op jit(solution)/shard_map/pallas_call | solution.py:746
  234.1 9.4 %all-gather.15.cloned.1.call-done = bf16[16,256,512]{2,1,0:T(8,128)(2,1)} async-done(((bf16[4,256,512]{2,1,0:T(8,128)(2,1)}), bf16[16,256,512]{2,1,0:T(8,128)(2,1)}) %all-gather.15.cloned.1.call-update) | async-done | bytes 4194320 | tf_op jit(solution)/shard_map/all_gather | solution.py:1888
  243.9 24.0 %shard_map.352 = (bf16[256,2048]{1,0:T(8,128)(2,1)}, bf16[256,2048]{1,0:T(8,128)(2,1)}, bf16[256,2048]{1,0:T(8,128)(2,1)}, bf16[128,2048]{1,0:T(8,128)(2,1)}, bf...) custom-call(s32[4]{0:T(128)} %copy-done.37, ...), custom_call_target="tpu_custom_call" | custom-call | flops 1 | bytes 1 | tf_op jit(solution)/shard_map/pallas_call | solution.py:746
  282.6 23.8 %shard_map.353 = (f32[1024,1024]{1,0:T(8,128)}, bf16[1024,1024]{1,0:T(8,128)(2,1)}, f32[8,1024]{1,0:T(8,128)}, bf16[128,1024]{1,0:T(8,128)(2,1)}, bf16[256,2048]...) custom-call(s32[4]{0:T(128)} %copy-done.37, ...), custom_call_target="tpu_custom_call" | custom-call | flops 1 | bytes 1 | tf_op jit(solution)/shard_map/pallas_call | solution.py:746
  312.9 27.9 %shard_map.355 = (f32[4,128,1024]{2,1,0:T(8,128)}, bf16[1024,1024]{1,0:T(8,128)(2,1)}, f32[8,1024]{1,0:T(8,128)}, bf16[1024,1536]{1,0:T(8,128)(2,1)}) custom-call(s32[4]{0:T(128)} %copy-done.37, f32[1024,1024]{1,0:T(8,128)} %get-tuple-element.916.after_in.refs_1_, bf16[1024,1024]{1,0:T(8,128)(2,1)} %get-tuple-element.917.refs_2_, ...), custom_call_target="tpu_custom_call" | custom-call | flops 1 | bytes 1 | tf_op jit(solution)/shard_map/pallas_call | solution.py:746
  340.8 6.2 %collective-permute-done.45.from_side = bf16[128,2048]{1,0:T(8,128)(2,1)S(1)} collective-permute-done((bf16[128,2048]{1,0:T(8,128)(2,1)}, bf16[128,2048]{1,0:T(8,128)(2,1)S(1)}, u32[]{:S(2)}, u32[]{:S(2)}) %collective-permute-start.45) | collective-permute-done | bytes 524320 | tf_op jit(solution)/shard_map/ppermute | solution.py:1781
  370.9 11.1 %shard_map.357 = (bf16[256,2048]{1,0:T(8,128)(2,1)S(1)}, bf16[256,2048]{1,0:T(8,128)(2,1)S(1)}, bf16[256,2048]{1,0:T(8,128)(2,1)S(1)}, bf16[128,2048]{1,0:T(8,128)(2,1)}, bf16[128,2048]{1,0:T(8,128)(2,1)}) custom-call(s32[4]{0:T(128)S(1)} %copy-done.41, bf16[1024,1024]{1,0:T(8,128)(2,1)S(1)} %copy-done.14, bf16[1024,1024]{1,0:T(8,128)(2,1)S(1)} %copy-done.15, ...), custom_call_target="tpu_custom_call" | custom-call | flops 1 | bytes 1 | tf_op jit(solution)/shard_map/pallas_call | solution.py:746
  392.4 4.0 shard_map.363
  413.8 15.5 %collective-permute-done.56.over = bf16[256,2048]{1,0:T(8,128)(2,1)S(1)} collective-permute-done((bf16[256,2048]{1,0:T(8,128)(2,1)S(1)}, bf16[256,2048]{1,0:T(8,128)(2,1)S(1)}, u32[]{:S(2)}, u32[]{:S(2)}) %collective-permute-start.56) | collective-permute-done | bytes 1048608 | tf_op jit(solution)/shard_map/ppermute | solution.py:1781
  434.7 7.7 %collective-permute-done.62.refs_3_ = bf16[176,1024]{1,0:T(8,128)(2,1)S(1)} collective-permute-done((bf16[176,1024]{1,0:T(8,128)(2,1)S(1)}, bf16[176,1024]{1,0:T(8,128)(2,1)S(1)}, u32[]{:S(2)}, u32[]{:S(2)}) %collective-permute-start.62) | collective-permute-done | bytes 360480 | tf_op jit(solution)/shard_map/ppermute | solution.py:1784
  447.4 3.2 collective-permute-start.65
  463.9 6.4 %collective-permute-done.65.two = bf16[256,512]{1,0:T(8,128)(2,1)S(1)} collective-permute-done((bf16[256,512]{1,0:T(8,128)(2,1)}, bf16[256,512]{1,0:T(8,128)(2,1)S(1)}, u32[]{:S(2)}, u32[]{:S(2)}) %collective-permute-start.65) | collective-permute-done | bytes 262176 | tf_op jit(solution)/shard_map/ppermute | solution.py:1784
  (401 shorter events, 177.7 us)
Async XLA Ops:
  7.2 93.1 %all-gather.9.cloned.1.call-start = ((), (), s32[]{:S(2)}) async-start(), calls=%async_computation.7 | async-start | bytes 1310720 | tf_op jit(solution)/shard_map/all_gather | solution.py:1793
  57.0 84.8 %all-gather.11.cloned.1.call-start = ((), (), s32[]{:S(2)}) async-start(), calls=%async_computation.8 | async-start | bytes 1310720 | tf_op jit(solution)/shard_map/all_gather | solution.py:1793
  102.2 81.7 %all-gather.13.cloned.1.call-start = ((), (), s32[]{:S(2)}) async-start(), calls=%async_computation.9 | async-start | bytes 1310720 | tf_op jit(solution)/shard_map/all_gather | solution.py:1793
  104.6 37.3 %collective-permute-start.20 = (bf16[4,256,512]{2,1,0:T(8,128)(2,1)}, bf16[4,256,512]{2,1,0:T(8,128)(2,1)}, u32[]{:S(2)}, u32[]{:S(2)}) collective-permute-start(bf16[4,256,512]{2,1,0:T(8,128)(2,1)} %bitcast.57), channel_id=1, source_target_pairs={{0,8},{8,0},{16,24},{24,16},{1,9},{9,1},{17,25},{25,17},{2,10},{10... | collective-permute-start | bytes 3145736 | tf_op jit(solution)/shard_map/ppermute | solution.py:1781
  105.7 36.2 %collective-permute-start.21 = (bf16[4,256,512]{2,1,0:T(8,128)(2,1)}, bf16[4,256,512]{2,1,0:T(8,128)(2,1)}, u32[]{:S(2)}, u32[]{:S(2)}) collective-permute-start(bf16[4,256,512]{2,1,0:T(8,128)(2,1)} %bitcast.58), channel_id=1, source_target_pairs={{0,16},{8,24},{16,0},{24,8},{1,17},{9,25},{17,1},{25,9},{2,18},{10... | collective-permute-start | bytes 3145736 | tf_op jit(solution)/shard_map/ppermute | solution.py:1781
  106.9 34.9 %collective-permute-start.19 = (bf16[128,1024]{1,0:T(8,128)(2,1)S(1)}, bf16[128,1024]{1,0:T(8,128)(2,1)S(1)}, u32[]{:S(2)}, u32[]{:S(2)}) collective-permute-start(bf16[128,1024]{1,0:T(8,128)(2,1)S(1)} %copy-done.78), channel_id=1, source_target_pairs={{2,0},{3,1},{0,2},{1,3},{6,4},{7,5},{4,6},{5,7},{10,8},{11,9},{8,1... | collective-permute-start | bytes 786440 | tf_op jit(solution)/shard_map/ppermute | solution.py:1784
  106.9 34.9 %collective-permute-start.22 = (bf16[48,1024]{1,0:T(8,128)(2,1)}, bf16[48,1024]{1,0:T(8,128)(2,1)S(1)}, u32[]{:S(2)}, u32[]{:S(2)}) collective-permute-start(bf16[48,1024]{1,0:T(8,128)(2,1)} %copy-done.89), channel_id=1, source_target_pairs={{1,0},{2,1},{3,2},{0,3},{5,4},{6,5},{7,6},{4,7},{9,8},{10,9},{11,1... | collective-permute-start | bytes 294920 | tf_op jit(solution)/shard_map/ppermute | solution.py:1784
  108.5 33.4 %collective-permute-start.23 = (bf16[48,1024]{1,0:T(8,128)(2,1)S(1)}, bf16[48,1024]{1,0:T(8,128)(2,1)S(1)}, u32[]{:S(2)}, u32[]{:S(2)}) collective-permute-start(bf16[48,1024]{1,0:T(8,128)(2,1)S(1)} %copy-done.88), channel_id=1, source_target_pairs={{3,0},{0,1},{1,2},{2,3},{7,4},{4,5},{5,6},{6,7},{11,8},{8,9},{9,10... | collective-permute-start | bytes 294920 | tf_op jit(solution)/shard_map/ppermute | solution.py:1784
  146.3 97.3 %all-gather.15.cloned.1.call-start = ((), (), s32[]{:S(2)}) async-start(), calls=%async_computation.10 | async-start | bytes 5242880 | tf_op jit(solution)/shard_map/all_gather | solution.py:1888
  184.2 124.0 %reduce-scatter.13.cloned.1.call-start = ((), (), s32[]{:S(2)}) async-start(), calls=%async_computation.11 | async-start | bytes 5242880
  243.6 104.2 %reduce-scatter.7.cloned.1.call-start = ((), (), s32[]{:S(2)}) async-start(), calls=%async_computation.4 | async-start | bytes 1310720 | tf_op jit(solution)/shard_map/reduce_scatter | solution.py:1923
  271.5 35.0 %collective-permute-start.38 = (bf16[128,2048]{1,0:T(8,128)(2,1)}, bf16[128,2048]{1,0:T(8,128)(2,1)S(1)}, u32[]{:S(2)}, u32[]{:S(2)}) collective-permute-start(bf16[128,2048]{1,0:T(8,128)(2,1)} %get-tuple-element.877), channel_id=1, source_target_pairs={{0,8},{8,0},{16,24},{24,16},{1,9},{9,1},{17,25},{25,17},{2,10},{10... | collective-permute-start | bytes 1572872 | tf_op jit(solution)/shard_map/ppermute | solution.py:1781
  272.7 33.8 %collective-permute-start.39 = (bf16[128,2048]{1,0:T(8,128)(2,1)}, bf16[128,2048]{1,0:T(8,128)(2,1)S(1)}, u32[]{:S(2)}, u32[]{:S(2)}) collective-permute-start(bf16[128,2048]{1,0:T(8,128)(2,1)} %get-tuple-element.878), channel_id=1, source_target_pairs={{0,16},{8,24},{16,0},{24,8},{1,17},{9,25},{17,1},{25,9},{2,18},{10... | collective-permute-start | bytes 1572872 | tf_op jit(solution)/shard_map/ppermute | solution.py:1781
  276.9 29.5 %collective-permute-start.41 = (bf16[128,1024]{1,0:T(8,128)(2,1)}, bf16[128,1024]{1,0:T(8,128)(2,1)S(1)}, u32[]{:S(2)}, u32[]{:S(2)}) collective-permute-start(bf16[128,1024]{1,0:T(8,128)(2,1)} %get-tuple-element.907), channel_id=1, source_target_pairs={{1,0},{2,1},{3,2},{0,3},{5,4},{6,5},{7,6},{4,7},{9,8},{10,9},{11,1... | collective-permute-start | bytes 786440 | tf_op jit(solution)/shard_map/ppermute | solution.py:1784
  277.2 29.3 %collective-permute-start.42 = (bf16[128,1024]{1,0:T(8,128)(2,1)}, bf16[128,1024]{1,0:T(8,128)(2,1)}, u32[]{:S(2)}, u32[]{:S(2)}) collective-permute-start(bf16[128,1024]{1,0:T(8,128)(2,1)} %get-tuple-element.908), channel_id=1, source_target_pairs={{2,0},{3,1},{0,2},{1,3},{6,4},{7,5},{4,6},{5,7},{10,8},{11,9},{8,1... | collective-permute-start | bytes 786440 | tf_op jit(solution)/shard_map/ppermute | solution.py:1784
  308.2 90.8 %reduce-scatter.11.cloned.1.call-start = ((), (), s32[]{:S(2)}) async-start(), calls=%async_computation.6 | async-start | bytes 1310720 | tf_op jit(solution)/shard_map/reduce_scatter | solution.py:1932
  309.9 37.9 %collective-permute-start.47 = (bf16[256,2048]{1,0:T(8,128)(2,1)}, bf16[256,2048]{1,0:T(8,128)(2,1)S(1)}, u32[]{:S(2)}, u32[]{:S(2)}) collective-permute-start(bf16[256,2048]{1,0:T(8,128)(2,1)} %get-tuple-element.946), channel_id=1, source_target_pairs={{0,16},{8,24},{16,0},{24,8},{1,17},{9,25},{17,1},{25,9},{2,18},{10... | collective-permute-start | bytes 3145736 | tf_op jit(solution)/shard_map/ppermute | solution.py:1781
  311.1 36.7 %collective-permute-start.48 = (bf16[256,2048]{1,0:T(8,128)(2,1)}, bf16[256,2048]{1,0:T(8,128)(2,1)}, u32[]{:S(2)}, u32[]{:S(2)}) collective-permute-start(bf16[256,2048]{1,0:T(8,128)(2,1)} %get-tuple-element.947), channel_id=1, source_target_pairs={{0,8},{8,0},{16,24},{24,16},{1,9},{9,1},{17,25},{25,17},{2,10},{10... | collective-permute-start | bytes 3145736 | tf_op jit(solution)/shard_map/ppermute | solution.py:1781
  311.4 35.6 %collective-permute-start.45 = (bf16[128,2048]{1,0:T(8,128)(2,1)}, bf16[128,2048]{1,0:T(8,128)(2,1)S(1)}, u32[]{:S(2)}, u32[]{:S(2)}) collective-permute-start(bf16[128,2048]{1,0:T(8,128)(2,1)} %get-tuple-element.925), channel_id=1, source_target_pairs={{0,8},{8,0},{16,24},{24,16},{1,9},{9,1},{17,25},{25,17},{2,10},{10... | collective-permute-start | bytes 1572872 | tf_op jit(solution)/shard_map/ppermute | solution.py:1781
  312.6 35.2 %collective-permute-start.46 = (bf16[128,2048]{1,0:T(8,128)(2,1)}, bf16[128,2048]{1,0:T(8,128)(2,1)}, u32[]{:S(2)}, u32[]{:S(2)}) collective-permute-start(bf16[128,2048]{1,0:T(8,128)(2,1)} %get-tuple-element.926), channel_id=1, source_target_pairs={{0,16},{8,24},{16,0},{24,8},{1,17},{9,25},{17,1},{25,9},{2,18},{10... | collective-permute-start | bytes 1572872 | tf_op jit(solution)/shard_map/ppermute | solution.py:1781
  357.1 93.5 %reduce-scatter.9.cloned.1.call-start = ((), (), s32[]{:S(2)}) async-start(), calls=%async_computation.5 | async-start | bytes 1310720 | tf_op jit(solution)/shard_map/reduce_scatter | solution.py:1941
  357.2 28.5 %collective-permute-start.51 = (bf16[256,2048]{1,0:T(8,128)(2,1)}, bf16[256,2048]{1,0:T(8,128)(2,1)}, u32[]{:S(2)}, u32[]{:S(2)}) collective-permute-start(bf16[256,2048]{1,0:T(8,128)(2,1)} %copy-done.71), channel_id=1, source_target_pairs={{0,16},{8,24},{16,0},{24,8},{1,17},{9,25},{17,1},{25,9},{2,18},{10... | collective-permute-start | bytes 3145736 | tf_op jit(solution)/shard_map/ppermute | solution.py:1781
  357.6 28.0 %collective-permute-start.52 = (bf16[256,2048]{1,0:T(8,128)(2,1)}, bf16[256,2048]{1,0:T(8,128)(2,1)}, u32[]{:S(2)}, u32[]{:S(2)}) collective-permute-start(bf16[256,2048]{1,0:T(8,128)(2,1)} %copy-done.70), channel_id=1, source_target_pairs={{0,8},{8,0},{16,24},{24,16},{1,9},{9,1},{17,25},{25,17},{2,10},{10... | collective-permute-start | bytes 3145736 | tf_op jit(solution)/shard_map/ppermute | solution.py:1781
  411.8 30.7 %collective-permute-start.62 = (bf16[176,1024]{1,0:T(8,128)(2,1)S(1)}, bf16[176,1024]{1,0:T(8,128)(2,1)S(1)}, u32[]{:S(2)}, u32[]{:S(2)}) collective-permute-start(bf16[176,1024]{1,0:T(8,128)(2,1)S(1)} %get-tuple-element.1049), channel_id=1, source_target_pairs={{3,0},{0,1},{1,2},{2,3},{7,4},{4,5},{5,6},{6,7},{11,8},{8,9},{9,10... | collective-permute-start | bytes 1081352 | tf_op jit(solution)/shard_map/ppermute | solution.py:1784
  (157 other events, 1802.5 us)
Sparse Core Ops, SparseCore 0:
  56.5 33.4 all-gather.8
  102.3 37.8 all-gather.10
  146.4 36.0 all-gather.12
  184.3 59.1 all-gather.14
  246.4 55.8 reduce-scatter.12
  308.3 23.0 reduce-scatter.6
  357.2 24.0 reduce-scatter.10
  390.3 23.9 reduce-scatter.8
